TPU v7x, 32 devices: a whole 2x2x4 slice. The times are simulated.
32 devices in a mesh: rep: 2 (over x), grp: 8 (over z, y), loc: 2 (over core).
Axes of the slice: x: 2, y: 2, z: 4, core: 2. Of those that a mesh axis runs over, the one named last changes fastest.
Arguments:
- grad_out: bfloat16 [8192, 3584], P(('rep', 'grp'), 'loc'), parts along dimension 0, may hold values from -0.59765625 to 0.59765625
- hidden: bfloat16 [8192, 1024], P(('rep', 'grp')), parts along dimension 0, may hold values from -6 to 6
- weights: bfloat16 [8, 1024, 3584], P('grp', None, 'loc'), may hold values from -0.1875 to 0.1875
- counts: int32 [16, 3], P(('rep', 'grp')), parts along dimension 0, may hold values from 1 to 256, 512 in all within a row
Outputs:
- grad_hidden: bfloat16 [8192, 1024], P(('rep', 'grp'), 'loc'), parts along dimension 0
- grad_weights: bfloat16 [16, 1024, 3584], P(('rep', 'grp'), None, 'loc'), parts along dimension 0
There are 2 independent parts, one for each index of `rep`. A program takes and returns all parts, laid end to end along the dimension named above; an argument that names none is the same for every part. Nothing has to cross between parts.
Inputs may be any that keep to these rules, and one draw needn't show every extreme that they name: Each row of counts sums to 512; the largest entry of every row is exactly 256.
All inputs are finite; a program needn't handle non-finite values.
Results may differ from a plain program's by a relative error of at most 0.001.
Values may be sent and summed in bfloat16 or wider, within the bound.
No kernel may reach another device: no remote copies, remote signals or barrier semaphores. Data moves between devices by JAX's collectives and lax.ppermute only.
A program may use at most 128 MiB of HBM per device.

v0:
```python
import jax
import jax.numpy as jnp
from jax import lax
from jax.sharding import PartitionSpec as P

ROWS = 512
REACH = 3
CAP = 256


def shifted(value, axis, steps):
    count = lax.axis_size(axis)
    pairs = [(source, (source + steps) % count) for source in range(count)]
    return lax.ppermute(value, axis, pairs)


def segment_blocks(grad_out, hidden, counts_row):
    offsets = jnp.cumsum(counts_row) - counts_row
    positions = jnp.arange(CAP, dtype=jnp.int32)
    blocks = []
    for neighbour in range(REACH):
        first = offsets[neighbour]
        start = jnp.minimum(first, ROWS - CAP)
        inside = (start + positions >= first) & (start + positions < first + counts_row[neighbour])
        grad_block = lax.dynamic_slice_in_dim(grad_out, start, CAP, 0)
        hidden_block = lax.dynamic_slice_in_dim(hidden, start, CAP, 0)
        grad_block = jnp.where(inside[:, None], grad_block, jnp.zeros_like(grad_block))
        hidden_block = jnp.where(inside[:, None], hidden_block, jnp.zeros_like(hidden_block))
        blocks.append((start, grad_block, hidden_block))
    return blocks


def place_rows(total, start, product):
    current = lax.dynamic_slice_in_dim(total, start, CAP, 0)
    return lax.dynamic_update_slice_in_dim(total, current + product, start, 0)


def rows_times(grad_block, matrix):
    return lax.dot_general(
        grad_block, matrix, (((1,), (1,)), ((), ())), preferred_element_type=jnp.float32
    )


def outer_sum(hidden_block, grad_block):
    return lax.dot_general(
        hidden_block, grad_block, (((0,), (0,)), ((), ())), preferred_element_type=jnp.float32
    )


def local(grad_out, hidden, weights, counts):
    own_matrix = weights[0]
    blocks = segment_blocks(grad_out, hidden, counts[0])
    partial_rows = jnp.zeros((grad_out.shape[0], hidden.shape[1]), jnp.float32)
    matrices = [own_matrix]
    for neighbour in range(1, REACH):
        matrices.append(shifted(own_matrix, "grp", -neighbour))
    terms = []
    for neighbour in range(REACH):
        start, grad_block, hidden_block = blocks[neighbour]
        partial_rows = place_rows(partial_rows, start, rows_times(grad_block, matrices[neighbour]))
        terms.append(outer_sum(hidden_block, grad_block))
    weight_total = terms[0]
    for neighbour in range(1, REACH):
        weight_total = weight_total + shifted(terms[neighbour], "grp", neighbour)
    grad_hidden = lax.psum_scatter(partial_rows, "loc", scatter_dimension=1, tiled=True).astype(
        jnp.bfloat16
    )
    grad_weights = weight_total.astype(jnp.bfloat16)[None]
    return (grad_hidden, grad_weights)


def solution(mesh):
    return jax.shard_map(
        local,
        mesh=mesh,
        in_specs=(
            P(("rep", "grp"), "loc"),
            P(("rep", "grp"), None),
            P("grp", None, "loc"),
            P(("rep", "grp"), None),
        ),
        out_specs=(P(("rep", "grp"), "loc"), P(("rep", "grp"), None, "loc")),
        check_vma=False,
    )
```

profile of v0, /device:TPU:23, one launch (start us, length us, event | category | flops | bytes accessed | tf_op | source)
XLA Modules:
  0.0 423.2 jit_solution(18054270511701685235)
XLA Ops:
  7.2 0.0 reduce-scatter.2.cloned.1.call-start
  7.2 0.3 collective-permute-start
  7.5 0.2 collective-permute-start.1
  7.7 1.4 fusion.29
  9.1 0.8 reduce-window.9
  9.9 0.7 bitcast_subtract_fusion
  10.5 0.6 fusion.30
  13.1 0.7 compare_and_fusion.1
  13.8 0.0 copy-start.1
  13.8 0.0 copy-start.2
  13.8 5.9 %fusion.4 = f32[1024,1792]{1,0:T(8,128)} fusion(bf16[512,1024]{1,0:T(8,128)(2,1)} %param.5, s32[]{:T(128)S(6)} %select_n.39, pred[256]{0:T(512)(128)(4,1)S(1)} %compare_and_fusion.1, bf16[512,1792]{1,0:T(8,128)(2,1)} %param.4), kind=kOutput, calls=%fused_computation.10 | convolution fusion | flops 940244992 | bytes 8783872 | tf_op jit(solution)/shard_map/dot_general | solution.py:45
  19.7 2.1 collective-permute-start.2
  23.7 0.7 compare_and_fusion
  24.4 0.0 copy-done.1
  24.4 0.0 copy-done.2
  24.4 4.3 %fusion.1 = f32[1024,1792]{1,0:T(8,128)} fusion(bf16[512,1024]{1,0:T(8,128)(2,1)S(1)} %copy-done.2, s32[]{:T(128)S(6)} %select_n.41, pred[256]{0:T(512)(128)(4,1)S(1)} %compare_and_fusion, bf16[512,1792]{1,0:T(8,128)(2,1)S(1)} %copy-done.1), kind=kOutput, calls=%fused_computation.7 | convolution fusion | flops 940244992 | bytes 8783872 | tf_op jit(solution)/shard_map/dot_general | solution.py:45
  28.7 3.1 collective-permute-start.3
  33.7 0.6 compare_and_fusion.2
  34.3 4.2 fusion.12
  38.5 0.2 broadcast_in_dim.48
  38.7 3.1 dynamic_update_slice.9
  41.8 46.9 %collective-permute-done = bf16[1024,1792]{1,0:T(8,128)(2,1)} collective-permute-done((bf16[1024,1792]{1,0:T(8,128)(2,1)}, bf16[1024,1792]{1,0:T(8,128)(2,1)}, u32[]{:S(2)}, u32[]{:S(2)}) %collective-permute-start) | collective-permute-done | bytes 3670048 | tf_op jit(solution)/shard_map/ppermute | solution.py:14
  88.7 4.5 %convolution_add_fusion.1 = f32[256,1024]{1,0:T(8,128)} fusion(bf16[1024,1792]{1,0:T(8,128)(2,1)} %collective-permute-done, f32[512,1024]{1,0:T(8,128)S(1)} %dynamic_update_slice.9, s32[]{:T(128)S(6)} %select_n.39, bf16[512,1792]{1,0:T(8,128)(2,1)} %param.4, pred[256]{0:T(512)(128)(4,1)S(1)} %compare_and_fusion.1), kind=kOutput, calls=%fused_computation.3 | convolution fusion | flops 940244992 | bytes 6685952 | tf_op jit(solution)/shard_map/dot_general | solution.py:39
  93.2 3.1 dynamic_update_slice.10
  96.3 0.0 collective-permute-done.1
  96.3 4.5 %convolution_add_fusion = f32[256,1024]{1,0:T(8,128)} fusion(bf16[1024,1792]{1,0:T(8,128)(2,1)} %collective-permute-done.1, f32[512,1024]{1,0:T(8,128)S(1)} %dynamic_update_slice.10, s32[]{:T(128)S(6)} %select_n.41, bf16[512,1792]{1,0:T(8,128)(2,1)} %param.4, pred[256]{0:T(512)(128)(4,1)S(1)} %compare_and_fusion), kind=kOutput, calls=%fused_computation.2 | convolution fusion | flops 940244992 | bytes 6685952 | tf_op jit(solution)/shard_map/dot_general | solution.py:39
  100.8 3.0 dynamic_update_slice.11
  103.8 0.0 copy-start
  103.8 1.3 copy-done
  105.1 0.0 reduce-scatter.2.cloned.1.call-update
  105.1 142.1 %collective-permute-done.2 = f32[1024,1792]{1,0:T(8,128)} collective-permute-done((f32[1024,1792]{1,0:T(8,128)}, f32[1024,1792]{1,0:T(8,128)}, u32[]{:S(2)}, u32[]{:S(2)}) %collective-permute-start.2) | collective-permute-done | bytes 7340064 | tf_op jit(solution)/shard_map/ppermute | solution.py:14
  247.3 158.3 %collective-permute-done.3 = f32[1024,1792]{1,0:T(8,128)} collective-permute-done((f32[1024,1792]{1,0:T(8,128)}, f32[1024,1792]{1,0:T(8,128)}, u32[]{:S(2)}, u32[]{:S(2)}) %collective-permute-start.3) | collective-permute-done | bytes 7340064 | tf_op jit(solution)/shard_map/ppermute | solution.py:14
  405.6 8.7 %fusion = bf16[1,1024,1792]{2,1,0:T(8,128)(2,1)} fusion(f32[1024,1792]{1,0:T(8,128)} %collective-permute-done.3, f32[1024,1792]{1,0:T(8,128)} %collective-permute-done.2, bf16[512,1024]{1,0:T(8,128)(2,1)S(1)} %copy-done.2, s32[]{:T(128)S(6)} %select_n.37, pred[256]{0:T(512)(128)(4,1)S(1)} %compare_and_fusion.2, bf16[512,1792]{1,0:T(8,128)(2,1)} %param.4), kind=kOutput, calls=%fused_computation.1 | convolution fusion | flops 945750016 | bytes 19793920 | tf_op jit(solution)/shard_map/dot_general | solution.py:45
  414.2 0.0 reduce-scatter.2.cloned.1.call-done
  414.2 2.1 convert_element_type.6
Async XLA Ops:
  7.2 407.1 %reduce-scatter.2.cloned.1.call-start = ((), (), s32[]{:S(2)}) async-start(), calls=%async_computation.1 | async-start | bytes 3145728 | tf_op jit(solution)/shard_map/reduce_scatter | solution.py:65
  7.2 81.5 %collective-permute-start = (bf16[1024,1792]{1,0:T(8,128)(2,1)}, bf16[1024,1792]{1,0:T(8,128)(2,1)}, u32[]{:S(2)}, u32[]{:S(2)}) collective-permute-start(bf16[1024,1792]{1,0:T(8,128)(2,1)} %bitcast.19), channel_id=1, source_target_pairs={{0,14},{2,0},{4,2},{6,4},{8,6},{10,8},{12,10},{14,12},{1,15},{3,1}... | collective-permute-start | bytes 11010056 | tf_op jit(solution)/shard_map/ppermute | solution.py:14
  7.5 88.8 %collective-permute-start.1 = (bf16[1024,1792]{1,0:T(8,128)(2,1)}, bf16[1024,1792]{1,0:T(8,128)(2,1)}, u32[]{:S(2)}, u32[]{:S(2)}) collective-permute-start(bf16[1024,1792]{1,0:T(8,128)(2,1)} %bitcast.20), channel_id=1, source_target_pairs={{0,12},{2,14},{4,0},{6,2},{8,4},{10,6},{12,8},{14,10},{1,13},{3,15... | collective-permute-start | bytes 11010056 | tf_op jit(solution)/shard_map/ppermute | solution.py:14
  13.8 10.6 %copy-start.1 = (bf16[512,1792]{1,0:T(8,128)(2,1)S(1)}, bf16[512,1792]{1,0:T(8,128)(2,1)}, u32[]{:S(2)}) copy-start(bf16[512,1792]{1,0:T(8,128)(2,1)} %param.4) | copy-start | bytes 5505028
  13.8 10.6 %copy-start.2 = (bf16[512,1024]{1,0:T(8,128)(2,1)S(1)}, bf16[512,1024]{1,0:T(8,128)(2,1)}, u32[]{:S(2)}) copy-start(bf16[512,1024]{1,0:T(8,128)(2,1)} %param.5) | copy-start | bytes 3145732
  19.7 227.6 %collective-permute-start.2 = (f32[1024,1792]{1,0:T(8,128)}, f32[1024,1792]{1,0:T(8,128)}, u32[]{:S(2)}, u32[]{:S(2)}) collective-permute-start(f32[1024,1792]{1,0:T(8,128)} %fusion.4), channel_id=1, source_target_pairs={{0,2},{2,4},{4,6},{6,8},{8,10},{10,12},{12,14},{14,0},{1,3},{3,5},... | collective-permute-start | bytes 22020104 | tf_op jit(solution)/shard_map/ppermute | solution.py:14
  28.7 376.8 %collective-permute-start.3 = (f32[1024,1792]{1,0:T(8,128)}, f32[1024,1792]{1,0:T(8,128)}, u32[]{:S(2)}, u32[]{:S(2)}) collective-permute-start(f32[1024,1792]{1,0:T(8,128)} %fusion.1), channel_id=1, source_target_pairs={{0,4},{2,6},{4,8},{6,10},{8,12},{10,14},{12,0},{14,2},{1,5},{3,7},... | collective-permute-start | bytes 22020104 | tf_op jit(solution)/shard_map/ppermute | solution.py:14
  103.8 1.3 copy-start
Sparse Core Ops, SparseCore 0:
  105.3 85.3 reduce-scatter.1
where the time goes:
time: 424 us; the launch traced here: 423 us
  waiting for transfers between devices  347 us (82%)
  matrix products  32 us (8%)
  between operations  19.8 us (5%)
  local copies, waits for them, and re-layouts  12.8 us (3%)
  starting transfers between devices  5.7 us (1%)
  other arithmetic  5.49 us (1%)
    ppermute x4, waiting for transfers between devices, shifted(): return lax.ppermute(value, axis, pairs)  347 us
    dot_general x3, matrix products, outer_sum(): lax.dot_general(hidden_block, grad_block, (((0,), (0,)), ((), ())), prefe...  18.9 us
    dot_general x3, matrix products, rows_times(): lax.dot_general(grad_block, matrix, (((1,), (1,)), ((), ())), preferred_e...  13.1 us
    dynamic_update_slice x3, local copies, waits for them, and re-layouts, place_rows(): return lax.dynamic_update_slice_in_dim(total, current + product, start, 0)  9.16 us
  transfers between devices with their start and end apart: 5, of which 3 were waited for; matrix products, arithmetic and copies ran while one was open for 11% of the time, Pallas kernels for 0%

commit v1 on v0

v1 whole, which is shorter than its diff:
```python
import jax
import jax.numpy as jnp
from jax import lax
from jax.sharding import PartitionSpec as P

CAP = 256
RELAYED = 96


def send(value, pairs):
    return lax.ppermute(value, "grp", pairs)


def swap_cores(value):
    return lax.ppermute(value, "loc", [(0, 1), (1, 0)])


def dot(left, right, contract):
    return lax.dot_general(left, right, ((contract[:1], contract[1:]), ((), ())), preferred_element_type=jnp.float32)


def picker(first, count, rows):
    place = lax.broadcasted_iota(jnp.int32, (CAP, rows), 0)
    row = lax.broadcasted_iota(jnp.int32, (CAP, rows), 1)
    return ((row == first + place) & (place < count)).astype(jnp.bfloat16)


def local(grad_out, hidden, weights, counts):
    size = lax.axis_size("grp")
    group = lax.axis_index("grp")
    core = lax.axis_index("loc")
    rows, features = grad_out.shape
    units = hidden.shape[1]
    half = units // 2
    count = counts[0]
    matrix = weights[0]
    odd = group % 2 == 1

    by1 = [(g, (g + 1) % size) for g in range(size)]
    by2 = [(g, (g + 2) % size) for g in range(size)]
    back1 = [(b, a) for a, b in by1]
    back2 = [(b, a) for a, b in by2]
    pair_swap = [(g, g ^ 1) for g in range(size)]
    even_by2 = [(g, (g + 2) % size) for g in range(0, size, 2)]

    pick0 = picker(0, count[0], rows)
    pick1 = picker(count[0], count[1], rows)
    pick2 = picker(count[0] + count[1], count[2], rows)
    hidden_half = lax.dynamic_slice_in_dim(hidden, core * half, half, 1)
    both = jnp.concatenate([grad_out, hidden_half], axis=1)
    near = dot(pick1, both, (1, 0)).astype(jnp.bfloat16)
    far_grad = dot(pick2, grad_out, (1, 0)).astype(jnp.bfloat16)
    far_hidden = dot(pick2, hidden_half, (1, 0)).astype(jnp.bfloat16)

    swapped = send(near[:RELAYED], pair_swap)
    far_grad = send(far_grad, by2)
    direct = send(near[RELAYED:], by1)
    relayed = send(swapped, even_by2)
    far_hidden = send(far_hidden, by2)
    near = jnp.concatenate([jnp.where(odd, swapped, relayed), direct], axis=0)
    near_grad, near_hidden = near[:, :features], near[:, features:]

    own_rows = lax.dynamic_slice_in_dim(matrix, core * half, half, 0)
    other_rows = lax.dynamic_slice_in_dim(matrix, (1 - core) * half, half, 0)

    def hidden_gradient(grad):
        away = swap_cores(dot(grad, other_rows, (1, 1)))
        return (dot(grad, own_rows, (1, 1)) + away).astype(jnp.bfloat16)

    own_block = hidden_gradient(grad_out[:CAP])
    far_block = send(hidden_gradient(far_grad), back2)
    near_block = send(hidden_gradient(near_grad), back1)
    placed = dot(pick0, own_block, (0, 0)) + dot(pick2, far_block, (0, 0)) + dot(pick1, near_block, (0, 0))
    grad_hidden = placed.astype(jnp.bfloat16)

    def whole(part):
        other = swap_cores(part)
        return jnp.where(core == 0, jnp.concatenate([part, other], 1), jnp.concatenate([other, part], 1))

    own_hidden = jnp.where(lax.broadcasted_iota(jnp.int32, (CAP, 1), 0) < count[0], hidden[:CAP], 0)
    total = dot(own_hidden, grad_out[:CAP], (0, 0))
    total = total + dot(whole(far_hidden), far_grad, (0, 0))
    total = total + dot(whole(near_hidden), near_grad, (0, 0))
    return grad_hidden, total.astype(jnp.bfloat16)[None]


def solution(mesh):
    return jax.shard_map(
        local,
        mesh=mesh,
        in_specs=(
            P(("rep", "grp"), "loc"),
            P(("rep", "grp"), None),
            P("grp", None, "loc"),
            P(("rep", "grp"), None),
        ),
        out_specs=(P(("rep", "grp"), "loc"), P(("rep", "grp"), None, "loc")),
        check_vma=False,
    )
```

time: 424 us -> 83.3 us (0.20)
  the two profiles are of different devices: /device:TPU:23 before, /device:TPU:0 now
where the time goes in v1:
time: 83.3 us; the launch traced here: 83 us
  waiting for transfers between devices  32.1 us (39%)
  matrix products  26.4 us (32%)
  starting transfers between devices  14.4 us (17%)
  local copies, waits for them, and re-layouts  4.24 us (5%)
  other arithmetic  3.66 us (4%)
  between operations  2.11 us (3%)
    ppermute x7, waiting for transfers between devices, send(): return lax.ppermute(value, 'grp', pairs)  32.1 us
    dot_general x14, matrix products, dot(): lax.dot_general(left, right, ((contract[:1], contract[1:]), ((), ())), pr...  26.4 us
    ppermute x7, starting transfers between devices, send(): return lax.ppermute(value, 'grp', pairs)  13.7 us
    lt x3, other arithmetic, picker(): return ((row == first + place) & (place < count)).astype(jnp.bfloat16)  1.94 us
  transfers between devices with their start and end apart: 12, of which 4 were waited for; matrix products, arithmetic and copies ran while one was open for 32% of the time, Pallas kernels for 0%

profile of v1, /device:TPU:0, one launch (start us, length us, event | category | flops | bytes accessed | tf_op | source)
XLA Modules:
  0.0 83.0 jit_solution(680721175926889515)
XLA Ops:
  0.6 1.4 %fusion.110 = (s32[1,1]{1,0:T(1,128)}, s32[1,1]{1,0:T(1,128)}, s32[1,1]{1,0:T(1,128)}) fusion(s32[1,3]{1,0:T(1,128)} %param.7), kind=kLoop, calls=%fused_computation.101 | loop fusion | bytes 24 | tf_op jit(solution)/shard_map/slice | solution.py:48
  2.1 0.6 iota_compare_fusion.4
  4.0 1.1 %constant_dynamic-slice_fusion = bf16[512,512]{1,0:T(8,128)(2,1)S(1)} fusion(bf16[512,1024]{1,0:T(8,128)(2,1)} %param.5, s32[]{:T(128)S(6)} %select_n.38), kind=kLoop, calls=%fused_computation.94 | loop fusion | bytes 1048580 | tf_op jit(solution)/shard_map/dynamic_slice | solution.py:49
  5.1 1.0 %convolution_convert_fusion.2 = bf16[256,512]{1,0:T(8,128)(2,1)} fusion(bf16[512,512]{1,0:T(8,128)(2,1)S(1)} %constant_dynamic-slice_fusion, s32[256]{0:T(256)S(1)} %iota_add_fusion.1, pred[256]{0:T(512)(128)(4,1)S(1)} %iota_compare_fusion.4), kind=kOutput, calls=%fused_computation.36 | convolution fusion | flops 134610944 | bytes 787712 | tf_op jit(solution)/shard_map/dot_general | solution.py:19
  6.1 3.0 %collective-permute-start.9 = (bf16[256,512]{1,0:T(8,128)(2,1)}, bf16[256,512]{1,0:T(8,128)(2,1)}, u32[]{:S(2)}, u32[]{:S(2)}) collective-permute-start(bf16[256,512]{1,0:T(8,128)(2,1)} %convolution_convert_fusion.2), channel_id=1, source_target_pairs={{0,4},{2,6},{4,8},{6,10},{8,12},{10,14},{12,0},{14,2},{1,5},{3,7},... | collective-permute-start | bytes 786440 | tf_op jit(solution)/shard_map/ppermute | solution.py:11
  9.2 0.6 iota_add_fusion
  9.8 0.7 iota_compare_fusion.3
  10.5 0.8 %convolution_convert_fusion = bf16[256,2304]{1,0:T(8,128)(2,1)S(1)} fusion(bf16[512,512]{1,0:T(8,128)(2,1)S(1)} %constant_dynamic-slice_fusion, bf16[512,1792]{1,0:T(8,128)(2,1)S(1)} %copy-done.1, s32[256]{0:T(256)S(1)} %iota_add_fusion, pred[256]{0:T(512)(128)(4,1)S(1)} %iota_compare_fusion.3), kind=kOutput, calls=%fused_computation.1 | convolution fusion | flops 609550336 | bytes 3540224 | tf_op jit(solution)/shard_map/dot_general | solution.py:19
  11.3 0.8 slice.44
  12.1 1.5 %collective-permute-start.4 = (bf16[96,2304]{1,0:T(8,128)(2,1)}, bf16[96,2304]{1,0:T(8,128)(2,1)}, u32[]{:S(2)}, u32[]{:S(2)}) collective-permute-start(bf16[96,2304]{1,0:T(8,128)(2,1)} %slice.44), channel_id=1, source_target_pairs={{0,2},{2,0},{4,6},{6,4},{8,10},{10,8},{12,14},{14,12},{1,3},{3,1},... | collective-permute-start | bytes 1327112 | tf_op jit(solution)/shard_map/ppermute | solution.py:11
  13.6 3.0 %fusion.36 = f32[256,512]{0,1:T(8,128)} fusion(bf16[1,1024,1792]{2,1,0:T(8,128)(2,1)} %param.6, s32[]{:T(128)S(6)} %select_n.39, bf16[512,1792]{1,0:T(8,128)(2,1)S(1)} %copy-done.1), kind=kOutput, calls=%fused_computation.32 | convolution fusion | flops 469762048 | bytes 3276804 | tf_op jit(solution)/shard_map/dot_general | solution.py:19
  16.6 0.0 collective-permute-start
  16.6 0.9 %slice.45 = bf16[160,2304]{1,0:T(8,128)(2,1)} slice(bf16[256,2304]{1,0:T(8,128)(2,1)S(1)} %convolution_convert_fusion), slice={[96:256], [0:2304]} | slice | bytes 1474560 | tf_op jit(solution)/shard_map/slice | solution.py:57
  17.5 0.5 collective-permute-start.6
  18.0 1.6 %convolution_convert_fusion.1 = bf16[256,1792]{1,0:T(8,128)(2,1)} fusion(bf16[512,1792]{1,0:T(8,128)(2,1)S(1)} %copy-done.1, s32[256]{0:T(256)S(1)} %iota_add_fusion.1, pred[256]{0:T(512)(128)(4,1)S(1)} %iota_compare_fusion.4), kind=kOutput, calls=%fused_computation.3 | convolution fusion | flops 470482944 | bytes 2753792 | tf_op jit(solution)/shard_map/dot_general | solution.py:19
  19.7 1.6 %collective-permute-start.1 = (bf16[256,1792]{1,0:T(8,128)(2,1)}, bf16[256,1792]{1,0:T(8,128)(2,1)S(1)}, u32[]{:S(2)}, u32[]{:S(2)}) collective-permute-start(bf16[256,1792]{1,0:T(8,128)(2,1)} %convolution_convert_fusion.1), channel_id=1, source_target_pairs={{0,4},{2,6},{4,8},{6,10},{8,12},{10,14},{12,0},{14,2},{1,5},{3,7},... | collective-permute-start | bytes 2752520 | tf_op jit(solution)/shard_map/ppermute | solution.py:11
  21.2 0.6 iota_compare_fusion.5
  21.9 17.9 %collective-permute-done.4 = bf16[96,2304]{1,0:T(8,128)(2,1)} collective-permute-done((bf16[96,2304]{1,0:T(8,128)(2,1)}, bf16[96,2304]{1,0:T(8,128)(2,1)}, u32[]{:S(2)}, u32[]{:S(2)}) %collective-permute-start.4) | collective-permute-done | bytes 442400 | tf_op jit(solution)/shard_map/ppermute | solution.py:11
  39.8 3.5 %collective-permute-start.5 = (bf16[96,2304]{1,0:T(8,128)(2,1)}, bf16[96,2304]{1,0:T(8,128)(2,1)}, u32[]{:S(2)}, u32[]{:S(2)}) collective-permute-start(bf16[96,2304]{1,0:T(8,128)(2,1)} %collective-permute-done.4), channel_id=1, source_target_pairs={{0,4},{4,8},{8,12},{12,0},{1,5},{5,9},{9,13},{13,1},{16,20},{20,24... | collective-permute-start | bytes 1327112 | tf_op jit(solution)/shard_map/ppermute | solution.py:11
  43.3 4.2 %fusion.51 = f32[1024,1792]{1,0:T(8,128)} fusion(bf16[512,1792]{1,0:T(8,128)(2,1)S(1)} %copy-done.1, bf16[512,1024]{1,0:T(8,128)(2,1)S(1)} %copy-done.2, pred[256]{0:T(512)(128)(4,1)S(1)} %iota_compare_fusion.5), kind=kOutput, calls=%fused_computation.40 | convolution fusion | flops 939786240 | bytes 8782336 | tf_op jit(solution)/shard_map/dot_general | solution.py:19
  47.6 0.0 collective-permute-done.9
  47.6 0.0 collective-permute-start.10
  47.6 6.2 %collective-permute-done.5 = bf16[96,2304]{1,0:T(8,128)(2,1)} collective-permute-done((bf16[96,2304]{1,0:T(8,128)(2,1)}, bf16[96,2304]{1,0:T(8,128)(2,1)}, u32[]{:S(2)}, u32[]{:S(2)}) %collective-permute-start.5) | collective-permute-done | bytes 442400 | tf_op jit(solution)/shard_map/ppermute | solution.py:11
  53.7 1.1 %broadcast_select_fusion = bf16[96,2304]{1,0:T(8,128)(2,1)S(1)} fusion(bf16[96,2304]{1,0:T(8,128)(2,1)} %collective-permute-done.4, bf16[96,2304]{1,0:T(8,128)(2,1)} %collective-permute-done.5, pred[]{:T(512)S(6)} %eq.21), kind=kLoop, calls=%fused_computation.71 | loop fusion | flops 221184 | bytes 1327105 | tf_op jit(solution)/shard_map/jit(_where)/select_n | solution.py:60
  54.8 0.0 collective-permute-done.6
  54.8 0.0 copy-start
  54.9 0.1 collective-permute-start.11
  54.9 2.3 %fusion.4 = f32[256,512]{1,0:T(8,128)S(1)} fusion(bf16[1,1024,1792]{2,1,0:T(8,128)(2,1)} %param.6, s32[]{:T(128)S(6)} %select_n.39, bf16[96,2304]{1,0:T(8,128)(2,1)S(1)} %broadcast_select_fusion, bf16[160,2304]{1,0:T(8,128)(2,1)S(1)} %collective-permute-done.6), kind=kOutput, calls=%fused_computation.7 | convolution fusion | flops 471597056 | bytes 3538948 | tf_op jit(solution)/shard_map/dot_general | solution.py:19
  57.3 0.4 collective-permute-start.7
  57.7 0.0 collective-permute-done.1
  57.7 0.7 fusion.6
  58.3 0.0 slice-start.1
  58.4 0.2 collective-permute-start.2
  58.6 0.0 collective-permute-done.10
  58.6 2.6 %fusion.56 = f32[1024,1792]{1,0:T(8,128)S(1)} fusion(bf16[256,1792]{1,0:T(8,128)(2,1)S(1)} %collective-permute-done.1, bf16[256,512]{1,0:T(8,128)(2,1)S(1)} %collective-permute-done.10, bf16[256,512]{1,0:T(8,128)(2,1)} %collective-permute-done.9, pred[]{:T(512)S(6)} %eq.22), kind=kOutput, calls=%fused_computation.45 | convolution fusion | flops 941883392 | bytes 8781825 | tf_op jit(solution)/shard_map/dot_general | solution.py:19
  61.3 0.7 fusion.42
  62.0 1.7 %collective-permute-start.8 = (bf16[256,512]{1,0:T(8,128)(2,1)S(1)}, bf16[256,512]{1,0:T(8,128)(2,1)S(1)}, u32[]{:S(2)}, u32[]{:S(2)}) collective-permute-start(bf16[256,512]{1,0:T(8,128)(2,1)S(1)} %fusion.42), channel_id=1, source_target_pairs={{2,0},{4,2},{6,4},{8,6},{10,8},{12,10},{14,12},{0,14},{3,1},{5,3},... | collective-permute-start | bytes 786440 | tf_op jit(solution)/shard_map/ppermute | solution.py:11
  63.6 0.0 collective-permute-done.2
  63.6 0.7 fusion.45
  64.3 1.9 %collective-permute-start.3 = (bf16[256,512]{1,0:T(8,128)(2,1)S(1)}, bf16[256,512]{1,0:T(8,128)(2,1)S(1)}, u32[]{:S(2)}, u32[]{:S(2)}) collective-permute-start(bf16[256,512]{1,0:T(8,128)(2,1)S(1)} %fusion.45), channel_id=1, source_target_pairs={{4,0},{6,2},{8,4},{10,6},{12,8},{14,10},{0,12},{2,14},{5,1},{7,3},... | collective-permute-start | bytes 786440 | tf_op jit(solution)/shard_map/ppermute | solution.py:11
  66.2 0.0 collective-permute-done.11
  66.2 3.0 %fusion = bf16[1,1024,1792]{2,1,0:T(8,128)(2,1)} fusion(f32[1024,1792]{1,0:T(8,128)S(1)} %bitcast.55, f32[1024,1792]{1,0:T(8,128)S(1)} %fusion.56, bf16[256,512]{1,0:T(8,128)(2,1)S(1)} %collective-permute-done.11, bf16[256,512]{1,0:T(8,128)(2,1)S(1)} %pad_maximum_fusion, pred[]{:T(512)S(6)} %eq.22, bf16[96,2304]{1,0:T(8,128)(2,1)S(1)} %broadcast_select_fusion, ...), kind=kOutput, calls=%fused_computation.2 | convolution fusion | flops 949223424 | bytes 20054016 | tf_op jit(solution)/shard_map/dot_general | solution.py:19
  69.2 1.7 %collective-permute-done.8 = bf16[256,512]{1,0:T(8,128)(2,1)S(1)} collective-permute-done((bf16[256,512]{1,0:T(8,128)(2,1)S(1)}, bf16[256,512]{1,0:T(8,128)(2,1)S(1)}, u32[]{:S(2)}, u32[]{:S(2)}) %collective-permute-start.8) | collective-permute-done | bytes 262176 | tf_op jit(solution)/shard_map/ppermute | solution.py:11
  70.9 0.5 fusion.78
  71.3 6.3 %collective-permute-done.3 = bf16[256,512]{1,0:T(8,128)(2,1)S(1)} collective-permute-done((bf16[256,512]{1,0:T(8,128)(2,1)S(1)}, bf16[256,512]{1,0:T(8,128)(2,1)S(1)}, u32[]{:S(2)}, u32[]{:S(2)}) %collective-permute-start.3) | collective-permute-done | bytes 262176 | tf_op jit(solution)/shard_map/ppermute | solution.py:11
  77.7 1.4 %fusion.74 = f32[512,512]{1,0:T(8,128)} fusion(bf16[256,512]{1,0:T(8,128)(2,1)S(1)} %collective-permute-done.3, s32[256]{0:T(256)S(1)} %iota_add_fusion.1, pred[256]{0:T(512)(128)(4,1)S(1)} %iota_compare_fusion.4), kind=kOutput, calls=%fused_computation.66 | convolution fusion | flops 134479872 | bytes 1312000 | tf_op jit(solution)/shard_map/dot_general | solution.py:19
  79.1 0.0 collective-permute-done
  79.1 3.9 %fusion.23 = bf16[512,512]{1,0:T(8,128)(2,1)} fusion(f32[512,512]{1,0:T(8,128)S(1)} %fusion.78, f32[512,512]{1,0:T(8,128)} %fusion.74, f32[256,512]{0,1:T(8,128)} %collective-permute-done, bf16[1,1024,1792]{2,1,0:T(8,128)(2,1)} %param.6, s32[]{:T(128)S(6)} %select_n.38, bf16[512,1792]{1,0:T(8,128)(2,1)S(1)} %copy-done.1, ...), kind=kOutput, calls=%fused_computation.27 | convolution fusion | flops 605421568 | bytes 5898756 | tf_op jit(solution)/shard_map/dot_general | solution.py:19
  (12 shorter events, 0.0 us)
Async XLA Ops:
  0.6 9.8 %copy-start.1 = (bf16[512,1792]{1,0:T(8,128)(2,1)S(1)}, bf16[512,1792]{1,0:T(8,128)(2,1)}, u32[]{:S(2)}) copy-start(bf16[512,1792]{1,0:T(8,128)(2,1)} %param.4) | copy-start | bytes 5505028
  6.1 41.4 %collective-permute-start.9 = (bf16[256,512]{1,0:T(8,128)(2,1)}, bf16[256,512]{1,0:T(8,128)(2,1)}, u32[]{:S(2)}, u32[]{:S(2)}) collective-permute-start(bf16[256,512]{1,0:T(8,128)(2,1)} %convolution_convert_fusion.2), channel_id=1, source_target_pairs={{0,4},{2,6},{4,8},{6,10},{8,12},{10,14},{12,0},{14,2},{1,5},{3,7},... | collective-permute-start | bytes 786440 | tf_op jit(solution)/shard_map/ppermute | solution.py:11
  12.1 27.7 %collective-permute-start.4 = (bf16[96,2304]{1,0:T(8,128)(2,1)}, bf16[96,2304]{1,0:T(8,128)(2,1)}, u32[]{:S(2)}, u32[]{:S(2)}) collective-permute-start(bf16[96,2304]{1,0:T(8,128)(2,1)} %slice.44), channel_id=1, source_target_pairs={{0,2},{2,0},{4,6},{6,4},{8,10},{10,8},{12,14},{14,12},{1,3},{3,1},... | collective-permute-start | bytes 1327112 | tf_op jit(solution)/shard_map/ppermute | solution.py:11
  16.6 26.7 %copy-start.2 = (bf16[512,1024]{1,0:T(8,128)(2,1)S(1)}, bf16[512,1024]{1,0:T(8,128)(2,1)}, u32[]{:S(2)}) copy-start(bf16[512,1024]{1,0:T(8,128)(2,1)} %param.5) | copy-start | bytes 3145732
  16.6 62.5 %collective-permute-start = (f32[256,512]{0,1:T(8,128)}, f32[256,512]{0,1:T(8,128)}, u32[]{:S(2)}, u32[]{:S(2)}) collective-permute-start(f32[256,512]{0,1:T(8,128)} %fusion.36), channel_id=1, source_target_pairs={{0,1},{1,0},{2,3},{3,2},{4,5},{5,4},{6,7},{7,6},{8,9},{9,8},{10,11... | collective-permute-start | bytes 1572872 | tf_op jit(solution)/shard_map/ppermute | solution.py:15
  17.5 37.3 %collective-permute-start.6 = (bf16[160,2304]{1,0:T(8,128)(2,1)}, bf16[160,2304]{1,0:T(8,128)(2,1)S(1)}, u32[]{:S(2)}, u32[]{:S(2)}) collective-permute-start(bf16[160,2304]{1,0:T(8,128)(2,1)} %slice.45), channel_id=1, source_target_pairs={{0,2},{2,4},{4,6},{6,8},{8,10},{10,12},{12,14},{14,0},{1,3},{3,5},... | collective-permute-start | bytes 2211848 | tf_op jit(solution)/shard_map/ppermute | solution.py:11
  19.7 38.0 %collective-permute-start.1 = (bf16[256,1792]{1,0:T(8,128)(2,1)}, bf16[256,1792]{1,0:T(8,128)(2,1)S(1)}, u32[]{:S(2)}, u32[]{:S(2)}) collective-permute-start(bf16[256,1792]{1,0:T(8,128)(2,1)} %convolution_convert_fusion.1), channel_id=1, source_target_pairs={{0,4},{2,6},{4,8},{6,10},{8,12},{10,14},{12,0},{14,2},{1,5},{3,7},... | collective-permute-start | bytes 2752520 | tf_op jit(solution)/shard_map/ppermute | solution.py:11
  39.8 13.9 %collective-permute-start.5 = (bf16[96,2304]{1,0:T(8,128)(2,1)}, bf16[96,2304]{1,0:T(8,128)(2,1)}, u32[]{:S(2)}, u32[]{:S(2)}) collective-permute-start(bf16[96,2304]{1,0:T(8,128)(2,1)} %collective-permute-done.4), channel_id=1, source_target_pairs={{0,4},{4,8},{8,12},{12,0},{1,5},{5,9},{9,13},{13,1},{16,20},{20,24... | collective-permute-start | bytes 1327112 | tf_op jit(solution)/shard_map/ppermute | solution.py:11
  47.6 11.0 %collective-permute-start.10 = (bf16[256,512]{1,0:T(8,128)(2,1)}, bf16[256,512]{1,0:T(8,128)(2,1)S(1)}, u32[]{:S(2)}, u32[]{:S(2)}) collective-permute-start(bf16[256,512]{1,0:T(8,128)(2,1)} %collective-permute-done.9), channel_id=1, source_target_pairs={{0,1},{1,0},{2,3},{3,2},{4,5},{5,4},{6,7},{7,6},{8,9},{9,8},{10,11... | collective-permute-start | bytes 786440 | tf_op jit(solution)/shard_map/ppermute | solution.py:15
  54.8 2.8 %copy-start = (bf16[1,1024,1792]{2,1,0:T(8,128)(2,1)S(1)}, bf16[1,1024,1792]{2,1,0:T(8,128)(2,1)}, u32[]{:S(2)}) copy-start(bf16[1,1024,1792]{2,1,0:T(8,128)(2,1)} %param.6) | copy-start | bytes 11010052
  54.9 11.3 %collective-permute-start.11 = (bf16[256,512]{1,0:T(8,128)(2,1)S(1)}, bf16[256,512]{1,0:T(8,128)(2,1)S(1)}, u32[]{:S(2)}, u32[]{:S(2)}) collective-permute-start(bf16[256,512]{1,0:T(8,128)(2,1)S(1)} %pad_maximum_fusion), channel_id=1, source_target_pairs={{0,1},{1,0},{2,3},{3,2},{4,5},{5,4},{6,7},{7,6},{8,9},{9,8},{10,11... | collective-permute-start | bytes 786440 | tf_op jit(solution)/shard_map/ppermute | solution.py:15
  57.3 4.0 %collective-permute-start.7 = (f32[256,512]{1,0:T(8,128)S(1)}, f32[256,512]{1,0:T(8,128)S(1)}, u32[]{:S(2)}, u32[]{:S(2)}) collective-permute-start(f32[256,512]{1,0:T(8,128)S(1)} %fusion.4), channel_id=1, source_target_pairs={{0,1},{1,0},{2,3},{3,2},{4,5},{5,4},{6,7},{7,6},{8,9},{9,8},{10,11... | collective-permute-start | bytes 1572872 | tf_op jit(solution)/shard_map/ppermute | solution.py:15
  57.7 8.5 %slice-start = ((s8[7340032]{0:T(1024)(128)(4,1)}), s8[4194304]{0:T(1024)(128)(4,1)S(1)}, s32[]{:S(2)}) async-start(s8[7340032]{0:T(1024)(128)(4,1)} %bitcast.54), calls=%async_computation | async-start | bytes 8388608
  58.3 7.8 %slice-start.1 = ((s8[7340032]{0:T(1024)(128)(4,1)}), s8[3145728]{0:T(1024)(128)(4,1)S(1)}, s32[]{:S(2)}) async-start(s8[7340032]{0:T(1024)(128)(4,1)} %bitcast.54), calls=%async_computation.1 | async-start | bytes 6291456
  58.4 5.3 %collective-permute-start.2 = (f32[256,512]{1,0:T(8,128)S(1)}, f32[256,512]{1,0:T(8,128)S(1)}, u32[]{:S(2)}, u32[]{:S(2)}) collective-permute-start(f32[256,512]{1,0:T(8,128)S(1)} %fusion.6), channel_id=1, source_target_pairs={{0,1},{1,0},{2,3},{3,2},{4,5},{5,4},{6,7},{7,6},{8,9},{9,8},{10,11... | collective-permute-start | bytes 1572872 | tf_op jit(solution)/shard_map/ppermute | solution.py:15
  62.0 8.9 %collective-permute-start.8 = (bf16[256,512]{1,0:T(8,128)(2,1)S(1)}, bf16[256,512]{1,0:T(8,128)(2,1)S(1)}, u32[]{:S(2)}, u32[]{:S(2)}) collective-permute-start(bf16[256,512]{1,0:T(8,128)(2,1)S(1)} %fusion.42), channel_id=1, source_target_pairs={{2,0},{4,2},{6,4},{8,6},{10,8},{12,10},{14,12},{0,14},{3,1},{5,3},... | collective-permute-start | bytes 786440 | tf_op jit(solution)/shard_map/ppermute | solution.py:11
  64.3 13.4 %collective-permute-start.3 = (bf16[256,512]{1,0:T(8,128)(2,1)S(1)}, bf16[256,512]{1,0:T(8,128)(2,1)S(1)}, u32[]{:S(2)}, u32[]{:S(2)}) collective-permute-start(bf16[256,512]{1,0:T(8,128)(2,1)S(1)} %fusion.45), channel_id=1, source_target_pairs={{4,0},{6,2},{8,4},{10,6},{12,8},{14,10},{0,12},{2,14},{5,1},{7,3},... | collective-permute-start | bytes 786440 | tf_op jit(solution)/shard_map/ppermute | solution.py:11

commit v2 on v1

v2 whole, which is shorter than its diff:
```python
import jax
import jax.numpy as jnp
from jax import lax
from jax.experimental import pallas as pl
from jax.experimental.pallas import tpu as pltpu
from jax.sharding import PartitionSpec as P

CAP = 256
RELAYED = 128
TILE = 256
BF16, F32 = jnp.bfloat16, jnp.float32
VMEM = pl.BlockSpec(memory_space=pltpu.VMEM)
SMEM = pl.BlockSpec(memory_space=pltpu.SMEM)
ANY = pl.BlockSpec(memory_space=pl.ANY)


def call(kernel, outs, *operands, after=(), scalars=0, grid=None, out_specs=None, cost=10**10):
    def body(*refs):
        kernel(*refs[: len(operands)], *refs[len(operands) + len(after) :])

    extra = {} if grid is None else {"grid": grid}
    return pl.pallas_call(
        body,
        out_shape=[jax.ShapeDtypeStruct(shape, dtype) for shape, dtype in outs],
        in_specs=[SMEM] * scalars + [VMEM] * (len(operands) - scalars) + [ANY] * len(after),
        out_specs=[VMEM] * len(outs) if out_specs is None else out_specs,
        cost_estimate=pl.CostEstimate(flops=cost, bytes_accessed=10**3, transcendentals=0),
        compiler_params=pltpu.CompilerParams(vmem_limit_bytes=16 << 20),
        name=kernel.__name__,
        **extra,
    )(*operands, *after)


def dot(left, right, contract=(1, 0)):
    return lax.dot_general(left, right, ((contract[:1], contract[1:]), ((), ())), preferred_element_type=F32)


def half_of(which, extent):
    return pl.ds(pl.multiple_of(which * extent, extent), extent)


def segment(counts, index):
    first = jnp.int32(0)
    for earlier in range(index):
        first = first + counts[0, earlier]
    return first, counts[0, index]


def picker(counts, index, rows):
    first, count = segment(counts, index)
    place = lax.broadcasted_iota(jnp.int32, (CAP, rows), 0)
    row = lax.broadcasted_iota(jnp.int32, (CAP, rows), 1)
    return ((row == first + place) & (place < count)).astype(BF16)


def placer(counts, index, rows):
    first, count = segment(counts, index)
    row = lax.broadcasted_iota(jnp.int32, (rows, CAP), 0)
    place = lax.broadcasted_iota(jnp.int32, (rows, CAP), 1)
    return ((row == first + place) & (place < count)).astype(BF16)


def tiles(extent):
    return [slice(at, min(at + TILE, extent)) for at in range(0, extent, TILE)]


def pick_far(counts, grad_out, far):
    pick = picker(counts, 2, grad_out.shape[0])
    for tile in tiles(grad_out.shape[1]):
        far[:, tile] = dot(pick, grad_out[:, tile]).astype(BF16)


def pick_turned(counts, grad_out, turned):
    pick = picker(counts, 1, grad_out.shape[0])[:RELAYED]
    for tile in tiles(grad_out.shape[1]):
        turned[:, tile] = dot(pick, grad_out[:, tile]).astype(BF16)


def pick_direct(counts, grad_out, direct):
    pick = picker(counts, 1, grad_out.shape[0])[RELAYED:]
    for tile in tiles(grad_out.shape[1]):
        direct[:, tile] = dot(pick, grad_out[:, tile]).astype(BF16)


def pick_hidden(counts, hidden, far, near, own, places):
    rows, units = hidden.shape
    columns = half_of(lax.axis_index("loc"), units // 2)
    for index, out in ((2, far), (1, near)):
        out[...] = dot(hidden[:, columns], picker(counts, index, rows), (0, 1)).astype(BF16)
    pick = picker(counts, 0, rows)
    for tile in tiles(units):
        own[tile, :] = dot(hidden[:, tile], pick, (0, 1)).astype(BF16)
    for index in range(3):
        places[:, index * CAP : (index + 1) * CAP] = placer(counts, index, rows)


def product_away(grad, weights, away):
    half = weights.shape[1] // 2
    away[...] = dot(grad[:CAP, :], weights[0, half_of(1 - lax.axis_index("loc"), half), :], (1, 1))


def product_here(grad, weights, here):
    half = weights.shape[1] // 2
    here[...] = dot(grad[:CAP, :], weights[0, half_of(lax.axis_index("loc"), half), :], (1, 1))


def join_near(turned, relayed, direct, weights, near, away):
    odd = lax.axis_index("grp") % 2 == 1

    @pl.when(odd)
    def _():
        near[:RELAYED, :] = turned[...]

    @pl.when(jnp.logical_not(odd))
    def _():
        near[:RELAYED, :] = relayed[...]

    near[RELAYED:, :] = direct[...]
    product_away(near, weights, away)


def add_halves(here, other, out):
    out[...] = (here[...] + other[...]).astype(BF16)


def place_rows(places, own, near, far, out):
    total = dot(places[:, :CAP], own[...])
    total = total + dot(places[:, CAP : 2 * CAP], near[...])
    total = total + dot(places[:, 2 * CAP :], far[...])
    out[...] = total.astype(BF16)


def weight_gradient_here(own_hidden, far_hidden, near_hidden, own, far, near, out):
    columns = half_of(pl.program_id(0), TILE)
    rows = half_of(lax.axis_index("loc"), far_hidden.shape[0])
    total = dot(own_hidden[rows, :], own[:CAP, columns])
    total = total + dot(far_hidden[...], far[:, columns])
    total = total + dot(near_hidden[...], near[:, columns])
    out[...] = total.astype(BF16)


def weight_gradient(own_hidden, far_hidden, near_hidden, own, far, near, here, out):
    columns = half_of(pl.program_id(0), TILE)
    core = lax.axis_index("loc")
    half = far_hidden.shape[0]
    rows = half_of(1 - core, half)
    total = dot(own_hidden[rows, :], own[:CAP, columns])
    total = total + dot(far_hidden[...], far[:, columns])
    total = total + dot(near_hidden[...], near[:, columns])
    out[0, rows, :] = total.astype(BF16)
    out[0, half_of(core, half), :] = here[:, columns]


def local(grad_out, hidden, weights, counts):
    size = lax.axis_size("grp")
    rows, features = grad_out.shape
    units = hidden.shape[1]
    half = units // 2

    by1 = [(g, (g + 1) % size) for g in range(size)]
    by2 = [(g, (g + 2) % size) for g in range(size)]
    back1 = [(b, a) for a, b in by1]
    back2 = [(b, a) for a, b in by2]
    turn = [(g, g ^ 1) for g in range(size)]
    even_by2 = by2[::2]

    def send(value, pairs):
        return lax.ppermute(value, "grp", pairs)

    def swap_cores(value):
        return lax.ppermute(value, "loc", [(0, 1), (1, 0)])

    partial = ((CAP, half), F32)
    block = ((CAP, half), BF16)
    (far,) = call(pick_far, [((CAP, features), BF16)], counts, grad_out, scalars=1)
    far_in = send(far, by2)
    (turned,) = call(pick_turned, [((RELAYED, features), BF16)], counts, grad_out, scalars=1, after=(far,))
    turned_in = send(turned, turn)

    (own_away,) = call(product_away, [partial], grad_out, weights, after=(turned,))
    own_other = swap_cores(own_away)
    (own_here,) = call(product_here, [partial], grad_out, weights, after=(own_away,))
    far_hidden, near_hidden, own_hidden, places = call(
        pick_hidden,
        [((half, CAP), BF16), ((half, CAP), BF16), ((units, CAP), BF16), ((rows, 3 * CAP), BF16)],
        counts, hidden, scalars=1, after=(own_here,),
    )
    (direct,) = call(
        pick_direct, [((CAP - RELAYED, features), BF16)], counts, grad_out, scalars=1, after=(places,)
    )
    direct_in = send(direct, by1)
    (own_block,) = call(add_halves, [block], own_here, own_other, after=(direct,))

    turned_in, own_block = lax.optimization_barrier((turned_in, own_block))
    relayed_in = send(turned_in, even_by2)

    (far_away,) = call(product_away, [partial], far_in, weights, after=(turned_in,))
    far_other = swap_cores(far_away)
    (far_here,) = call(product_here, [partial], far_in, weights, after=(far_away,))
    (far_block,) = call(add_halves, [block], far_here, far_other)
    far_back = send(far_block, back2)
    far_hidden, near_hidden, far_here = lax.optimization_barrier((far_hidden, near_hidden, far_here))
    far_hidden_in = send(far_hidden, by2)
    near_hidden_in = send(near_hidden, by1)

    near_in, near_away = call(
        join_near, [((CAP, features), BF16), partial], turned_in, relayed_in, direct_in, weights, after=(far_block,)
    )
    near_other = swap_cores(near_away)
    (near_here,) = call(product_here, [partial], near_in, weights, after=(near_away,))
    (near_block,) = call(add_halves, [block], near_here, near_other)
    near_back = send(near_block, back1)

    far_hidden_in, near_hidden_in, near_block = lax.optimization_barrier((far_hidden_in, near_hidden_in, near_block))
    strips = (features // TILE,)
    (here,) = call(
        weight_gradient_here, [((half, features), BF16)],
        own_hidden, far_hidden_in, near_hidden_in, grad_out, far_in, near_in,
        grid=strips, out_specs=[pl.BlockSpec((half, TILE), lambda tile: (0, tile))],
    )
    (grad_hidden,) = call(
        place_rows, [((rows, half), BF16)], places, own_block, near_back, far_back, after=(here,)
    )
    (grad_weights,) = call(
        weight_gradient, [((1, units, features), BF16)],
        own_hidden, swap_cores(far_hidden_in), swap_cores(near_hidden_in), grad_out, far_in, near_in, here,
        grid=strips, out_specs=[pl.BlockSpec((1, units, TILE), lambda tile: (0, 0, tile))],
    )
    return grad_hidden, grad_weights


def solution(mesh):
    return jax.shard_map(
        local,
        mesh=mesh,
        in_specs=(
            P(("rep", "grp"), "loc"),
            P(("rep", "grp"), None),
            P("grp", None, "loc"),
            P(("rep", "grp"), None),
        ),
        out_specs=(P(("rep", "grp"), "loc"), P(("rep", "grp"), None, "loc")),
        check_vma=False,
    )
```

time: 83.3 us -> 63.5 us (0.76)
  the two profiles are of different devices: /device:TPU:0 before, /device:TPU:25 now
where the time goes in v2:
time: 63.5 us; the launch traced here: 63.3 us
  starting transfers between devices  21.8 us (34%)
  waiting for transfers between devices  20.8 us (33%)
  Pallas kernels  17.4 us (27%)
  local copies, waits for them, and re-layouts  2.42 us (4%)
  between operations  0.84 us (1%)
    ppermute x8, waiting for transfers between devices, send(): return lax.ppermute(value, 'grp', pairs)  19.9 us
    pallas_call x16, Pallas kernels, call(): pl.pallas_call(body, out_shape=[jax.ShapeDtypeStruct(shape, dtype) for sh...  17.4 us
    ppermute x5, starting transfers between devices, swap_cores(): return lax.ppermute(value, 'loc', [(0, 1), (1, 0)])  13.4 us
    ppermute x8, starting transfers between devices, send(): return lax.ppermute(value, 'grp', pairs)  8.38 us
    unnamed x10, local copies, waits for them, and re-layouts  2.42 us
  transfers between devices with their start and end apart: 13, of which 5 were waited for; matrix products, arithmetic and copies ran while one was open for 0% of the time, Pallas kernels for 24%

profile of v2, /device:TPU:25, one launch (start us, length us, event | category | flops | bytes accessed | tf_op | source)
XLA Modules:
  0.0 63.3 jit_solution(518135241176055772)
XLA Ops:
  0.6 0.0 copy-start.1
  0.6 1.5 %copy-done.1 = bf16[512,1792]{1,0:T(8,128)(2,1)S(1)} copy-done((bf16[512,1792]{1,0:T(8,128)(2,1)S(1)}, bf16[512,1792]{1,0:T(8,128)(2,1)}, u32[]{:S(2)}) %copy-start.1) | copy-done | bytes 1835032
  2.1 0.7 %copy-done.4 = s32[1,3]{1,0:T(1,128)S(1)} copy-done((s32[1,3]{1,0:T(1,128)S(1)}, s32[1,3]{1,0:T(1,128)}, u32[]{:S(2)}) %copy-start.4) | copy-done | bytes 36
  2.8 1.2 %pick_far.1.refs_2_ = bf16[256,1792]{1,0:T(8,128)(2,1)S(1)} custom-call(s32[1,3]{1,0:T(1,128)S(1)} %copy-done.4, bf16[512,1792]{1,0:T(8,128)(2,1)S(1)} %copy-done.1), custom_call_target="tpu_custom_call" | custom-call | flops 10000000000 | bytes 1000 | tf_op jit(solution)/shard_map/pick_far/pallas_call | solution.py:22
  4.0 0.0 copy-start
  4.0 0.0 copy-start.2
  4.0 0.1 collective-permute-start.4
  4.1 0.9 %pick_turned.1.refs_2_ = bf16[128,1792]{1,0:T(8,128)(2,1)S(1)} custom-call(s32[1,3]{1,0:T(1,128)S(1)} %copy-done.4, bf16[512,1792]{1,0:T(8,128)(2,1)S(1)} %copy-done.1, bf16[256,1792]{1,0:T(8,128)(2,1)S(1)} %pick_far.1.refs_2_), custom_call_target="tpu_custom_call" | custom-call | flops 10000000000 | bytes 1000 | tf_op jit(solution)/shard_map/pick_turned/pallas_call | solution.py:22
  5.0 1.3 %collective-permute-start = (bf16[128,1792]{1,0:T(8,128)(2,1)S(1)}, bf16[128,1792]{1,0:T(8,128)(2,1)S(1)}, u32[]{:S(2)}, u32[]{:S(2)}) collective-permute-start(bf16[128,1792]{1,0:T(8,128)(2,1)S(1)} %pick_turned.1.refs_2_), channel_id=1, source_target_pairs={{0,2},{2,0},{4,6},{6,4},{8,10},{10,8},{12,14},{14,12},{1,3},{3,1},... | collective-permute-start | bytes 1376264 | tf_op jit(solution)/shard_map/ppermute | solution.py:168
  6.3 0.0 copy-done
  6.3 0.3 copy-done.2
  6.6 0.7 %product_away.2.refs_2_ = f32[256,512]{1,0:T(8,128)S(1)} custom-call(bf16[512,1792]{1,0:T(8,128)(2,1)S(1)} %copy-done.2, bf16[1,1024,1792]{2,1,0:T(8,128)(2,1)S(1)} %copy-done, bf16[128,1792]{1,0:T(8,128)(2,1)S(1)} %pick_turned.1.refs_2_), custom_call_target="tpu_custom_call" | custom-call | flops 10000000000 | bytes 1000 | tf_op jit(solution)/shard_map/product_away/pallas_call | solution.py:22
  7.3 0.0 copy-start.3
  7.3 1.0 %collective-permute-start.1 = (f32[256,512]{1,0:T(8,128)S(1)}, f32[256,512]{1,0:T(8,128)S(1)}, u32[]{:S(2)}, u32[]{:S(2)}) collective-permute-start(f32[256,512]{1,0:T(8,128)S(1)} %product_away.2.refs_2_), channel_id=1, source_target_pairs={{0,1},{1,0},{2,3},{3,2},{4,5},{5,4},{6,7},{7,6},{8,9},{9,8},{10,11... | collective-permute-start | bytes 1572872 | tf_op jit(solution)/shard_map/ppermute | solution.py:171
  8.2 0.7 %product_here.3.refs_2_.refs_0_ = f32[256,512]{1,0:T(8,128)S(1)} custom-call(bf16[512,1792]{1,0:T(8,128)(2,1)S(1)} %copy-done.2, bf16[1,1024,1792]{2,1,0:T(8,128)(2,1)S(1)} %copy-done, f32[256,512]{1,0:T(8,128)S(1)} %product_away.2.refs_2_), custom_call_target="tpu_custom_call" | custom-call | flops 10000000000 | bytes 1000 | tf_op jit(solution)/shard_map/product_here/pallas_call | solution.py:22
  8.9 0.0 copy-done.3
  8.9 1.4 %pick_hidden.1 = (bf16[512,256]{1,0:T(8,128)(2,1)S(1)}, bf16[512,256]{1,0:T(8,128)(2,1)S(1)}, bf16[1024,256]{1,0:T(8,128)(2,1)S(1)}, bf16[512,768]{1,0:T(8,128)(2,1)S(1)}) custom-call(s32[1,3]{1,0:T(1,128)S(1)} %copy-done.4, bf16[512,1024]{1,0:T(8,128)(2,1)S(1)} %copy-done.3, f32[256,512]{1,0:T(8,128)S(1)} %product_here.3.refs_2_.refs_0_), custom_call_target="tpu_custom_call" | custom-call | flops 10000000000 | bytes 1000 | tf_op jit(solution)/shard_map/pick_hidden/pallas_call | solution.py:22
  10.4 0.9 %pick_direct.1.refs_2_ = bf16[128,1792]{1,0:T(8,128)(2,1)S(1)} custom-call(s32[1,3]{1,0:T(1,128)S(1)} %copy-done.4, bf16[512,1792]{1,0:T(8,128)(2,1)S(1)} %copy-done.2, bf16[512,768]{1,0:T(8,128)(2,1)S(1)} %get-tuple-element.14.refs_2_.refs_0_), custom_call_target="tpu_custom_call" | custom-call | flops 10000000000 | bytes 1000 | tf_op jit(solution)/shard_map/pick_direct/pallas_call | solution.py:22
  11.3 1.1 %collective-permute-start.3 = (bf16[128,1792]{1,0:T(8,128)(2,1)S(1)}, bf16[128,1792]{1,0:T(8,128)(2,1)S(1)}, u32[]{:S(2)}, u32[]{:S(2)}) collective-permute-start(bf16[128,1792]{1,0:T(8,128)(2,1)S(1)} %pick_direct.1.refs_2_), channel_id=1, source_target_pairs={{0,2},{2,4},{4,6},{6,8},{8,10},{10,12},{12,14},{14,0},{1,3},{3,5},... | collective-permute-start | bytes 1376264 | tf_op jit(solution)/shard_map/ppermute | solution.py:168
  12.4 0.0 collective-permute-done.1.refs_1_
  12.4 4.0 %collective-permute-done.refs_2_.refs_0_ = bf16[128,1792]{1,0:T(8,128)(2,1)S(1)} collective-permute-done((bf16[128,1792]{1,0:T(8,128)(2,1)S(1)}, bf16[128,1792]{1,0:T(8,128)(2,1)S(1)}, u32[]{:S(2)}, u32[]{:S(2)}) %collective-permute-start) | collective-permute-done | bytes 458784 | tf_op jit(solution)/shard_map/ppermute | solution.py:168
  16.5 2.8 %collective-permute-start.2 = (bf16[128,1792]{1,0:T(8,128)(2,1)S(1)}, bf16[128,1792]{1,0:T(8,128)(2,1)S(1)}, u32[]{:S(2)}, u32[]{:S(2)}) collective-permute-start(bf16[128,1792]{1,0:T(8,128)(2,1)S(1)} %collective-permute-done.refs_2_.refs_0_), channel_id=1, source_target_pairs={{0,4},{4,8},{8,12},{12,0},{1,5},{5,9},{9,13},{13,1},{16,20},{20,24... | collective-permute-start | bytes 1376264 | tf_op jit(solution)/shard_map/ppermute | solution.py:168
  19.3 6.0 %collective-permute-done.4.refs_0_.refs_4_ = bf16[256,1792]{1,0:T(8,128)(2,1)S(1)} collective-permute-done((bf16[256,1792]{1,0:T(8,128)(2,1)S(1)}, bf16[256,1792]{1,0:T(8,128)(2,1)S(1)}, u32[]{:S(2)}, u32[]{:S(2)}) %collective-permute-start.4) | collective-permute-done | bytes 917536 | tf_op jit(solution)/shard_map/ppermute | solution.py:168
  25.3 0.7 %product_away.3.refs_2_ = f32[256,512]{1,0:T(8,128)S(1)} custom-call(bf16[256,1792]{1,0:T(8,128)(2,1)S(1)} %collective-permute-done.4.refs_0_.refs_4_, bf16[1,1024,1792]{2,1,0:T(8,128)(2,1)S(1)} %copy-done, bf16[128,1792]{1,0:T(8,128)(2,1)S(1)} %collective-permute-done.refs_2_.refs_0_), custom_call_target="tpu_custom_call" | custom-call | flops 10000000000 | bytes 1000 | tf_op jit(solution)/shard_map/product_away/pallas_call | solution.py:22
  25.9 2.8 %collective-permute-start.5 = (f32[256,512]{1,0:T(8,128)S(1)}, f32[256,512]{1,0:T(8,128)S(1)}, u32[]{:S(2)}, u32[]{:S(2)}) collective-permute-start(f32[256,512]{1,0:T(8,128)S(1)} %product_away.3.refs_2_), channel_id=1, source_target_pairs={{0,1},{1,0},{2,3},{3,2},{4,5},{5,4},{6,7},{7,6},{8,9},{9,8},{10,11... | collective-permute-start | bytes 1572872 | tf_op jit(solution)/shard_map/ppermute | solution.py:171
  28.7 0.7 %product_here.4.refs_0_ = f32[256,512]{1,0:T(8,128)S(1)} custom-call(bf16[256,1792]{1,0:T(8,128)(2,1)S(1)} %collective-permute-done.4.refs_0_.refs_4_, bf16[1,1024,1792]{2,1,0:T(8,128)(2,1)S(1)} %copy-done, f32[256,512]{1,0:T(8,128)S(1)} %product_away.3.refs_2_), custom_call_target="tpu_custom_call" | custom-call | flops 10000000000 | bytes 1000 | tf_op jit(solution)/shard_map/product_here/pallas_call | solution.py:22
  29.4 1.5 %collective-permute-start.9 = (bf16[512,256]{1,0:T(8,128)(2,1)S(1)}, bf16[512,256]{1,0:T(8,128)(2,1)S(1)}, u32[]{:S(2)}, u32[]{:S(2)}) collective-permute-start(bf16[512,256]{1,0:T(8,128)(2,1)S(1)} %get-tuple-element.22), channel_id=1, source_target_pairs={{0,4},{2,6},{4,8},{6,10},{8,12},{10,14},{12,0},{14,2},{1,5},{3,7},... | collective-permute-start | bytes 786440 | tf_op jit(solution)/shard_map/ppermute | solution.py:168
  30.9 1.5 %collective-permute-start.10 = (bf16[512,256]{1,0:T(8,128)(2,1)S(1)}, bf16[512,256]{1,0:T(8,128)(2,1)S(1)}, u32[]{:S(2)}, u32[]{:S(2)}) collective-permute-start(bf16[512,256]{1,0:T(8,128)(2,1)S(1)} %get-tuple-element.23), channel_id=1, source_target_pairs={{0,2},{2,4},{4,6},{6,8},{8,10},{10,12},{12,14},{14,0},{1,3},{3,5},... | collective-permute-start | bytes 786440 | tf_op jit(solution)/shard_map/ppermute | solution.py:168
  32.4 0.0 collective-permute-done.5.refs_1_
  32.5 0.1 collective-permute-start.8
  32.5 3.5 %collective-permute-done.3.refs_2_ = bf16[128,1792]{1,0:T(8,128)(2,1)S(1)} collective-permute-done((bf16[128,1792]{1,0:T(8,128)(2,1)S(1)}, bf16[128,1792]{1,0:T(8,128)(2,1)S(1)}, u32[]{:S(2)}, u32[]{:S(2)}) %collective-permute-start.3) | collective-permute-done | bytes 458784 | tf_op jit(solution)/shard_map/ppermute | solution.py:168
  36.1 0.0 collective-permute-done.2.refs_1_
  36.1 0.7 %join_near.1 = (bf16[256,1792]{1,0:T(8,128)(2,1)S(1)}, f32[256,512]{1,0:T(8,128)S(1)}) custom-call(bf16[128,1792]{1,0:T(8,128)(2,1)S(1)} %collective-permute-done.refs_2_.refs_0_, bf16[128,1792]{1,0:T(8,128)(2,1)S(1)} %collective-permute-done.2.refs_1_, bf16[128,1792]{1,0:T(8,128)(2,1)S(1)} %collective-permute-done.3.refs_2_, ...), custom_call_target="tpu_custom_call" | custom-call | flops 10000000000 | bytes 1000 | tf_op jit(solution)/shard_map/join_near/pallas_call | solution.py:22
  36.8 2.8 %collective-permute-start.6 = (f32[256,512]{1,0:T(8,128)S(1)}, f32[256,512]{1,0:T(8,128)S(1)}, u32[]{:S(2)}, u32[]{:S(2)}) collective-permute-start(f32[256,512]{1,0:T(8,128)S(1)} %get-tuple-element.18.refs_2_), channel_id=1, source_target_pairs={{0,1},{1,0},{2,3},{3,2},{4,5},{5,4},{6,7},{7,6},{8,9},{9,8},{10,11... | collective-permute-start | bytes 1572872 | tf_op jit(solution)/shard_map/ppermute | solution.py:171
  39.5 0.7 %product_here.5.refs_0_ = f32[256,512]{1,0:T(8,128)S(1)} custom-call(bf16[256,1792]{1,0:T(8,128)(2,1)S(1)} %get-tuple-element.17.refs_0_.refs_5_, bf16[1,1024,1792]{2,1,0:T(8,128)(2,1)S(1)} %copy-done, f32[256,512]{1,0:T(8,128)S(1)} %get-tuple-element.18.refs_2_), custom_call_target="tpu_custom_call" | custom-call | flops 10000000000 | bytes 1000 | tf_op jit(solution)/shard_map/product_here/pallas_call | solution.py:22
  40.2 0.9 %collective-permute-done.6.refs_1_ = f32[256,512]{1,0:T(8,128)S(1)} collective-permute-done((f32[256,512]{1,0:T(8,128)S(1)}, f32[256,512]{1,0:T(8,128)S(1)}, u32[]{:S(2)}, u32[]{:S(2)}) %collective-permute-start.6) | collective-permute-done | bytes 524320 | tf_op jit(solution)/shard_map/ppermute | solution.py:171
  41.1 0.1 collective-permute-start.7
  41.2 0.0 collective-permute-done.9.refs_1_
  41.2 6.4 %collective-permute-done.10.refs_2_ = bf16[512,256]{1,0:T(8,128)(2,1)S(1)} collective-permute-done((bf16[512,256]{1,0:T(8,128)(2,1)S(1)}, bf16[512,256]{1,0:T(8,128)(2,1)S(1)}, u32[]{:S(2)}, u32[]{:S(2)}) %collective-permute-start.10) | collective-permute-done | bytes 262176 | tf_op jit(solution)/shard_map/ppermute | solution.py:168
  47.6 6.9 %collective-permute-start.11 = (bf16[512,256]{1,0:T(8,128)(2,1)S(1)}, bf16[512,256]{1,0:T(8,128)(2,1)S(1)}, u32[]{:S(2)}, u32[]{:S(2)}) collective-permute-start(bf16[512,256]{1,0:T(8,128)(2,1)S(1)} %collective-permute-done.9.refs_1_), channel_id=1, source_target_pairs={{0,1},{1,0},{2,3},{3,2},{4,5},{5,4},{6,7},{7,6},{8,9},{9,8},{10,11... | collective-permute-start | bytes 786440 | tf_op jit(solution)/shard_map/ppermute | solution.py:171
  54.5 0.0 collective-permute-start.12
  54.5 2.7 %weight_gradient_here.1.refs_4_.refs_6_ = bf16[512,1792]{1,0:T(8,128)(2,1)S(1)} custom-call(bf16[1024,256]{1,0:T(8,128)(2,1)S(1)} %get-tuple-element.19.refs_0_, bf16[512,256]{1,0:T(8,128)(2,1)S(1)} %collective-permute-done.9.refs_1_, bf16[512,256]{1,0:T(8,128)(2,1)S(1)} %collective-permute-done.10.refs_2_, bf16[512,1792]{1,0:T(8,128)(2,1)S(1)} %copy-done.2, ...), custom_call_target="tpu_custom_call" | custom-call | flops 10000000000 | bytes 1000 | tf_op jit(solution)/shard_map/weight_gradient_here/pallas_call | solution.py:22
  57.2 0.0 collective-permute-done.11.refs_1_
  57.2 0.0 collective-permute-done.12.refs_2_
  57.2 4.7 %weight_gradient.1 = bf16[1,1024,1792]{2,1,0:T(8,128)(2,1)} custom-call(bf16[1024,256]{1,0:T(8,128)(2,1)S(1)} %get-tuple-element.19.refs_0_, bf16[512,256]{1,0:T(8,128)(2,1)S(1)} %collective-permute-done.11.refs_1_, bf16[512,256]{1,0:T(8,128)(2,1)S(1)} %collective-permute-done.12.refs_2_, bf16[512,1792]{1,0:T(8,128)(2,1)S(1)} %copy-done.2, ...), custom_call_target="tpu_custom_call" | custom-call | flops 10000000000 | bytes 1000 | tf_op jit(solution)/shard_map/weight_gradient/pallas_call | solution.py:22
  61.9 0.0 collective-permute-done.8.refs_3_
  61.9 0.0 collective-permute-done.7.refs_2_
  61.9 1.4 %place_rows.1 = bf16[512,512]{1,0:T(8,128)(2,1)} custom-call(bf16[512,768]{1,0:T(8,128)(2,1)S(1)} %get-tuple-element.14.refs_2_.refs_0_, bf16[256,512]{1,0:T(8,128)(2,1)S(1)} %add_halves.3.refs_1_, bf16[256,512]{1,0:T(8,128)(2,1)S(1)} %collective-permute-done.7.refs_2_, bf16[256,512]{1,0:T(8,128)(2,1)S(1)} %collective-permute-done.8.refs_3_, ...), custom_call_target="tpu_custom_call" | custom-call | flops 10000000000 | bytes 1000 | tf_op jit(solution)/shard_map/place_rows/pallas_call | solution.py:22
  (4 shorter events, 0.1 us)
Async XLA Ops:
  0.6 1.5 %copy-start.1 = (bf16[512,1792]{1,0:T(8,128)(2,1)S(1)}, bf16[512,1792]{1,0:T(8,128)(2,1)}, u32[]{:S(2)}) copy-start(bf16[512,1792]{1,0:T(8,128)(2,1)} %refs_3_.5) | copy-start | bytes 5505028
  2.1 0.7 %copy-start.4 = (s32[1,3]{1,0:T(1,128)S(1)}, s32[1,3]{1,0:T(1,128)}, u32[]{:S(2)}) copy-start(s32[1,3]{1,0:T(1,128)} %refs_0_.11) | copy-start | bytes 40
  4.0 2.4 %copy-start = (bf16[1,1024,1792]{2,1,0:T(8,128)(2,1)S(1)}, bf16[1,1024,1792]{2,1,0:T(8,128)(2,1)}, u32[]{:S(2)}) copy-start(bf16[1,1024,1792]{2,1,0:T(8,128)(2,1)} %refs_1_.17) | copy-start | bytes 11010052
  4.0 2.6 %copy-start.2 = (bf16[512,1792]{1,0:T(8,128)(2,1)S(1)}, bf16[512,1792]{1,0:T(8,128)(2,1)}, u32[]{:S(2)}) copy-start(bf16[512,1792]{1,0:T(8,128)(2,1)} %refs_3_.5) | copy-start | bytes 5505028
  4.0 21.3 %collective-permute-start.4 = (bf16[256,1792]{1,0:T(8,128)(2,1)S(1)}, bf16[256,1792]{1,0:T(8,128)(2,1)S(1)}, u32[]{:S(2)}, u32[]{:S(2)}) collective-permute-start(bf16[256,1792]{1,0:T(8,128)(2,1)S(1)} %pick_far.1.refs_2_), channel_id=1, source_target_pairs={{0,4},{2,6},{4,8},{6,10},{8,12},{10,14},{12,0},{14,2},{1,5},{3,7},... | collective-permute-start | bytes 2752520 | tf_op jit(solution)/shard_map/ppermute | solution.py:168
  5.0 11.4 %collective-permute-start = (bf16[128,1792]{1,0:T(8,128)(2,1)S(1)}, bf16[128,1792]{1,0:T(8,128)(2,1)S(1)}, u32[]{:S(2)}, u32[]{:S(2)}) collective-permute-start(bf16[128,1792]{1,0:T(8,128)(2,1)S(1)} %pick_turned.1.refs_2_), channel_id=1, source_target_pairs={{0,2},{2,0},{4,6},{6,4},{8,10},{10,8},{12,14},{14,12},{1,3},{3,1},... | collective-permute-start | bytes 1376264 | tf_op jit(solution)/shard_map/ppermute | solution.py:168
  7.3 1.7 %copy-start.3 = (bf16[512,1024]{1,0:T(8,128)(2,1)S(1)}, bf16[512,1024]{1,0:T(8,128)(2,1)}, u32[]{:S(2)}) copy-start(bf16[512,1024]{1,0:T(8,128)(2,1)} %refs_1_.13) | copy-start | bytes 3145732
  7.3 5.1 %collective-permute-start.1 = (f32[256,512]{1,0:T(8,128)S(1)}, f32[256,512]{1,0:T(8,128)S(1)}, u32[]{:S(2)}, u32[]{:S(2)}) collective-permute-start(f32[256,512]{1,0:T(8,128)S(1)} %product_away.2.refs_2_), channel_id=1, source_target_pairs={{0,1},{1,0},{2,3},{3,2},{4,5},{5,4},{6,7},{7,6},{8,9},{9,8},{10,11... | collective-permute-start | bytes 1572872 | tf_op jit(solution)/shard_map/ppermute | solution.py:171
  11.3 24.7 %collective-permute-start.3 = (bf16[128,1792]{1,0:T(8,128)(2,1)S(1)}, bf16[128,1792]{1,0:T(8,128)(2,1)S(1)}, u32[]{:S(2)}, u32[]{:S(2)}) collective-permute-start(bf16[128,1792]{1,0:T(8,128)(2,1)S(1)} %pick_direct.1.refs_2_), channel_id=1, source_target_pairs={{0,2},{2,4},{4,6},{6,8},{8,10},{10,12},{12,14},{14,0},{1,3},{3,5},... | collective-permute-start | bytes 1376264 | tf_op jit(solution)/shard_map/ppermute | solution.py:168
  16.5 19.6 %collective-permute-start.2 = (bf16[128,1792]{1,0:T(8,128)(2,1)S(1)}, bf16[128,1792]{1,0:T(8,128)(2,1)S(1)}, u32[]{:S(2)}, u32[]{:S(2)}) collective-permute-start(bf16[128,1792]{1,0:T(8,128)(2,1)S(1)} %collective-permute-done.refs_2_.refs_0_), channel_id=1, source_target_pairs={{0,4},{4,8},{8,12},{12,0},{1,5},{5,9},{9,13},{13,1},{16,20},{20,24... | collective-permute-start | bytes 1376264 | tf_op jit(solution)/shard_map/ppermute | solution.py:168
  25.9 6.5 %collective-permute-start.5 = (f32[256,512]{1,0:T(8,128)S(1)}, f32[256,512]{1,0:T(8,128)S(1)}, u32[]{:S(2)}, u32[]{:S(2)}) collective-permute-start(f32[256,512]{1,0:T(8,128)S(1)} %product_away.3.refs_2_), channel_id=1, source_target_pairs={{0,1},{1,0},{2,3},{3,2},{4,5},{5,4},{6,7},{7,6},{8,9},{9,8},{10,11... | collective-permute-start | bytes 1572872 | tf_op jit(solution)/shard_map/ppermute | solution.py:171
  29.4 11.8 %collective-permute-start.9 = (bf16[512,256]{1,0:T(8,128)(2,1)S(1)}, bf16[512,256]{1,0:T(8,128)(2,1)S(1)}, u32[]{:S(2)}, u32[]{:S(2)}) collective-permute-start(bf16[512,256]{1,0:T(8,128)(2,1)S(1)} %get-tuple-element.22), channel_id=1, source_target_pairs={{0,4},{2,6},{4,8},{6,10},{8,12},{10,14},{12,0},{14,2},{1,5},{3,7},... | collective-permute-start | bytes 786440 | tf_op jit(solution)/shard_map/ppermute | solution.py:168
  30.9 16.6 %collective-permute-start.10 = (bf16[512,256]{1,0:T(8,128)(2,1)S(1)}, bf16[512,256]{1,0:T(8,128)(2,1)S(1)}, u32[]{:S(2)}, u32[]{:S(2)}) collective-permute-start(bf16[512,256]{1,0:T(8,128)(2,1)S(1)} %get-tuple-element.23), channel_id=1, source_target_pairs={{0,2},{2,4},{4,6},{6,8},{8,10},{10,12},{12,14},{14,0},{1,3},{3,5},... | collective-permute-start | bytes 786440 | tf_op jit(solution)/shard_map/ppermute | solution.py:168
  32.5 29.5 %collective-permute-start.8 = (bf16[256,512]{1,0:T(8,128)(2,1)S(1)}, bf16[256,512]{1,0:T(8,128)(2,1)S(1)}, u32[]{:S(2)}, u32[]{:S(2)}) collective-permute-start(bf16[256,512]{1,0:T(8,128)(2,1)S(1)} %add_halves.4.refs_4_), channel_id=1, source_target_pairs={{4,0},{6,2},{8,4},{10,6},{12,8},{14,10},{0,12},{2,14},{5,1},{7,3},... | collective-permute-start | bytes 786440 | tf_op jit(solution)/shard_map/ppermute | solution.py:168
  36.8 4.3 %collective-permute-start.6 = (f32[256,512]{1,0:T(8,128)S(1)}, f32[256,512]{1,0:T(8,128)S(1)}, u32[]{:S(2)}, u32[]{:S(2)}) collective-permute-start(f32[256,512]{1,0:T(8,128)S(1)} %get-tuple-element.18.refs_2_), channel_id=1, source_target_pairs={{0,1},{1,0},{2,3},{3,2},{4,5},{5,4},{6,7},{7,6},{8,9},{9,8},{10,11... | collective-permute-start | bytes 1572872 | tf_op jit(solution)/shard_map/ppermute | solution.py:171
  41.1 20.8 %collective-permute-start.7 = (bf16[256,512]{1,0:T(8,128)(2,1)S(1)}, bf16[256,512]{1,0:T(8,128)(2,1)S(1)}, u32[]{:S(2)}, u32[]{:S(2)}) collective-permute-start(bf16[256,512]{1,0:T(8,128)(2,1)S(1)} %add_halves.5), channel_id=1, source_target_pairs={{2,0},{4,2},{6,4},{8,6},{10,8},{12,10},{14,12},{0,14},{3,1},{5,3},... | collective-permute-start | bytes 786440 | tf_op jit(solution)/shard_map/ppermute | solution.py:168
  47.6 9.7 %collective-permute-start.11 = (bf16[512,256]{1,0:T(8,128)(2,1)S(1)}, bf16[512,256]{1,0:T(8,128)(2,1)S(1)}, u32[]{:S(2)}, u32[]{:S(2)}) collective-permute-start(bf16[512,256]{1,0:T(8,128)(2,1)S(1)} %collective-permute-done.9.refs_1_), channel_id=1, source_target_pairs={{0,1},{1,0},{2,3},{3,2},{4,5},{5,4},{6,7},{7,6},{8,9},{9,8},{10,11... | collective-permute-start | bytes 786440 | tf_op jit(solution)/shard_map/ppermute | solution.py:171
  54.5 2.7 %collective-permute-start.12 = (bf16[512,256]{1,0:T(8,128)(2,1)S(1)}, bf16[512,256]{1,0:T(8,128)(2,1)S(1)}, u32[]{:S(2)}, u32[]{:S(2)}) collective-permute-start(bf16[512,256]{1,0:T(8,128)(2,1)S(1)} %collective-permute-done.10.refs_2_), channel_id=1, source_target_pairs={{0,1},{1,0},{2,3},{3,2},{4,5},{5,4},{6,7},{7,6},{8,9},{9,8},{10,11... | collective-permute-start | bytes 786440 | tf_op jit(solution)/shard_map/ppermute | solution.py:171

commit v3 on v2

--- a/solution.py
+++ b/solution.py
@@ -1,3 +1,5 @@
+import functools
+
 import jax
 import jax.numpy as jnp
 from jax import lax
@@ -6,8 +8,9 @@
 from jax.sharding import PartitionSpec as P
 
 CAP = 256
-RELAYED = 128
+RELAYED = 144
 TILE = 256
+BLOCK = 256
 BF16, F32 = jnp.bfloat16, jnp.float32
 VMEM = pl.BlockSpec(memory_space=pltpu.VMEM)
 SMEM = pl.BlockSpec(memory_space=pltpu.SMEM)
@@ -130,25 +133,31 @@
     out[...] = total.astype(BF16)
 
 
-def weight_gradient_here(own_hidden, far_hidden, near_hidden, own, far, near, out):
-    columns = half_of(pl.program_id(0), TILE)
-    rows = half_of(lax.axis_index("loc"), far_hidden.shape[0])
-    total = dot(own_hidden[rows, :], own[:CAP, columns])
-    total = total + dot(far_hidden[...], far[:, columns])
-    total = total + dot(near_hidden[...], near[:, columns])
-    out[...] = total.astype(BF16)
-
-
-def weight_gradient(own_hidden, far_hidden, near_hidden, own, far, near, here, out):
-    columns = half_of(pl.program_id(0), TILE)
-    core = lax.axis_index("loc")
-    half = far_hidden.shape[0]
-    rows = half_of(1 - core, half)
-    total = dot(own_hidden[rows, :], own[:CAP, columns])
-    total = total + dot(far_hidden[...], far[:, columns])
-    total = total + dot(near_hidden[...], near[:, columns])
-    out[0, rows, :] = total.astype(BF16)
-    out[0, half_of(core, half), :] = here[:, columns]
+def half_weights(side, own_hidden, far_hidden, near_hidden, own, far, near, *refs):
+    out, token = refs[-2:]
+    step = pl.program_id(0)
+    rows = half_of(step, BLOCK)
+    whole = half_of(side() * (far_hidden.shape[0] // BLOCK) + step, BLOCK)
+    for tile in tiles(far.shape[1]):
+        total = dot(own_hidden[whole, :], own[:CAP, tile])
+        total = total + dot(far_hidden[rows, :], far[:, tile])
+        out[0, :, tile] = (total + dot(near_hidden[rows, :], near[:, tile])).astype(BF16)
+    token[...] = jnp.zeros_like(token)
+
+
+def rows_of_half(side, *operands, units, features, before=()):
+    steps = units // 2 // BLOCK
+    return pl.pallas_call(
+        functools.partial(half_weights, side),
+        out_shape=[jax.ShapeDtypeStruct((1, units, features), BF16), jax.ShapeDtypeStruct((16, 128), BF16)],
+        grid=(steps,),
+        in_specs=[VMEM] * len(operands) + [ANY] * len(before),
+        out_specs=[pl.BlockSpec((1, BLOCK, features), lambda step: (0, side() * steps + step, 0)), VMEM],
+        input_output_aliases={len(operands): 0} if before else {},
+        cost_estimate=pl.CostEstimate(flops=10**10, bytes_accessed=10**3, transcendentals=0),
+        compiler_params=pltpu.CompilerParams(vmem_limit_bytes=16 << 20),
+        name="half_weights",
+    )(*operands, *before)
 
 
 def local(grad_out, hidden, weights, counts):
@@ -197,34 +206,30 @@
     (far_away,) = call(product_away, [partial], far_in, weights, after=(turned_in,))
     far_other = swap_cores(far_away)
     (far_here,) = call(product_here, [partial], far_in, weights, after=(far_away,))
-    (far_block,) = call(add_halves, [block], far_here, far_other)
-    far_back = send(far_block, back2)
     far_hidden, near_hidden, far_here = lax.optimization_barrier((far_hidden, near_hidden, far_here))
     far_hidden_in = send(far_hidden, by2)
     near_hidden_in = send(near_hidden, by1)
 
     near_in, near_away = call(
-        join_near, [((CAP, features), BF16), partial], turned_in, relayed_in, direct_in, weights, after=(far_block,)
+        join_near, [((CAP, features), BF16), partial], turned_in, relayed_in, direct_in, weights, after=(far_here,)
     )
     near_other = swap_cores(near_away)
     (near_here,) = call(product_here, [partial], near_in, weights, after=(near_away,))
     (near_block,) = call(add_halves, [block], near_here, near_other)
     near_back = send(near_block, back1)
-
-    far_hidden_in, near_hidden_in, near_block = lax.optimization_barrier((far_hidden_in, near_hidden_in, near_block))
-    strips = (features // TILE,)
-    (here,) = call(
-        weight_gradient_here, [((half, features), BF16)],
-        own_hidden, far_hidden_in, near_hidden_in, grad_out, far_in, near_in,
-        grid=strips, out_specs=[pl.BlockSpec((half, TILE), lambda tile: (0, tile))],
+    (far_block,) = call(add_halves, [block], far_here, far_other, after=(near_block,))
+    far_back = send(far_block, back2)
+
+    far_hidden_in, near_hidden_in, far_block = lax.optimization_barrier((far_hidden_in, near_hidden_in, far_block))
+    here, _ = rows_of_half(
+        lambda: lax.axis_index("loc"), own_hidden, far_hidden_in, near_hidden_in, grad_out, far_in, near_in, units=units, features=features
+    )
+    grad_weights, done = rows_of_half(
+        lambda: 1 - lax.axis_index("loc"), own_hidden, swap_cores(far_hidden_in), swap_cores(near_hidden_in), grad_out, far_in, near_in,
+        units=units, features=features, before=(here,),
     )
     (grad_hidden,) = call(
-        place_rows, [((rows, half), BF16)], places, own_block, near_back, far_back, after=(here,)
-    )
-    (grad_weights,) = call(
-        weight_gradient, [((1, units, features), BF16)],
-        own_hidden, swap_cores(far_hidden_in), swap_cores(near_hidden_in), grad_out, far_in, near_in, here,
-        grid=strips, out_specs=[pl.BlockSpec((1, units, TILE), lambda tile: (0, 0, tile))],
+        place_rows, [((rows, half), BF16)], places, own_block, near_back, far_back, after=(done,)
     )
     return grad_hidden, grad_weights
 

time: 63.5 us -> 59 us (0.929)
  the two profiles are of different devices: /device:TPU:25 before, /device:TPU:0 now
where the time goes in v3:
time: 59 us; the launch traced here: 58.7 us
  waiting for transfers between devices  26.2 us (44%)
  Pallas kernels  15.6 us (26%)
  starting transfers between devices  13.5 us (23%)
  local copies, waits for them, and re-layouts  2.62 us (4%)
  between operations  0.81 us (1%)
    ppermute x8, waiting for transfers between devices, send(): return lax.ppermute(value, 'grp', pairs)  25 us
    ppermute x8, starting transfers between devices, send(): return lax.ppermute(value, 'grp', pairs)  12.7 us
    pallas_call x14, Pallas kernels, call(): pl.pallas_call(body, out_shape=[jax.ShapeDtypeStruct(shape, dtype) for sh...  10.2 us
    pallas_call x2, Pallas kernels, rows_of_half(): pl.pallas_call(functools.partial(half_weights, side), out_shape=[jax.Shap...  5.45 us
    unnamed x10, local copies, waits for them, and re-layouts  2.62 us
    ppermute x5, waiting for transfers between devices, swap_cores(): return lax.ppermute(value, 'loc', [(0, 1), (1, 0)])  1.23 us
  transfers between devices with their start and end apart: 13, of which 7 were waited for; matrix products, arithmetic and copies ran while one was open for 0% of the time, Pallas kernels for 22%

profile of v3, /device:TPU:0, one launch (start us, length us, event | category | flops | bytes accessed | tf_op | source)
XLA Modules:
  0.0 58.7 jit_solution(16114400596591910614)
XLA Ops:
  0.6 0.0 copy-start.1
  0.6 1.5 %copy-done.1 = bf16[512,1792]{1,0:T(8,128)(2,1)S(1)} copy-done((bf16[512,1792]{1,0:T(8,128)(2,1)S(1)}, bf16[512,1792]{1,0:T(8,128)(2,1)}, u32[]{:S(2)}) %copy-start.1) | copy-done | bytes 1835032
  2.1 0.7 %copy-done.4 = s32[1,3]{1,0:T(1,128)S(1)} copy-done((s32[1,3]{1,0:T(1,128)S(1)}, s32[1,3]{1,0:T(1,128)}, u32[]{:S(2)}) %copy-start.4) | copy-done | bytes 36
  2.8 1.2 %pick_far.1.refs_2_ = bf16[256,1792]{1,0:T(8,128)(2,1)S(1)} custom-call(s32[1,3]{1,0:T(1,128)S(1)} %copy-done.4, bf16[512,1792]{1,0:T(8,128)(2,1)S(1)} %copy-done.1), custom_call_target="tpu_custom_call" | custom-call | flops 10000000000 | bytes 1000 | tf_op jit(solution)/shard_map/pick_far/pallas_call | solution.py:25
  4.0 0.0 copy-start
  4.0 0.0 copy-start.2
  4.0 3.1 %collective-permute-start.4 = (bf16[256,1792]{1,0:T(8,128)(2,1)S(1)}, bf16[256,1792]{1,0:T(8,128)(2,1)S(1)}, u32[]{:S(2)}, u32[]{:S(2)}) collective-permute-start(bf16[256,1792]{1,0:T(8,128)(2,1)S(1)} %pick_far.1.refs_2_), channel_id=1, source_target_pairs={{0,4},{2,6},{4,8},{6,10},{8,12},{10,14},{12,0},{14,2},{1,5},{3,7},... | collective-permute-start | bytes 2752520 | tf_op jit(solution)/shard_map/ppermute | solution.py:177
  7.1 1.0 %pick_turned.1.refs_2_ = bf16[144,1792]{1,0:T(8,128)(2,1)S(1)} custom-call(s32[1,3]{1,0:T(1,128)S(1)} %copy-done.4, bf16[512,1792]{1,0:T(8,128)(2,1)S(1)} %copy-done.1, bf16[256,1792]{1,0:T(8,128)(2,1)S(1)} %pick_far.1.refs_2_), custom_call_target="tpu_custom_call" | custom-call | flops 10000000000 | bytes 1000 | tf_op jit(solution)/shard_map/pick_turned/pallas_call | solution.py:25
  8.1 1.6 %collective-permute-start = (bf16[144,1792]{1,0:T(8,128)(2,1)S(1)}, bf16[144,1792]{1,0:T(8,128)(2,1)S(1)}, u32[]{:S(2)}, u32[]{:S(2)}) collective-permute-start(bf16[144,1792]{1,0:T(8,128)(2,1)S(1)} %pick_turned.1.refs_2_), channel_id=1, source_target_pairs={{0,2},{2,0},{4,6},{6,4},{8,10},{10,8},{12,14},{14,12},{1,3},{3,1},... | collective-permute-start | bytes 1548296 | tf_op jit(solution)/shard_map/ppermute | solution.py:177
  9.7 0.7 %product_away.2.refs_2_ = f32[256,512]{1,0:T(8,128)S(1)} custom-call(bf16[512,1792]{1,0:T(8,128)(2,1)S(1)} %copy-done.2, bf16[1,1024,1792]{2,1,0:T(8,128)(2,1)S(1)} %copy-done, bf16[144,1792]{1,0:T(8,128)(2,1)S(1)} %pick_turned.1.refs_2_), custom_call_target="tpu_custom_call" | custom-call | flops 10000000000 | bytes 1000 | tf_op jit(solution)/shard_map/product_away/pallas_call | solution.py:25
  10.3 0.0 copy-start.3
  10.3 0.1 collective-permute-start.1
  10.4 0.7 %product_here.3.refs_2_.refs_0_ = f32[256,512]{1,0:T(8,128)S(1)} custom-call(bf16[512,1792]{1,0:T(8,128)(2,1)S(1)} %copy-done.2, bf16[1,1024,1792]{2,1,0:T(8,128)(2,1)S(1)} %copy-done, f32[256,512]{1,0:T(8,128)S(1)} %product_away.2.refs_2_), custom_call_target="tpu_custom_call" | custom-call | flops 10000000000 | bytes 1000 | tf_op jit(solution)/shard_map/product_here/pallas_call | solution.py:25
  11.1 0.5 copy-done.3
  11.6 1.4 %pick_hidden.1 = (bf16[512,256]{1,0:T(8,128)(2,1)S(1)}, bf16[512,256]{1,0:T(8,128)(2,1)S(1)}, bf16[1024,256]{1,0:T(8,128)(2,1)S(1)}, bf16[512,768]{1,0:T(8,128)(2,1)S(1)}) custom-call(s32[1,3]{1,0:T(1,128)S(1)} %copy-done.4, bf16[512,1024]{1,0:T(8,128)(2,1)S(1)} %copy-done.3, f32[256,512]{1,0:T(8,128)S(1)} %product_here.3.refs_2_.refs_0_), custom_call_target="tpu_custom_call" | custom-call | flops 10000000000 | bytes 1000 | tf_op jit(solution)/shard_map/pick_hidden/pallas_call | solution.py:25
  13.0 1.0 %pick_direct.1.refs_2_ = bf16[112,1792]{1,0:T(8,128)(2,1)S(1)} custom-call(s32[1,3]{1,0:T(1,128)S(1)} %copy-done.4, bf16[512,1792]{1,0:T(8,128)(2,1)S(1)} %copy-done.2, bf16[512,768]{1,0:T(8,128)(2,1)S(1)} %get-tuple-element.18.refs_2_.refs_0_), custom_call_target="tpu_custom_call" | custom-call | flops 10000000000 | bytes 1000 | tf_op jit(solution)/shard_map/pick_direct/pallas_call | solution.py:25
  14.0 0.6 collective-permute-start.3
  14.5 0.0 collective-permute-done.1.refs_1_
  14.5 0.1 add_halves.3.refs_1_
  14.6 7.2 %collective-permute-done.refs_2_.refs_0_ = bf16[144,1792]{1,0:T(8,128)(2,1)S(1)} collective-permute-done((bf16[144,1792]{1,0:T(8,128)(2,1)S(1)}, bf16[144,1792]{1,0:T(8,128)(2,1)S(1)}, u32[]{:S(2)}, u32[]{:S(2)}) %collective-permute-start) | collective-permute-done | bytes 516128 | tf_op jit(solution)/shard_map/ppermute | solution.py:177
  21.8 3.5 %collective-permute-start.2 = (bf16[144,1792]{1,0:T(8,128)(2,1)S(1)}, bf16[144,1792]{1,0:T(8,128)(2,1)S(1)}, u32[]{:S(2)}, u32[]{:S(2)}) collective-permute-start(bf16[144,1792]{1,0:T(8,128)(2,1)S(1)} %collective-permute-done.refs_2_.refs_0_), channel_id=1, source_target_pairs={{0,4},{4,8},{8,12},{12,0},{1,5},{5,9},{9,13},{13,1},{16,20},{20,24... | collective-permute-start | bytes 1548296 | tf_op jit(solution)/shard_map/ppermute | solution.py:177
  25.3 5.0 %collective-permute-done.4.refs_0_.far = bf16[256,1792]{1,0:T(8,128)(2,1)S(1)} collective-permute-done((bf16[256,1792]{1,0:T(8,128)(2,1)S(1)}, bf16[256,1792]{1,0:T(8,128)(2,1)S(1)}, u32[]{:S(2)}, u32[]{:S(2)}) %collective-permute-start.4) | collective-permute-done | bytes 917536 | tf_op jit(solution)/shard_map/ppermute | solution.py:177
  30.3 0.7 %product_away.3.refs_2_ = f32[256,512]{1,0:T(8,128)S(1)} custom-call(bf16[256,1792]{1,0:T(8,128)(2,1)S(1)} %collective-permute-done.4.refs_0_.far, bf16[1,1024,1792]{2,1,0:T(8,128)(2,1)S(1)} %copy-done, bf16[144,1792]{1,0:T(8,128)(2,1)S(1)} %collective-permute-done.refs_2_.refs_0_), custom_call_target="tpu_custom_call" | custom-call | flops 10000000000 | bytes 1000 | tf_op jit(solution)/shard_map/product_away/pallas_call | solution.py:25
  31.0 0.1 collective-permute-start.7
  31.0 0.7 %product_here.4.refs_4_.refs_0_ = f32[256,512]{1,0:T(8,128)S(1)} custom-call(bf16[256,1792]{1,0:T(8,128)(2,1)S(1)} %collective-permute-done.4.refs_0_.far, bf16[1,1024,1792]{2,1,0:T(8,128)(2,1)S(1)} %copy-done, f32[256,512]{1,0:T(8,128)S(1)} %product_away.3.refs_2_), custom_call_target="tpu_custom_call" | custom-call | flops 10000000000 | bytes 1000 | tf_op jit(solution)/shard_map/product_here/pallas_call | solution.py:25
  31.7 0.1 collective-permute-start.9
  31.8 1.8 %collective-permute-start.10 = (bf16[512,256]{1,0:T(8,128)(2,1)S(1)}, bf16[512,256]{1,0:T(8,128)(2,1)S(1)}, u32[]{:S(2)}, u32[]{:S(2)}) collective-permute-start(bf16[512,256]{1,0:T(8,128)(2,1)S(1)} %get-tuple-element.28), channel_id=1, source_target_pairs={{0,2},{2,4},{4,6},{6,8},{8,10},{10,12},{12,14},{14,0},{1,3},{3,5},... | collective-permute-start | bytes 786440 | tf_op jit(solution)/shard_map/ppermute | solution.py:177
  33.6 6.5 %collective-permute-done.3.refs_2_ = bf16[112,1792]{1,0:T(8,128)(2,1)S(1)} collective-permute-done((bf16[112,1792]{1,0:T(8,128)(2,1)S(1)}, bf16[112,1792]{1,0:T(8,128)(2,1)S(1)}, u32[]{:S(2)}, u32[]{:S(2)}) %collective-permute-start.3) | collective-permute-done | bytes 401440 | tf_op jit(solution)/shard_map/ppermute | solution.py:177
  40.1 1.3 %collective-permute-done.2.refs_1_ = bf16[144,1792]{1,0:T(8,128)(2,1)S(1)} collective-permute-done((bf16[144,1792]{1,0:T(8,128)(2,1)S(1)}, bf16[144,1792]{1,0:T(8,128)(2,1)S(1)}, u32[]{:S(2)}, u32[]{:S(2)}) %collective-permute-start.2) | collective-permute-done | bytes 516128 | tf_op jit(solution)/shard_map/ppermute | solution.py:177
  41.3 0.7 %join_near.1 = (bf16[256,1792]{1,0:T(8,128)(2,1)S(1)}, f32[256,512]{1,0:T(8,128)S(1)}) custom-call(bf16[144,1792]{1,0:T(8,128)(2,1)S(1)} %collective-permute-done.refs_2_.refs_0_, bf16[144,1792]{1,0:T(8,128)(2,1)S(1)} %collective-permute-done.2.refs_1_, bf16[112,1792]{1,0:T(8,128)(2,1)S(1)} %collective-permute-done.3.refs_2_, ...), custom_call_target="tpu_custom_call" | custom-call | flops 10000000000 | bytes 1000 | tf_op jit(solution)/shard_map/join_near/pallas_call | solution.py:25
  42.1 0.1 collective-permute-start.5
  42.1 0.7 %product_here.5.refs_0_ = f32[256,512]{1,0:T(8,128)S(1)} custom-call(bf16[256,1792]{1,0:T(8,128)(2,1)S(1)} %get-tuple-element.24.refs_0_.near, bf16[1,1024,1792]{2,1,0:T(8,128)(2,1)S(1)} %copy-done, f32[256,512]{1,0:T(8,128)S(1)} %get-tuple-element.25.refs_2_), custom_call_target="tpu_custom_call" | custom-call | flops 10000000000 | bytes 1000 | tf_op jit(solution)/shard_map/product_here/pallas_call | solution.py:25
  42.8 1.2 %collective-permute-done.5.refs_1_ = f32[256,512]{1,0:T(8,128)S(1)} collective-permute-done((f32[256,512]{1,0:T(8,128)S(1)}, f32[256,512]{1,0:T(8,128)S(1)}, u32[]{:S(2)}, u32[]{:S(2)}) %collective-permute-start.5) | collective-permute-done | bytes 524320 | tf_op jit(solution)/shard_map/ppermute | solution.py:180
  44.1 0.1 collective-permute-start.6
  44.2 0.0 collective-permute-done.7.refs_1_
  44.2 0.1 add_halves.5
  44.3 2.1 %collective-permute-start.8 = (bf16[256,512]{1,0:T(8,128)(2,1)S(1)}, bf16[256,512]{1,0:T(8,128)(2,1)S(1)}, u32[]{:S(2)}, u32[]{:S(2)}) collective-permute-start(bf16[256,512]{1,0:T(8,128)(2,1)S(1)} %add_halves.5), channel_id=1, source_target_pairs={{4,0},{6,2},{8,4},{10,6},{12,8},{14,10},{0,12},{2,14},{5,1},{7,3},... | collective-permute-start | bytes 786440 | tf_op jit(solution)/shard_map/ppermute | solution.py:177
  46.4 0.0 collective-permute-done.9.far_hidden
  46.4 5.0 %collective-permute-done.10.near_hidden = bf16[512,256]{1,0:T(8,128)(2,1)S(1)} collective-permute-done((bf16[512,256]{1,0:T(8,128)(2,1)S(1)}, bf16[512,256]{1,0:T(8,128)(2,1)S(1)}, u32[]{:S(2)}, u32[]{:S(2)}) %collective-permute-start.10) | collective-permute-done | bytes 262176 | tf_op jit(solution)/shard_map/ppermute | solution.py:177
  51.3 0.0 collective-permute-start.11
  51.3 0.5 collective-permute-start.12
  51.8 2.7 %half_weights.2 = (bf16[1,1024,1792]{2,1,0:T(8,128)(2,1)}, bf16[16,128]{1,0:T(8,128)(2,1)}) custom-call(bf16[1024,256]{1,0:T(8,128)(2,1)S(1)} %get-tuple-element.26.own_hidden, bf16[512,256]{1,0:T(8,128)(2,1)S(1)} %collective-permute-done.9.far_hidden, bf16[512,256]{1,0:T(8,128)(2,1)S(1)} %collective-permute-done.10.near_hidden, ...), custom_call_target="tpu_custom_call" | custom-call | flops 10000000000 | bytes 1000 | tf_op jit(solution)/shard_map/half_weights/pallas_call | solution.py:150
  54.6 0.0 collective-permute-done.11.far_hidden
  54.6 0.0 collective-permute-done.12.near_hidden
  54.6 2.7 %half_weights.3 = (bf16[1,1024,1792]{2,1,0:T(8,128)(2,1)}, bf16[16,128]{1,0:T(8,128)(2,1)S(1)}) custom-call(bf16[1024,256]{1,0:T(8,128)(2,1)S(1)} %get-tuple-element.26.own_hidden, bf16[512,256]{1,0:T(8,128)(2,1)S(1)} %collective-permute-done.11.far_hidden, ...), custom_call_target="tpu_custom_call", output_to_operand_aliasing={{0}: (6, {})} | custom-call | flops 10000000000 | bytes 1000 | tf_op jit(solution)/shard_map/half_weights/pallas_call | solution.py:150
  57.3 0.0 collective-permute-done.6.refs_2_
  57.3 0.1 collective-permute-done.8.refs_3_
  57.4 1.4 %place_rows.1 = bf16[512,512]{1,0:T(8,128)(2,1)} custom-call(bf16[512,768]{1,0:T(8,128)(2,1)S(1)} %get-tuple-element.18.refs_2_.refs_0_, bf16[256,512]{1,0:T(8,128)(2,1)S(1)} %add_halves.3.refs_1_, bf16[256,512]{1,0:T(8,128)(2,1)S(1)} %collective-permute-done.6.refs_2_, bf16[256,512]{1,0:T(8,128)(2,1)S(1)} %collective-permute-done.8.refs_3_, ...), custom_call_target="tpu_custom_call" | custom-call | flops 10000000000 | bytes 1000 | tf_op jit(solution)/shard_map/place_rows/pallas_call | solution.py:25
  (4 shorter events, 0.1 us)
Async XLA Ops:
  0.6 1.5 %copy-start.1 = (bf16[512,1792]{1,0:T(8,128)(2,1)S(1)}, bf16[512,1792]{1,0:T(8,128)(2,1)}, u32[]{:S(2)}) copy-start(bf16[512,1792]{1,0:T(8,128)(2,1)} %own.3) | copy-start | bytes 5505028
  2.1 0.7 %copy-start.4 = (s32[1,3]{1,0:T(1,128)S(1)}, s32[1,3]{1,0:T(1,128)}, u32[]{:S(2)}) copy-start(s32[1,3]{1,0:T(1,128)} %refs_0_.11) | copy-start | bytes 40
  4.0 5.7 %copy-start = (bf16[1,1024,1792]{2,1,0:T(8,128)(2,1)S(1)}, bf16[1,1024,1792]{2,1,0:T(8,128)(2,1)}, u32[]{:S(2)}) copy-start(bf16[1,1024,1792]{2,1,0:T(8,128)(2,1)} %refs_1_.17) | copy-start | bytes 11010052
  4.0 5.7 %copy-start.2 = (bf16[512,1792]{1,0:T(8,128)(2,1)S(1)}, bf16[512,1792]{1,0:T(8,128)(2,1)}, u32[]{:S(2)}) copy-start(bf16[512,1792]{1,0:T(8,128)(2,1)} %own.3) | copy-start | bytes 5505028
  4.0 26.3 %collective-permute-start.4 = (bf16[256,1792]{1,0:T(8,128)(2,1)S(1)}, bf16[256,1792]{1,0:T(8,128)(2,1)S(1)}, u32[]{:S(2)}, u32[]{:S(2)}) collective-permute-start(bf16[256,1792]{1,0:T(8,128)(2,1)S(1)} %pick_far.1.refs_2_), channel_id=1, source_target_pairs={{0,4},{2,6},{4,8},{6,10},{8,12},{10,14},{12,0},{14,2},{1,5},{3,7},... | collective-permute-start | bytes 2752520 | tf_op jit(solution)/shard_map/ppermute | solution.py:177
  8.1 13.8 %collective-permute-start = (bf16[144,1792]{1,0:T(8,128)(2,1)S(1)}, bf16[144,1792]{1,0:T(8,128)(2,1)S(1)}, u32[]{:S(2)}, u32[]{:S(2)}) collective-permute-start(bf16[144,1792]{1,0:T(8,128)(2,1)S(1)} %pick_turned.1.refs_2_), channel_id=1, source_target_pairs={{0,2},{2,0},{4,6},{6,4},{8,10},{10,8},{12,14},{14,12},{1,3},{3,1},... | collective-permute-start | bytes 1548296 | tf_op jit(solution)/shard_map/ppermute | solution.py:177
  10.3 1.2 %copy-start.3 = (bf16[512,1024]{1,0:T(8,128)(2,1)S(1)}, bf16[512,1024]{1,0:T(8,128)(2,1)}, u32[]{:S(2)}) copy-start(bf16[512,1024]{1,0:T(8,128)(2,1)} %refs_1_.13) | copy-start | bytes 3145732
  10.3 4.2 %collective-permute-start.1 = (f32[256,512]{1,0:T(8,128)S(1)}, f32[256,512]{1,0:T(8,128)S(1)}, u32[]{:S(2)}, u32[]{:S(2)}) collective-permute-start(f32[256,512]{1,0:T(8,128)S(1)} %product_away.2.refs_2_), channel_id=1, source_target_pairs={{0,1},{1,0},{2,3},{3,2},{4,5},{5,4},{6,7},{7,6},{8,9},{9,8},{10,11... | collective-permute-start | bytes 1572872 | tf_op jit(solution)/shard_map/ppermute | solution.py:180
  14.0 26.1 %collective-permute-start.3 = (bf16[112,1792]{1,0:T(8,128)(2,1)S(1)}, bf16[112,1792]{1,0:T(8,128)(2,1)S(1)}, u32[]{:S(2)}, u32[]{:S(2)}) collective-permute-start(bf16[112,1792]{1,0:T(8,128)(2,1)S(1)} %pick_direct.1.refs_2_), channel_id=1, source_target_pairs={{0,2},{2,4},{4,6},{6,8},{8,10},{10,12},{12,14},{14,0},{1,3},{3,5},... | collective-permute-start | bytes 1204232 | tf_op jit(solution)/shard_map/ppermute | solution.py:177
  21.8 19.5 %collective-permute-start.2 = (bf16[144,1792]{1,0:T(8,128)(2,1)S(1)}, bf16[144,1792]{1,0:T(8,128)(2,1)S(1)}, u32[]{:S(2)}, u32[]{:S(2)}) collective-permute-start(bf16[144,1792]{1,0:T(8,128)(2,1)S(1)} %collective-permute-done.refs_2_.refs_0_), channel_id=1, source_target_pairs={{0,4},{4,8},{8,12},{12,0},{1,5},{5,9},{9,13},{13,1},{16,20},{20,24... | collective-permute-start | bytes 1548296 | tf_op jit(solution)/shard_map/ppermute | solution.py:177
  31.0 13.2 %collective-permute-start.7 = (f32[256,512]{1,0:T(8,128)S(1)}, f32[256,512]{1,0:T(8,128)S(1)}, u32[]{:S(2)}, u32[]{:S(2)}) collective-permute-start(f32[256,512]{1,0:T(8,128)S(1)} %product_away.3.refs_2_), channel_id=1, source_target_pairs={{0,1},{1,0},{2,3},{3,2},{4,5},{5,4},{6,7},{7,6},{8,9},{9,8},{10,11... | collective-permute-start | bytes 1572872 | tf_op jit(solution)/shard_map/ppermute | solution.py:180
  31.7 14.6 %collective-permute-start.9 = (bf16[512,256]{1,0:T(8,128)(2,1)S(1)}, bf16[512,256]{1,0:T(8,128)(2,1)S(1)}, u32[]{:S(2)}, u32[]{:S(2)}) collective-permute-start(bf16[512,256]{1,0:T(8,128)(2,1)S(1)} %get-tuple-element.27), channel_id=1, source_target_pairs={{0,4},{2,6},{4,8},{6,10},{8,12},{10,14},{12,0},{14,2},{1,5},{3,7},... | collective-permute-start | bytes 786440 | tf_op jit(solution)/shard_map/ppermute | solution.py:177
  31.8 19.5 %collective-permute-start.10 = (bf16[512,256]{1,0:T(8,128)(2,1)S(1)}, bf16[512,256]{1,0:T(8,128)(2,1)S(1)}, u32[]{:S(2)}, u32[]{:S(2)}) collective-permute-start(bf16[512,256]{1,0:T(8,128)(2,1)S(1)} %get-tuple-element.28), channel_id=1, source_target_pairs={{0,2},{2,4},{4,6},{6,8},{8,10},{10,12},{12,14},{14,0},{1,3},{3,5},... | collective-permute-start | bytes 786440 | tf_op jit(solution)/shard_map/ppermute | solution.py:177
  42.1 2.0 %collective-permute-start.5 = (f32[256,512]{1,0:T(8,128)S(1)}, f32[256,512]{1,0:T(8,128)S(1)}, u32[]{:S(2)}, u32[]{:S(2)}) collective-permute-start(f32[256,512]{1,0:T(8,128)S(1)} %get-tuple-element.25.refs_2_), channel_id=1, source_target_pairs={{0,1},{1,0},{2,3},{3,2},{4,5},{5,4},{6,7},{7,6},{8,9},{9,8},{10,11... | collective-permute-start | bytes 1572872 | tf_op jit(solution)/shard_map/ppermute | solution.py:180
  44.1 13.2 %collective-permute-start.6 = (bf16[256,512]{1,0:T(8,128)(2,1)S(1)}, bf16[256,512]{1,0:T(8,128)(2,1)S(1)}, u32[]{:S(2)}, u32[]{:S(2)}) collective-permute-start(bf16[256,512]{1,0:T(8,128)(2,1)S(1)} %add_halves.4.refs_2_), channel_id=1, source_target_pairs={{2,0},{4,2},{6,4},{8,6},{10,8},{12,10},{14,12},{0,14},{3,1},{5,3},... | collective-permute-start | bytes 786440 | tf_op jit(solution)/shard_map/ppermute | solution.py:177
  44.3 13.1 %collective-permute-start.8 = (bf16[256,512]{1,0:T(8,128)(2,1)S(1)}, bf16[256,512]{1,0:T(8,128)(2,1)S(1)}, u32[]{:S(2)}, u32[]{:S(2)}) collective-permute-start(bf16[256,512]{1,0:T(8,128)(2,1)S(1)} %add_halves.5), channel_id=1, source_target_pairs={{4,0},{6,2},{8,4},{10,6},{12,8},{14,10},{0,12},{2,14},{5,1},{7,3},... | collective-permute-start | bytes 786440 | tf_op jit(solution)/shard_map/ppermute | solution.py:177
  51.3 3.2 %collective-permute-start.11 = (bf16[512,256]{1,0:T(8,128)(2,1)S(1)}, bf16[512,256]{1,0:T(8,128)(2,1)S(1)}, u32[]{:S(2)}, u32[]{:S(2)}) collective-permute-start(bf16[512,256]{1,0:T(8,128)(2,1)S(1)} %collective-permute-done.9.far_hidden), channel_id=1, source_target_pairs={{0,1},{1,0},{2,3},{3,2},{4,5},{5,4},{6,7},{7,6},{8,9},{9,8},{10,11... | collective-permute-start | bytes 786440 | tf_op jit(solution)/shard_map/ppermute | solution.py:180
  51.3 3.2 %collective-permute-start.12 = (bf16[512,256]{1,0:T(8,128)(2,1)S(1)}, bf16[512,256]{1,0:T(8,128)(2,1)S(1)}, u32[]{:S(2)}, u32[]{:S(2)}) collective-permute-start(bf16[512,256]{1,0:T(8,128)(2,1)S(1)} %collective-permute-done.10.near_hidden), channel_id=1, source_target_pairs={{0,1},{1,0},{2,3},{3,2},{4,5},{5,4},{6,7},{7,6},{8,9},{9,8},{10,11... | collective-permute-start | bytes 786440 | tf_op jit(solution)/shard_map/ppermute | solution.py:180

commit v4 on v3

--- a/solution.py
+++ b/solution.py
@@ -9,6 +9,7 @@
 
 CAP = 256
 RELAYED = 144
+LAST = 2
 TILE = 256
 BLOCK = 256
 BF16, F32 = jnp.bfloat16, jnp.float32
@@ -49,28 +50,27 @@
     return first, counts[0, index]
 
 
+def picked(counts, index, place, row, rows):
+    first, count = segment(counts, index)
+    if index == LAST:
+        return (row == rows - CAP + place) & (place >= CAP - count)
+    return (row == first + place) & (place < count)
+
+
 def picker(counts, index, rows):
-    first, count = segment(counts, index)
     place = lax.broadcasted_iota(jnp.int32, (CAP, rows), 0)
     row = lax.broadcasted_iota(jnp.int32, (CAP, rows), 1)
-    return ((row == first + place) & (place < count)).astype(BF16)
+    return picked(counts, index, place, row, rows).astype(BF16)
 
 
 def placer(counts, index, rows):
-    first, count = segment(counts, index)
     row = lax.broadcasted_iota(jnp.int32, (rows, CAP), 0)
     place = lax.broadcasted_iota(jnp.int32, (rows, CAP), 1)
-    return ((row == first + place) & (place < count)).astype(BF16)
+    return picked(counts, index, place, row, rows).astype(BF16)
 
 
 def tiles(extent):
     return [slice(at, min(at + TILE, extent)) for at in range(0, extent, TILE)]
-
-
-def pick_far(counts, grad_out, far):
-    pick = picker(counts, 2, grad_out.shape[0])
-    for tile in tiles(grad_out.shape[1]):
-        far[:, tile] = dot(pick, grad_out[:, tile]).astype(BF16)
 
 
 def pick_turned(counts, grad_out, turned):
@@ -181,7 +181,7 @@
 
     partial = ((CAP, half), F32)
     block = ((CAP, half), BF16)
-    (far,) = call(pick_far, [((CAP, features), BF16)], counts, grad_out, scalars=1)
+    far = grad_out[rows - CAP :]
     far_in = send(far, by2)
     (turned,) = call(pick_turned, [((RELAYED, features), BF16)], counts, grad_out, scalars=1, after=(far,))
     turned_in = send(turned, turn)
@@ -207,8 +207,8 @@
     far_other = swap_cores(far_away)
     (far_here,) = call(product_here, [partial], far_in, weights, after=(far_away,))
     far_hidden, near_hidden, far_here = lax.optimization_barrier((far_hidden, near_hidden, far_here))
+    near_hidden_in = send(near_hidden, by1)
     far_hidden_in = send(far_hidden, by2)
-    near_hidden_in = send(near_hidden, by1)
 
     near_in, near_away = call(
         join_near, [((CAP, features), BF16), partial], turned_in, relayed_in, direct_in, weights, after=(far_here,)
@@ -220,7 +220,7 @@
     (far_block,) = call(add_halves, [block], far_here, far_other, after=(near_block,))
     far_back = send(far_block, back2)
 
-    far_hidden_in, near_hidden_in, far_block = lax.optimization_barrier((far_hidden_in, near_hidden_in, far_block))
+    near_hidden_in, far_hidden_in, far_block = lax.optimization_barrier((near_hidden_in, far_hidden_in, far_block))
     here, _ = rows_of_half(
         lambda: lax.axis_index("loc"), own_hidden, far_hidden_in, near_hidden_in, grad_out, far_in, near_in, units=units, features=features
     )

time: 59 us -> 56.9 us (0.964)
  waiting for transfers between devices: 26.2 us -> 24.1 us
  local copies, waits for them, and re-layouts: 2.62 us -> 3.88 us
  Pallas kernels: 15.6 us -> 14.4 us
    ppermute x8, waiting for transfers between devices: 25 us -> 22.9 us  [send(): return lax.ppermute(value, 'grp', pairs)]
    slice x0 -> x1, local copies, waits for them, and re-layouts: none -> 1.24 us  [local(): far = grad_out[rows - CAP:]]
    pallas_call x14 -> x13, Pallas kernels: 10.2 us -> 9 us  [call(): pl.pallas_call(body, out_shape=[jax.ShapeDtypeStruct(shape, dtype) for sh...]
  transfers between devices with their start and end apart: 13 -> 13, of which waited for: 7 -> 7; matrix products, arithmetic and copies ran while one was open for 0% -> 0% of each run, Pallas kernels for 22% -> 23%
where the time goes in v4:
time: 56.9 us; the launch traced here: 56.6 us
  waiting for transfers between devices  24.1 us (42%)
  Pallas kernels  14.4 us (25%)
  starting transfers between devices  13.4 us (24%)
  local copies, waits for them, and re-layouts  3.88 us (7%)
  between operations  0.78 us (1%)
    ppermute x8, waiting for transfers between devices, send(): return lax.ppermute(value, 'grp', pairs)  22.9 us
    ppermute x8, starting transfers between devices, send(): return lax.ppermute(value, 'grp', pairs)  12.7 us
    pallas_call x13, Pallas kernels, call(): pl.pallas_call(body, out_shape=[jax.ShapeDtypeStruct(shape, dtype) for sh...  9 us
    pallas_call x2, Pallas kernels, rows_of_half(): pl.pallas_call(functools.partial(half_weights, side), out_shape=[jax.Shap...  5.45 us
    unnamed x10, local copies, waits for them, and re-layouts  2.63 us
    slice x1, local copies, waits for them, and re-layouts, local(): far = grad_out[rows - CAP:]  1.24 us
    ppermute x5, waiting for transfers between devices, swap_cores(): return lax.ppermute(value, 'loc', [(0, 1), (1, 0)])  1.22 us
  transfers between devices with their start and end apart: 13, of which 7 were waited for; matrix products, arithmetic and copies ran while one was open for 0% of the time, Pallas kernels for 23%

profile of v4, /device:TPU:0, one launch (start us, length us, event | category | flops | bytes accessed | tf_op | source)
XLA Modules:
  0.0 56.6 jit_solution(12650202003580192055)
XLA Ops:
  0.6 1.2 %slice.3.refs_2_ = bf16[256,1792]{1,0:T(8,128)(2,1)S(1)} slice(bf16[512,1792]{1,0:T(8,128)(2,1)} %own.3), slice={[256:512], [0:1792]} | slice | bytes 1835008 | tf_op jit(solution)/shard_map/slice | solution.py:184
  1.9 3.1 %collective-permute-start.4 = (bf16[256,1792]{1,0:T(8,128)(2,1)S(1)}, bf16[256,1792]{1,0:T(8,128)(2,1)S(1)}, u32[]{:S(2)}, u32[]{:S(2)}) collective-permute-start(bf16[256,1792]{1,0:T(8,128)(2,1)S(1)} %slice.3.refs_2_), channel_id=1, source_target_pairs={{0,4},{2,6},{4,8},{6,10},{8,12},{10,14},{12,0},{14,2},{1,5},{3,7},... | collective-permute-start | bytes 2752520 | tf_op jit(solution)/shard_map/ppermute | solution.py:177
  5.0 0.0 copy-start
  5.0 1.5 %copy-done = bf16[512,1792]{1,0:T(8,128)(2,1)S(1)} copy-done((bf16[512,1792]{1,0:T(8,128)(2,1)S(1)}, bf16[512,1792]{1,0:T(8,128)(2,1)}, u32[]{:S(2)}) %copy-start) | copy-done | bytes 1835032
  6.5 0.7 %copy-done.4 = s32[1,3]{1,0:T(1,128)S(1)} copy-done((s32[1,3]{1,0:T(1,128)S(1)}, s32[1,3]{1,0:T(1,128)}, u32[]{:S(2)}) %copy-start.4) | copy-done | bytes 36
  7.1 1.0 %pick_turned.1.refs_2_ = bf16[144,1792]{1,0:T(8,128)(2,1)S(1)} custom-call(s32[1,3]{1,0:T(1,128)S(1)} %copy-done.4, bf16[512,1792]{1,0:T(8,128)(2,1)S(1)} %copy-done, bf16[256,1792]{1,0:T(8,128)(2,1)S(1)} %slice.3.refs_2_), custom_call_target="tpu_custom_call" | custom-call | flops 10000000000 | bytes 1000 | tf_op jit(solution)/shard_map/pick_turned/pallas_call | solution.py:26
  8.1 1.6 %collective-permute-start = (bf16[144,1792]{1,0:T(8,128)(2,1)S(1)}, bf16[144,1792]{1,0:T(8,128)(2,1)S(1)}, u32[]{:S(2)}, u32[]{:S(2)}) collective-permute-start(bf16[144,1792]{1,0:T(8,128)(2,1)S(1)} %pick_turned.1.refs_2_), channel_id=1, source_target_pairs={{0,2},{2,0},{4,6},{6,4},{8,10},{10,8},{12,14},{14,12},{1,3},{3,1},... | collective-permute-start | bytes 1548296 | tf_op jit(solution)/shard_map/ppermute | solution.py:177
  9.7 0.0 copy-done.1
  9.7 0.0 copy-done.2
  9.7 0.7 %product_away.2.refs_2_ = f32[256,512]{1,0:T(8,128)S(1)} custom-call(bf16[512,1792]{1,0:T(8,128)(2,1)S(1)} %copy-done.1, bf16[1,1024,1792]{2,1,0:T(8,128)(2,1)S(1)} %copy-done.2, bf16[144,1792]{1,0:T(8,128)(2,1)S(1)} %pick_turned.1.refs_2_), custom_call_target="tpu_custom_call" | custom-call | flops 10000000000 | bytes 1000 | tf_op jit(solution)/shard_map/product_away/pallas_call | solution.py:26
  10.4 0.0 copy-start.3
  10.4 0.1 collective-permute-start.1
  10.5 0.7 %product_here.3.refs_2_.refs_0_ = f32[256,512]{1,0:T(8,128)S(1)} custom-call(bf16[512,1792]{1,0:T(8,128)(2,1)S(1)} %copy-done.1, bf16[1,1024,1792]{2,1,0:T(8,128)(2,1)S(1)} %copy-done.2, f32[256,512]{1,0:T(8,128)S(1)} %product_away.2.refs_2_), custom_call_target="tpu_custom_call" | custom-call | flops 10000000000 | bytes 1000 | tf_op jit(solution)/shard_map/product_here/pallas_call | solution.py:26
  11.1 0.5 copy-done.3
  11.6 1.4 %pick_hidden.1 = (bf16[512,256]{1,0:T(8,128)(2,1)S(1)}, bf16[512,256]{1,0:T(8,128)(2,1)S(1)}, bf16[1024,256]{1,0:T(8,128)(2,1)S(1)}, bf16[512,768]{1,0:T(8,128)(2,1)S(1)}) custom-call(s32[1,3]{1,0:T(1,128)S(1)} %copy-done.4, bf16[512,1024]{1,0:T(8,128)(2,1)S(1)} %copy-done.3, f32[256,512]{1,0:T(8,128)S(1)} %product_here.3.refs_2_.refs_0_), custom_call_target="tpu_custom_call" | custom-call | flops 10000000000 | bytes 1000 | tf_op jit(solution)/shard_map/pick_hidden/pallas_call | solution.py:26
  13.0 1.0 %pick_direct.1.refs_2_ = bf16[112,1792]{1,0:T(8,128)(2,1)S(1)} custom-call(s32[1,3]{1,0:T(1,128)S(1)} %copy-done.4, bf16[512,1792]{1,0:T(8,128)(2,1)S(1)} %copy-done.1, bf16[512,768]{1,0:T(8,128)(2,1)S(1)} %get-tuple-element.18.refs_2_.refs_0_), custom_call_target="tpu_custom_call" | custom-call | flops 10000000000 | bytes 1000 | tf_op jit(solution)/shard_map/pick_direct/pallas_call | solution.py:26
  14.0 1.6 %collective-permute-start.3 = (bf16[112,1792]{1,0:T(8,128)(2,1)S(1)}, bf16[112,1792]{1,0:T(8,128)(2,1)S(1)}, u32[]{:S(2)}, u32[]{:S(2)}) collective-permute-start(bf16[112,1792]{1,0:T(8,128)(2,1)S(1)} %pick_direct.1.refs_2_), channel_id=1, source_target_pairs={{0,2},{2,4},{4,6},{6,8},{8,10},{10,12},{12,14},{14,0},{1,3},{3,5},... | collective-permute-start | bytes 1204232 | tf_op jit(solution)/shard_map/ppermute | solution.py:177
  15.6 0.0 collective-permute-done.1.refs_1_
  15.6 0.1 add_halves.3.refs_1_
  15.6 6.2 %collective-permute-done.refs_2_.refs_0_ = bf16[144,1792]{1,0:T(8,128)(2,1)S(1)} collective-permute-done((bf16[144,1792]{1,0:T(8,128)(2,1)S(1)}, bf16[144,1792]{1,0:T(8,128)(2,1)S(1)}, u32[]{:S(2)}, u32[]{:S(2)}) %collective-permute-start) | collective-permute-done | bytes 516128 | tf_op jit(solution)/shard_map/ppermute | solution.py:177
  21.9 3.5 %collective-permute-start.2 = (bf16[144,1792]{1,0:T(8,128)(2,1)S(1)}, bf16[144,1792]{1,0:T(8,128)(2,1)S(1)}, u32[]{:S(2)}, u32[]{:S(2)}) collective-permute-start(bf16[144,1792]{1,0:T(8,128)(2,1)S(1)} %collective-permute-done.refs_2_.refs_0_), channel_id=1, source_target_pairs={{0,4},{4,8},{8,12},{12,0},{1,5},{5,9},{9,13},{13,1},{16,20},{20,24... | collective-permute-start | bytes 1548296 | tf_op jit(solution)/shard_map/ppermute | solution.py:177
  25.4 2.8 %collective-permute-done.4.refs_0_.far = bf16[256,1792]{1,0:T(8,128)(2,1)S(1)} collective-permute-done((bf16[256,1792]{1,0:T(8,128)(2,1)S(1)}, bf16[256,1792]{1,0:T(8,128)(2,1)S(1)}, u32[]{:S(2)}, u32[]{:S(2)}) %collective-permute-start.4) | collective-permute-done | bytes 917536 | tf_op jit(solution)/shard_map/ppermute | solution.py:177
  28.2 0.7 %product_away.3.refs_2_ = f32[256,512]{1,0:T(8,128)S(1)} custom-call(bf16[256,1792]{1,0:T(8,128)(2,1)S(1)} %collective-permute-done.4.refs_0_.far, bf16[1,1024,1792]{2,1,0:T(8,128)(2,1)S(1)} %copy-done.2, bf16[144,1792]{1,0:T(8,128)(2,1)S(1)} %collective-permute-done.refs_2_.refs_0_), custom_call_target="tpu_custom_call" | custom-call | flops 10000000000 | bytes 1000 | tf_op jit(solution)/shard_map/product_away/pallas_call | solution.py:26
  28.8 0.1 collective-permute-start.7
  28.9 0.7 %product_here.4.refs_4_.refs_0_ = f32[256,512]{1,0:T(8,128)S(1)} custom-call(bf16[256,1792]{1,0:T(8,128)(2,1)S(1)} %collective-permute-done.4.refs_0_.far, bf16[1,1024,1792]{2,1,0:T(8,128)(2,1)S(1)} %copy-done.2, f32[256,512]{1,0:T(8,128)S(1)} %product_away.3.refs_2_), custom_call_target="tpu_custom_call" | custom-call | flops 10000000000 | bytes 1000 | tf_op jit(solution)/shard_map/product_here/pallas_call | solution.py:26
  29.6 1.8 %collective-permute-start.9 = (bf16[512,256]{1,0:T(8,128)(2,1)S(1)}, bf16[512,256]{1,0:T(8,128)(2,1)S(1)}, u32[]{:S(2)}, u32[]{:S(2)}) collective-permute-start(bf16[512,256]{1,0:T(8,128)(2,1)S(1)} %get-tuple-element.27), channel_id=1, source_target_pairs={{0,2},{2,4},{4,6},{6,8},{8,10},{10,12},{12,14},{14,0},{1,3},{3,5},... | collective-permute-start | bytes 786440 | tf_op jit(solution)/shard_map/ppermute | solution.py:177
  31.4 0.0 collective-permute-start.10
  31.4 6.6 %collective-permute-done.3.refs_2_ = bf16[112,1792]{1,0:T(8,128)(2,1)S(1)} collective-permute-done((bf16[112,1792]{1,0:T(8,128)(2,1)S(1)}, bf16[112,1792]{1,0:T(8,128)(2,1)S(1)}, u32[]{:S(2)}, u32[]{:S(2)}) %collective-permute-start.3) | collective-permute-done | bytes 401440 | tf_op jit(solution)/shard_map/ppermute | solution.py:177
  38.0 2.3 %collective-permute-done.2.refs_1_ = bf16[144,1792]{1,0:T(8,128)(2,1)S(1)} collective-permute-done((bf16[144,1792]{1,0:T(8,128)(2,1)S(1)}, bf16[144,1792]{1,0:T(8,128)(2,1)S(1)}, u32[]{:S(2)}, u32[]{:S(2)}) %collective-permute-start.2) | collective-permute-done | bytes 516128 | tf_op jit(solution)/shard_map/ppermute | solution.py:177
  40.2 0.7 %join_near.1 = (bf16[256,1792]{1,0:T(8,128)(2,1)S(1)}, f32[256,512]{1,0:T(8,128)S(1)}) custom-call(bf16[144,1792]{1,0:T(8,128)(2,1)S(1)} %collective-permute-done.refs_2_.refs_0_, bf16[144,1792]{1,0:T(8,128)(2,1)S(1)} %collective-permute-done.2.refs_1_, bf16[112,1792]{1,0:T(8,128)(2,1)S(1)} %collective-permute-done.3.refs_2_, ...), custom_call_target="tpu_custom_call" | custom-call | flops 10000000000 | bytes 1000 | tf_op jit(solution)/shard_map/join_near/pallas_call | solution.py:26
  41.0 0.1 collective-permute-start.5
  41.0 0.7 %product_here.5.refs_0_ = f32[256,512]{1,0:T(8,128)S(1)} custom-call(bf16[256,1792]{1,0:T(8,128)(2,1)S(1)} %get-tuple-element.24.refs_0_.near, bf16[1,1024,1792]{2,1,0:T(8,128)(2,1)S(1)} %copy-done.2, f32[256,512]{1,0:T(8,128)S(1)} %get-tuple-element.25.refs_2_), custom_call_target="tpu_custom_call" | custom-call | flops 10000000000 | bytes 1000 | tf_op jit(solution)/shard_map/product_here/pallas_call | solution.py:26
  41.7 1.2 %collective-permute-done.5.refs_1_ = f32[256,512]{1,0:T(8,128)S(1)} collective-permute-done((f32[256,512]{1,0:T(8,128)S(1)}, f32[256,512]{1,0:T(8,128)S(1)}, u32[]{:S(2)}, u32[]{:S(2)}) %collective-permute-start.5) | collective-permute-done | bytes 524320 | tf_op jit(solution)/shard_map/ppermute | solution.py:180
  43.0 0.1 collective-permute-start.6
  43.0 0.0 collective-permute-done.7.refs_1_
  43.1 0.1 add_halves.5
  43.2 1.1 %collective-permute-start.8 = (bf16[256,512]{1,0:T(8,128)(2,1)S(1)}, bf16[256,512]{1,0:T(8,128)(2,1)S(1)}, u32[]{:S(2)}, u32[]{:S(2)}) collective-permute-start(bf16[256,512]{1,0:T(8,128)(2,1)S(1)} %add_halves.5), channel_id=1, source_target_pairs={{4,0},{6,2},{8,4},{10,6},{12,8},{14,10},{0,12},{2,14},{5,1},{7,3},... | collective-permute-start | bytes 786440 | tf_op jit(solution)/shard_map/ppermute | solution.py:177
  44.2 0.0 collective-permute-done.9.near_hidden
  44.2 0.0 collective-permute-done.10.far_hidden
  44.2 0.0 collective-permute-start.11
  44.2 0.5 collective-permute-start.12
  44.7 2.7 %half_weights.2 = (bf16[1,1024,1792]{2,1,0:T(8,128)(2,1)}, bf16[16,128]{1,0:T(8,128)(2,1)}) custom-call(bf16[1024,256]{1,0:T(8,128)(2,1)S(1)} %get-tuple-element.26.own_hidden, bf16[512,256]{1,0:T(8,128)(2,1)S(1)} %collective-permute-done.10.far_hidden, bf16[512,256]{1,0:T(8,128)(2,1)S(1)} %collective-permute-done.9.near_hidden, ...), custom_call_target="tpu_custom_call" | custom-call | flops 10000000000 | bytes 1000 | tf_op jit(solution)/shard_map/half_weights/pallas_call | solution.py:150
  47.5 0.0 collective-permute-done.11.far_hidden
  47.5 0.0 collective-permute-done.12.near_hidden
  47.5 2.7 %half_weights.3 = (bf16[1,1024,1792]{2,1,0:T(8,128)(2,1)}, bf16[16,128]{1,0:T(8,128)(2,1)S(1)}) custom-call(bf16[1024,256]{1,0:T(8,128)(2,1)S(1)} %get-tuple-element.26.own_hidden, bf16[512,256]{1,0:T(8,128)(2,1)S(1)} %collective-permute-done.11.far_hidden, ...), custom_call_target="tpu_custom_call", output_to_operand_aliasing={{0}: (6, {})} | custom-call | flops 10000000000 | bytes 1000 | tf_op jit(solution)/shard_map/half_weights/pallas_call | solution.py:150
  50.2 1.2 %collective-permute-done.6.refs_2_ = bf16[256,512]{1,0:T(8,128)(2,1)S(1)} collective-permute-done((bf16[256,512]{1,0:T(8,128)(2,1)S(1)}, bf16[256,512]{1,0:T(8,128)(2,1)S(1)}, u32[]{:S(2)}, u32[]{:S(2)}) %collective-permute-start.6) | collective-permute-done | bytes 262176 | tf_op jit(solution)/shard_map/ppermute | solution.py:177
  51.4 3.9 %collective-permute-done.8.refs_3_ = bf16[256,512]{1,0:T(8,128)(2,1)S(1)} collective-permute-done((bf16[256,512]{1,0:T(8,128)(2,1)S(1)}, bf16[256,512]{1,0:T(8,128)(2,1)S(1)}, u32[]{:S(2)}, u32[]{:S(2)}) %collective-permute-start.8) | collective-permute-done | bytes 262176 | tf_op jit(solution)/shard_map/ppermute | solution.py:177
  55.2 1.4 %place_rows.1 = bf16[512,512]{1,0:T(8,128)(2,1)} custom-call(bf16[512,768]{1,0:T(8,128)(2,1)S(1)} %get-tuple-element.18.refs_2_.refs_0_, bf16[256,512]{1,0:T(8,128)(2,1)S(1)} %add_halves.3.refs_1_, bf16[256,512]{1,0:T(8,128)(2,1)S(1)} %collective-permute-done.6.refs_2_, bf16[256,512]{1,0:T(8,128)(2,1)S(1)} %collective-permute-done.8.refs_3_, ...), custom_call_target="tpu_custom_call" | custom-call | flops 10000000000 | bytes 1000 | tf_op jit(solution)/shard_map/place_rows/pallas_call | solution.py:26
  (4 shorter events, 0.1 us)
Async XLA Ops:
  1.9 26.3 %collective-permute-start.4 = (bf16[256,1792]{1,0:T(8,128)(2,1)S(1)}, bf16[256,1792]{1,0:T(8,128)(2,1)S(1)}, u32[]{:S(2)}, u32[]{:S(2)}) collective-permute-start(bf16[256,1792]{1,0:T(8,128)(2,1)S(1)} %slice.3.refs_2_), channel_id=1, source_target_pairs={{0,4},{2,6},{4,8},{6,10},{8,12},{10,14},{12,0},{14,2},{1,5},{3,7},... | collective-permute-start | bytes 2752520 | tf_op jit(solution)/shard_map/ppermute | solution.py:177
  5.0 1.5 %copy-start = (bf16[512,1792]{1,0:T(8,128)(2,1)S(1)}, bf16[512,1792]{1,0:T(8,128)(2,1)}, u32[]{:S(2)}) copy-start(bf16[512,1792]{1,0:T(8,128)(2,1)} %own.3) | copy-start | bytes 5505028
  6.5 0.7 %copy-start.4 = (s32[1,3]{1,0:T(1,128)S(1)}, s32[1,3]{1,0:T(1,128)}, u32[]{:S(2)}) copy-start(s32[1,3]{1,0:T(1,128)} %refs_0_.9) | copy-start | bytes 40
  7.1 2.6 %copy-start.1 = (bf16[512,1792]{1,0:T(8,128)(2,1)S(1)}, bf16[512,1792]{1,0:T(8,128)(2,1)}, u32[]{:S(2)}) copy-start(bf16[512,1792]{1,0:T(8,128)(2,1)} %own.3) | copy-start | bytes 5505028
  7.1 2.6 %copy-start.2 = (bf16[1,1024,1792]{2,1,0:T(8,128)(2,1)S(1)}, bf16[1,1024,1792]{2,1,0:T(8,128)(2,1)}, u32[]{:S(2)}) copy-start(bf16[1,1024,1792]{2,1,0:T(8,128)(2,1)} %refs_1_.15) | copy-start | bytes 11010052
  8.1 13.8 %collective-permute-start = (bf16[144,1792]{1,0:T(8,128)(2,1)S(1)}, bf16[144,1792]{1,0:T(8,128)(2,1)S(1)}, u32[]{:S(2)}, u32[]{:S(2)}) collective-permute-start(bf16[144,1792]{1,0:T(8,128)(2,1)S(1)} %pick_turned.1.refs_2_), channel_id=1, source_target_pairs={{0,2},{2,0},{4,6},{6,4},{8,10},{10,8},{12,14},{14,12},{1,3},{3,1},... | collective-permute-start | bytes 1548296 | tf_op jit(solution)/shard_map/ppermute | solution.py:177
  10.4 1.2 %copy-start.3 = (bf16[512,1024]{1,0:T(8,128)(2,1)S(1)}, bf16[512,1024]{1,0:T(8,128)(2,1)}, u32[]{:S(2)}) copy-start(bf16[512,1024]{1,0:T(8,128)(2,1)} %refs_1_.11) | copy-start | bytes 3145732
  10.4 5.2 %collective-permute-start.1 = (f32[256,512]{1,0:T(8,128)S(1)}, f32[256,512]{1,0:T(8,128)S(1)}, u32[]{:S(2)}, u32[]{:S(2)}) collective-permute-start(f32[256,512]{1,0:T(8,128)S(1)} %product_away.2.refs_2_), channel_id=1, source_target_pairs={{0,1},{1,0},{2,3},{3,2},{4,5},{5,4},{6,7},{7,6},{8,9},{9,8},{10,11... | collective-permute-start | bytes 1572872 | tf_op jit(solution)/shard_map/ppermute | solution.py:180
  14.0 24.0 %collective-permute-start.3 = (bf16[112,1792]{1,0:T(8,128)(2,1)S(1)}, bf16[112,1792]{1,0:T(8,128)(2,1)S(1)}, u32[]{:S(2)}, u32[]{:S(2)}) collective-permute-start(bf16[112,1792]{1,0:T(8,128)(2,1)S(1)} %pick_direct.1.refs_2_), channel_id=1, source_target_pairs={{0,2},{2,4},{4,6},{6,8},{8,10},{10,12},{12,14},{14,0},{1,3},{3,5},... | collective-permute-start | bytes 1204232 | tf_op jit(solution)/shard_map/ppermute | solution.py:177
  21.9 18.4 %collective-permute-start.2 = (bf16[144,1792]{1,0:T(8,128)(2,1)S(1)}, bf16[144,1792]{1,0:T(8,128)(2,1)S(1)}, u32[]{:S(2)}, u32[]{:S(2)}) collective-permute-start(bf16[144,1792]{1,0:T(8,128)(2,1)S(1)} %collective-permute-done.refs_2_.refs_0_), channel_id=1, source_target_pairs={{0,4},{4,8},{8,12},{12,0},{1,5},{5,9},{9,13},{13,1},{16,20},{20,24... | collective-permute-start | bytes 1548296 | tf_op jit(solution)/shard_map/ppermute | solution.py:177
  28.8 14.2 %collective-permute-start.7 = (f32[256,512]{1,0:T(8,128)S(1)}, f32[256,512]{1,0:T(8,128)S(1)}, u32[]{:S(2)}, u32[]{:S(2)}) collective-permute-start(f32[256,512]{1,0:T(8,128)S(1)} %product_away.3.refs_2_), channel_id=1, source_target_pairs={{0,1},{1,0},{2,3},{3,2},{4,5},{5,4},{6,7},{7,6},{8,9},{9,8},{10,11... | collective-permute-start | bytes 1572872 | tf_op jit(solution)/shard_map/ppermute | solution.py:180
  29.6 14.6 %collective-permute-start.9 = (bf16[512,256]{1,0:T(8,128)(2,1)S(1)}, bf16[512,256]{1,0:T(8,128)(2,1)S(1)}, u32[]{:S(2)}, u32[]{:S(2)}) collective-permute-start(bf16[512,256]{1,0:T(8,128)(2,1)S(1)} %get-tuple-element.27), channel_id=1, source_target_pairs={{0,2},{2,4},{4,6},{6,8},{8,10},{10,12},{12,14},{14,0},{1,3},{3,5},... | collective-permute-start | bytes 786440 | tf_op jit(solution)/shard_map/ppermute | solution.py:177
  31.4 12.8 %collective-permute-start.10 = (bf16[512,256]{1,0:T(8,128)(2,1)S(1)}, bf16[512,256]{1,0:T(8,128)(2,1)S(1)}, u32[]{:S(2)}, u32[]{:S(2)}) collective-permute-start(bf16[512,256]{1,0:T(8,128)(2,1)S(1)} %get-tuple-element.28), channel_id=1, source_target_pairs={{0,4},{2,6},{4,8},{6,10},{8,12},{10,14},{12,0},{14,2},{1,5},{3,7},... | collective-permute-start | bytes 786440 | tf_op jit(solution)/shard_map/ppermute | solution.py:177
  41.0 2.0 %collective-permute-start.5 = (f32[256,512]{1,0:T(8,128)S(1)}, f32[256,512]{1,0:T(8,128)S(1)}, u32[]{:S(2)}, u32[]{:S(2)}) collective-permute-start(f32[256,512]{1,0:T(8,128)S(1)} %get-tuple-element.25.refs_2_), channel_id=1, source_target_pairs={{0,1},{1,0},{2,3},{3,2},{4,5},{5,4},{6,7},{7,6},{8,9},{9,8},{10,11... | collective-permute-start | bytes 1572872 | tf_op jit(solution)/shard_map/ppermute | solution.py:180
  43.0 8.4 %collective-permute-start.6 = (bf16[256,512]{1,0:T(8,128)(2,1)S(1)}, bf16[256,512]{1,0:T(8,128)(2,1)S(1)}, u32[]{:S(2)}, u32[]{:S(2)}) collective-permute-start(bf16[256,512]{1,0:T(8,128)(2,1)S(1)} %add_halves.4.refs_2_), channel_id=1, source_target_pairs={{2,0},{4,2},{6,4},{8,6},{10,8},{12,10},{14,12},{0,14},{3,1},{5,3},... | collective-permute-start | bytes 786440 | tf_op jit(solution)/shard_map/ppermute | solution.py:177
  43.2 12.1 %collective-permute-start.8 = (bf16[256,512]{1,0:T(8,128)(2,1)S(1)}, bf16[256,512]{1,0:T(8,128)(2,1)S(1)}, u32[]{:S(2)}, u32[]{:S(2)}) collective-permute-start(bf16[256,512]{1,0:T(8,128)(2,1)S(1)} %add_halves.5), channel_id=1, source_target_pairs={{4,0},{6,2},{8,4},{10,6},{12,8},{14,10},{0,12},{2,14},{5,1},{7,3},... | collective-permute-start | bytes 786440 | tf_op jit(solution)/shard_map/ppermute | solution.py:177
  44.2 3.2 %collective-permute-start.11 = (bf16[512,256]{1,0:T(8,128)(2,1)S(1)}, bf16[512,256]{1,0:T(8,128)(2,1)S(1)}, u32[]{:S(2)}, u32[]{:S(2)}) collective-permute-start(bf16[512,256]{1,0:T(8,128)(2,1)S(1)} %collective-permute-done.10.far_hidden), channel_id=1, source_target_pairs={{0,1},{1,0},{2,3},{3,2},{4,5},{5,4},{6,7},{7,6},{8,9},{9,8},{10,11... | collective-permute-start | bytes 786440 | tf_op jit(solution)/shard_map/ppermute | solution.py:180
  44.2 3.2 %collective-permute-start.12 = (bf16[512,256]{1,0:T(8,128)(2,1)S(1)}, bf16[512,256]{1,0:T(8,128)(2,1)S(1)}, u32[]{:S(2)}, u32[]{:S(2)}) collective-permute-start(bf16[512,256]{1,0:T(8,128)(2,1)S(1)} %collective-permute-done.9.near_hidden), channel_id=1, source_target_pairs={{0,1},{1,0},{2,3},{3,2},{4,5},{5,4},{6,7},{7,6},{8,9},{9,8},{10,11... | collective-permute-start | bytes 786440 | tf_op jit(solution)/shard_map/ppermute | solution.py:180

commit v5 on v4

--- a/solution.py
+++ b/solution.py
@@ -8,7 +8,7 @@
 from jax.sharding import PartitionSpec as P
 
 CAP = 256
-RELAYED = 144
+RELAYED = 128
 LAST = 2
 TILE = 256
 BLOCK = 256
@@ -85,11 +85,15 @@
         direct[:, tile] = dot(pick, grad_out[:, tile]).astype(BF16)
 
 
-def pick_hidden(counts, hidden, far, near, own, places):
+def pick_hidden(counts, hidden, far, near):
     rows, units = hidden.shape
     columns = half_of(lax.axis_index("loc"), units // 2)
     for index, out in ((2, far), (1, near)):
         out[...] = dot(hidden[:, columns], picker(counts, index, rows), (0, 1)).astype(BF16)
+
+
+def pick_own(counts, hidden, own, places):
+    rows, units = hidden.shape
     pick = picker(counts, 0, rows)
     for tile in tiles(units):
         own[tile, :] = dot(hidden[:, tile], pick, (0, 1)).astype(BF16)
@@ -126,21 +130,27 @@
     out[...] = (here[...] + other[...]).astype(BF16)
 
 
-def place_rows(places, own, near, far, out):
+def place_first(places, own, near, out):
     total = dot(places[:, :CAP], own[...])
-    total = total + dot(places[:, CAP : 2 * CAP], near[...])
-    total = total + dot(places[:, 2 * CAP :], far[...])
-    out[...] = total.astype(BF16)
-
-
-def half_weights(side, own_hidden, far_hidden, near_hidden, own, far, near, *refs):
+    out[...] = (total + dot(places[:, CAP : 2 * CAP], near[...])).astype(BF16)
+
+
+def place_last(places, first, far, out):
+    out[...] = (first[...].astype(F32) + dot(places[:, 2 * CAP :], far[...])).astype(BF16)
+
+
+def own_weights(own_hidden, own, total):
+    for tile in tiles(own.shape[1]):
+        total[:, tile] = dot(own_hidden[...], own[:CAP, tile])
+
+
+def half_weights(side, far_hidden, near_hidden, far, near, before, *refs):
     out, token = refs[-2:]
     step = pl.program_id(0)
     rows = half_of(step, BLOCK)
     whole = half_of(side() * (far_hidden.shape[0] // BLOCK) + step, BLOCK)
     for tile in tiles(far.shape[1]):
-        total = dot(own_hidden[whole, :], own[:CAP, tile])
-        total = total + dot(far_hidden[rows, :], far[:, tile])
+        total = before[whole, tile] + dot(far_hidden[rows, :], far[:, tile])
         out[0, :, tile] = (total + dot(near_hidden[rows, :], near[:, tile])).astype(BF16)
     token[...] = jnp.zeros_like(token)
 
@@ -189,13 +199,11 @@
     (own_away,) = call(product_away, [partial], grad_out, weights, after=(turned,))
     own_other = swap_cores(own_away)
     (own_here,) = call(product_here, [partial], grad_out, weights, after=(own_away,))
-    far_hidden, near_hidden, own_hidden, places = call(
-        pick_hidden,
-        [((half, CAP), BF16), ((half, CAP), BF16), ((units, CAP), BF16), ((rows, 3 * CAP), BF16)],
-        counts, hidden, scalars=1, after=(own_here,),
+    far_hidden, near_hidden = call(
+        pick_hidden, [((half, CAP), BF16), ((half, CAP), BF16)], counts, hidden, scalars=1, after=(own_here,)
     )
     (direct,) = call(
-        pick_direct, [((CAP - RELAYED, features), BF16)], counts, grad_out, scalars=1, after=(places,)
+        pick_direct, [((CAP - RELAYED, features), BF16)], counts, grad_out, scalars=1, after=(far_hidden,)
     )
     direct_in = send(direct, by1)
     (own_block,) = call(add_halves, [block], own_here, own_other, after=(direct,))
@@ -217,20 +225,23 @@
     (near_here,) = call(product_here, [partial], near_in, weights, after=(near_away,))
     (near_block,) = call(add_halves, [block], near_here, near_other)
     near_back = send(near_block, back1)
-    (far_block,) = call(add_halves, [block], far_here, far_other, after=(near_block,))
+    own_hidden, places = call(
+        pick_own, [((units, CAP), BF16), ((rows, 3 * CAP), BF16)], counts, hidden, scalars=1, after=(near_block,)
+    )
+    (total,) = call(own_weights, [((units, features), F32)], own_hidden, grad_out)
+    (far_block,) = call(add_halves, [block], far_here, far_other, after=(total,))
     far_back = send(far_block, back2)
 
     near_hidden_in, far_hidden_in, far_block = lax.optimization_barrier((near_hidden_in, far_hidden_in, far_block))
     here, _ = rows_of_half(
-        lambda: lax.axis_index("loc"), own_hidden, far_hidden_in, near_hidden_in, grad_out, far_in, near_in, units=units, features=features
+        lambda: lax.axis_index("loc"), far_hidden_in, near_hidden_in, far_in, near_in, total, units=units, features=features
     )
     grad_weights, done = rows_of_half(
-        lambda: 1 - lax.axis_index("loc"), own_hidden, swap_cores(far_hidden_in), swap_cores(near_hidden_in), grad_out, far_in, near_in,
+        lambda: 1 - lax.axis_index("loc"), swap_cores(far_hidden_in), swap_cores(near_hidden_in), far_in, near_in, total,
         units=units, features=features, before=(here,),
     )
-    (grad_hidden,) = call(
-        place_rows, [((rows, half), BF16)], places, own_block, near_back, far_back, after=(done,)
-    )
+    (placed,) = call(place_first, [((rows, half), BF16)], places, own_block, near_back, after=(done,))
+    (grad_hidden,) = call(place_last, [((rows, half), BF16)], places, placed, far_back)
     return grad_hidden, grad_weights
 
 

time: 56.9 us -> 55.4 us (0.974)
  waiting for transfers between devices: 24.1 us -> 20.8 us
  Pallas kernels: 14.4 us -> 15.4 us
  starting transfers between devices: 13.4 us -> 14.2 us
    ppermute x8, waiting for transfers between devices: 22.9 us -> 19.6 us  [send(): return lax.ppermute(value, 'grp', pairs)]
    pallas_call x13 -> x16, Pallas kernels: 9 us -> 10.8 us  [call(): pl.pallas_call(body, out_shape=[jax.ShapeDtypeStruct(shape, dtype) for sh...]
    pallas_call x2, Pallas kernels: 5.45 us -> 4.53 us  [rows_of_half(): pl.pallas_call(functools.partial(half_weights, side), out_shape=[jax.Shap...]
    ppermute x8, starting transfers between devices: 12.7 us -> 13.4 us  [send(): return lax.ppermute(value, 'grp', pairs)]
    unnamed x10 -> x12, local copies, waits for them, and re-layouts: 2.63 us -> 2.67 us
  transfers between devices with their start and end apart: 13 -> 13, of which waited for: 7 -> 5; matrix products, arithmetic and copies ran while one was open for 0% -> 0% of each run, Pallas kernels for 23% -> 26%
where the time goes in v5:
time: 55.4 us; the launch traced here: 55.1 us
  waiting for transfers between devices  20.8 us (38%)
  Pallas kernels  15.4 us (28%)
  starting transfers between devices  14.2 us (26%)
  local copies, waits for them, and re-layouts  3.91 us (7%)
  between operations  0.83 us (1%)
    ppermute x8, waiting for transfers between devices, send(): return lax.ppermute(value, 'grp', pairs)  19.6 us
    ppermute x8, starting transfers between devices, send(): return lax.ppermute(value, 'grp', pairs)  13.4 us
    pallas_call x16, Pallas kernels, call(): pl.pallas_call(body, out_shape=[jax.ShapeDtypeStruct(shape, dtype) for sh...  10.8 us
    pallas_call x2, Pallas kernels, rows_of_half(): pl.pallas_call(functools.partial(half_weights, side), out_shape=[jax.Shap...  4.53 us
    unnamed x12, local copies, waits for them, and re-layouts  2.67 us
    slice x1, local copies, waits for them, and re-layouts, local(): far = grad_out[rows - CAP:]  1.24 us
    ppermute x5, waiting for transfers between devices, swap_cores(): return lax.ppermute(value, 'loc', [(0, 1), (1, 0)])  1.21 us
  transfers between devices with their start and end apart: 13, of which 5 were waited for; matrix products, arithmetic and copies ran while one was open for 0% of the time, Pallas kernels for 26%

profile of v5, /device:TPU:0, one launch (start us, length us, event | category | flops | bytes accessed | tf_op | source)
XLA Modules:
  0.0 55.1 jit_solution(9895342083718242176)
XLA Ops:
  0.6 1.2 %slice.3.refs_2_ = bf16[256,1792]{1,0:T(8,128)(2,1)S(1)} slice(bf16[512,1792]{1,0:T(8,128)(2,1)} %refs_1_.19), slice={[256:512], [0:1792]} | slice | bytes 1835008 | tf_op jit(solution)/shard_map/slice | solution.py:194
  1.9 3.1 %collective-permute-start.4 = (bf16[256,1792]{1,0:T(8,128)(2,1)S(1)}, bf16[256,1792]{1,0:T(8,128)(2,1)S(1)}, u32[]{:S(2)}, u32[]{:S(2)}) collective-permute-start(bf16[256,1792]{1,0:T(8,128)(2,1)S(1)} %slice.3.refs_2_), channel_id=1, source_target_pairs={{0,4},{2,6},{4,8},{6,10},{8,12},{10,14},{12,0},{14,2},{1,5},{3,7},... | collective-permute-start | bytes 2752520 | tf_op jit(solution)/shard_map/ppermute | solution.py:187
  5.0 1.5 %copy-done = bf16[512,1792]{1,0:T(8,128)(2,1)S(1)} copy-done((bf16[512,1792]{1,0:T(8,128)(2,1)S(1)}, bf16[512,1792]{1,0:T(8,128)(2,1)}, u32[]{:S(2)}) %copy-start) | copy-done | bytes 1835032
  6.5 0.7 %copy-done.4 = s32[1,3]{1,0:T(1,128)S(1)} copy-done((s32[1,3]{1,0:T(1,128)S(1)}, s32[1,3]{1,0:T(1,128)}, u32[]{:S(2)}) %copy-start.4) | copy-done | bytes 36
  7.1 0.9 %pick_turned.1.refs_2_ = bf16[128,1792]{1,0:T(8,128)(2,1)S(1)} custom-call(s32[1,3]{1,0:T(1,128)S(1)} %copy-done.4, bf16[512,1792]{1,0:T(8,128)(2,1)S(1)} %copy-done, bf16[256,1792]{1,0:T(8,128)(2,1)S(1)} %slice.3.refs_2_), custom_call_target="tpu_custom_call" | custom-call | flops 10000000000 | bytes 1000 | tf_op jit(solution)/shard_map/pick_turned/pallas_call | solution.py:26
  8.1 1.6 %collective-permute-start = (bf16[128,1792]{1,0:T(8,128)(2,1)S(1)}, bf16[128,1792]{1,0:T(8,128)(2,1)S(1)}, u32[]{:S(2)}, u32[]{:S(2)}) collective-permute-start(bf16[128,1792]{1,0:T(8,128)(2,1)S(1)} %pick_turned.1.refs_2_), channel_id=1, source_target_pairs={{0,2},{2,0},{4,6},{6,4},{8,10},{10,8},{12,14},{14,12},{1,3},{3,1},... | collective-permute-start | bytes 1376264 | tf_op jit(solution)/shard_map/ppermute | solution.py:187
  9.7 0.0 copy-done.2
  9.7 0.7 %product_away.2.refs_2_ = f32[256,512]{1,0:T(8,128)S(1)} custom-call(bf16[512,1792]{1,0:T(8,128)(2,1)S(1)} %copy-done.1, bf16[1,1024,1792]{2,1,0:T(8,128)(2,1)S(1)} %copy-done.2, bf16[128,1792]{1,0:T(8,128)(2,1)S(1)} %pick_turned.1.refs_2_), custom_call_target="tpu_custom_call" | custom-call | flops 10000000000 | bytes 1000 | tf_op jit(solution)/shard_map/product_away/pallas_call | solution.py:26
  10.4 0.0 copy-start.3
  10.4 0.1 collective-permute-start.1
  10.5 0.7 %product_here.3.refs_2_.refs_0_ = f32[256,512]{1,0:T(8,128)S(1)} custom-call(bf16[512,1792]{1,0:T(8,128)(2,1)S(1)} %copy-done.1, bf16[1,1024,1792]{2,1,0:T(8,128)(2,1)S(1)} %copy-done.2, f32[256,512]{1,0:T(8,128)S(1)} %product_away.2.refs_2_), custom_call_target="tpu_custom_call" | custom-call | flops 10000000000 | bytes 1000 | tf_op jit(solution)/shard_map/product_here/pallas_call | solution.py:26
  11.1 0.5 copy-done.3
  11.6 1.0 %pick_hidden.1 = (bf16[512,256]{1,0:T(8,128)(2,1)S(1)}, bf16[512,256]{1,0:T(8,128)(2,1)S(1)}) custom-call(s32[1,3]{1,0:T(1,128)S(1)} %copy-done.4, bf16[512,1024]{1,0:T(8,128)(2,1)S(1)} %copy-done.3, f32[256,512]{1,0:T(8,128)S(1)} %product_here.3.refs_2_.refs_0_), custom_call_target="tpu_custom_call" | custom-call | flops 10000000000 | bytes 1000 | tf_op jit(solution)/shard_map/pick_hidden/pallas_call | solution.py:26
  12.6 1.0 %pick_direct.1.refs_2_ = bf16[128,1792]{1,0:T(8,128)(2,1)S(1)} custom-call(s32[1,3]{1,0:T(1,128)S(1)} %copy-done.4, bf16[512,1792]{1,0:T(8,128)(2,1)S(1)} %copy-done.1, bf16[512,256]{1,0:T(8,128)(2,1)S(1)} %get-tuple-element.27.refs_2_), custom_call_target="tpu_custom_call" | custom-call | flops 10000000000 | bytes 1000 | tf_op jit(solution)/shard_map/pick_direct/pallas_call | solution.py:26
  13.6 1.6 %collective-permute-start.3 = (bf16[128,1792]{1,0:T(8,128)(2,1)S(1)}, bf16[128,1792]{1,0:T(8,128)(2,1)S(1)}, u32[]{:S(2)}, u32[]{:S(2)}) collective-permute-start(bf16[128,1792]{1,0:T(8,128)(2,1)S(1)} %pick_direct.1.refs_2_), channel_id=1, source_target_pairs={{0,2},{2,4},{4,6},{6,8},{8,10},{10,12},{12,14},{14,0},{1,3},{3,5},... | collective-permute-start | bytes 1376264 | tf_op jit(solution)/shard_map/ppermute | solution.py:187
  15.2 0.0 collective-permute-done.1.refs_1_
  15.2 5.4 %collective-permute-done.refs_2_.refs_0_ = bf16[128,1792]{1,0:T(8,128)(2,1)S(1)} collective-permute-done((bf16[128,1792]{1,0:T(8,128)(2,1)S(1)}, bf16[128,1792]{1,0:T(8,128)(2,1)S(1)}, u32[]{:S(2)}, u32[]{:S(2)}) %collective-permute-start) | collective-permute-done | bytes 458784 | tf_op jit(solution)/shard_map/ppermute | solution.py:187
  20.6 3.5 %collective-permute-start.2 = (bf16[128,1792]{1,0:T(8,128)(2,1)S(1)}, bf16[128,1792]{1,0:T(8,128)(2,1)S(1)}, u32[]{:S(2)}, u32[]{:S(2)}) collective-permute-start(bf16[128,1792]{1,0:T(8,128)(2,1)S(1)} %collective-permute-done.refs_2_.refs_0_), channel_id=1, source_target_pairs={{0,4},{4,8},{8,12},{12,0},{1,5},{5,9},{9,13},{13,1},{16,20},{20,24... | collective-permute-start | bytes 1376264 | tf_op jit(solution)/shard_map/ppermute | solution.py:187
  24.1 4.1 %collective-permute-done.4.refs_0_.far = bf16[256,1792]{1,0:T(8,128)(2,1)S(1)} collective-permute-done((bf16[256,1792]{1,0:T(8,128)(2,1)S(1)}, bf16[256,1792]{1,0:T(8,128)(2,1)S(1)}, u32[]{:S(2)}, u32[]{:S(2)}) %collective-permute-start.4) | collective-permute-done | bytes 917536 | tf_op jit(solution)/shard_map/ppermute | solution.py:187
  28.2 0.7 %product_away.3.refs_2_ = f32[256,512]{1,0:T(8,128)S(1)} custom-call(bf16[256,1792]{1,0:T(8,128)(2,1)S(1)} %collective-permute-done.4.refs_0_.far, bf16[1,1024,1792]{2,1,0:T(8,128)(2,1)S(1)} %copy-done.2, bf16[128,1792]{1,0:T(8,128)(2,1)S(1)} %collective-permute-done.refs_2_.refs_0_), custom_call_target="tpu_custom_call" | custom-call | flops 10000000000 | bytes 1000 | tf_op jit(solution)/shard_map/product_away/pallas_call | solution.py:26
  28.8 0.1 collective-permute-start.9
  28.9 0.7 %product_here.4.refs_4_.refs_0_ = f32[256,512]{1,0:T(8,128)S(1)} custom-call(bf16[256,1792]{1,0:T(8,128)(2,1)S(1)} %collective-permute-done.4.refs_0_.far, bf16[1,1024,1792]{2,1,0:T(8,128)(2,1)S(1)} %copy-done.2, f32[256,512]{1,0:T(8,128)S(1)} %product_away.3.refs_2_), custom_call_target="tpu_custom_call" | custom-call | flops 10000000000 | bytes 1000 | tf_op jit(solution)/shard_map/product_here/pallas_call | solution.py:26
  29.6 1.8 %collective-permute-start.7 = (bf16[512,256]{1,0:T(8,128)(2,1)S(1)}, bf16[512,256]{1,0:T(8,128)(2,1)S(1)}, u32[]{:S(2)}, u32[]{:S(2)}) collective-permute-start(bf16[512,256]{1,0:T(8,128)(2,1)S(1)} %get-tuple-element.26), channel_id=1, source_target_pairs={{0,2},{2,4},{4,6},{6,8},{8,10},{10,12},{12,14},{14,0},{1,3},{3,5},... | collective-permute-start | bytes 786440 | tf_op jit(solution)/shard_map/ppermute | solution.py:187
  31.4 0.0 collective-permute-start.8
  31.4 7.8 %collective-permute-done.3.refs_2_ = bf16[128,1792]{1,0:T(8,128)(2,1)S(1)} collective-permute-done((bf16[128,1792]{1,0:T(8,128)(2,1)S(1)}, bf16[128,1792]{1,0:T(8,128)(2,1)S(1)}, u32[]{:S(2)}, u32[]{:S(2)}) %collective-permute-start.3) | collective-permute-done | bytes 458784 | tf_op jit(solution)/shard_map/ppermute | solution.py:187
  39.2 0.0 collective-permute-done.2.refs_1_
  39.2 0.7 %join_near.1 = (bf16[256,1792]{1,0:T(8,128)(2,1)S(1)}, f32[256,512]{1,0:T(8,128)S(1)}) custom-call(bf16[128,1792]{1,0:T(8,128)(2,1)S(1)} %collective-permute-done.refs_2_.refs_0_, bf16[128,1792]{1,0:T(8,128)(2,1)S(1)} %collective-permute-done.2.refs_1_, bf16[128,1792]{1,0:T(8,128)(2,1)S(1)} %collective-permute-done.3.refs_2_, ...), custom_call_target="tpu_custom_call" | custom-call | flops 10000000000 | bytes 1000 | tf_op jit(solution)/shard_map/join_near/pallas_call | solution.py:26
  39.9 0.1 collective-permute-start.5
  40.0 0.7 %product_here.5.refs_0_ = f32[256,512]{1,0:T(8,128)S(1)} custom-call(bf16[256,1792]{1,0:T(8,128)(2,1)S(1)} %get-tuple-element.22.refs_0_.near, bf16[1,1024,1792]{2,1,0:T(8,128)(2,1)S(1)} %copy-done.2, f32[256,512]{1,0:T(8,128)S(1)} %get-tuple-element.23.refs_2_), custom_call_target="tpu_custom_call" | custom-call | flops 10000000000 | bytes 1000 | tf_op jit(solution)/shard_map/product_here/pallas_call | solution.py:26
  40.7 0.0 copy-start.5
  40.7 1.2 %collective-permute-done.5.refs_1_ = f32[256,512]{1,0:T(8,128)S(1)} collective-permute-done((f32[256,512]{1,0:T(8,128)S(1)}, f32[256,512]{1,0:T(8,128)S(1)}, u32[]{:S(2)}, u32[]{:S(2)}) %collective-permute-start.5) | collective-permute-done | bytes 524320 | tf_op jit(solution)/shard_map/ppermute | solution.py:190
  41.9 0.1 collective-permute-start.6
  42.0 1.1 %pick_own.1 = (bf16[1024,256]{1,0:T(8,128)(2,1)S(1)}, bf16[512,768]{1,0:T(8,128)(2,1)S(1)}) custom-call(s32[1,3]{1,0:T(1,128)S(1)} %copy-done.5, bf16[512,1024]{1,0:T(8,128)(2,1)S(1)} %copy-done.3, bf16[256,512]{1,0:T(8,128)(2,1)S(1)} %add_halves.4.refs_2_), custom_call_target="tpu_custom_call" | custom-call | flops 10000000000 | bytes 1000 | tf_op jit(solution)/shard_map/pick_own/pallas_call | solution.py:26
  43.1 1.1 %own_weights.1.refs_2_.before = f32[1024,1792]{1,0:T(8,128)S(1)} custom-call(bf16[1024,256]{1,0:T(8,128)(2,1)S(1)} %get-tuple-element.28.refs_0_, bf16[512,1792]{1,0:T(8,128)(2,1)S(1)} %copy-done.1), custom_call_target="tpu_custom_call" | custom-call | flops 10000000000 | bytes 1000 | tf_op jit(solution)/shard_map/own_weights/pallas_call | solution.py:26
  44.2 0.0 collective-permute-done.9.refs_1_
  44.2 0.1 add_halves.5
  44.3 1.9 %collective-permute-start.12 = (bf16[256,512]{1,0:T(8,128)(2,1)S(1)}, bf16[256,512]{1,0:T(8,128)(2,1)S(1)}, u32[]{:S(2)}, u32[]{:S(2)}) collective-permute-start(bf16[256,512]{1,0:T(8,128)(2,1)S(1)} %add_halves.5), channel_id=1, source_target_pairs={{4,0},{6,2},{8,4},{10,6},{12,8},{14,10},{0,12},{2,14},{5,1},{7,3},... | collective-permute-start | bytes 786440 | tf_op jit(solution)/shard_map/ppermute | solution.py:187
  46.1 0.0 collective-permute-done.7.near_hidden
  46.1 0.0 collective-permute-done.8.far_hidden
  46.1 0.0 collective-permute-start.10
  46.1 0.5 collective-permute-start.11
  46.6 2.3 %half_weights.2 = (bf16[1,1024,1792]{2,1,0:T(8,128)(2,1)}, bf16[16,128]{1,0:T(8,128)(2,1)}) custom-call(bf16[512,256]{1,0:T(8,128)(2,1)S(1)} %collective-permute-done.8.far_hidden, bf16[512,256]{1,0:T(8,128)(2,1)S(1)} %collective-permute-done.7.near_hidden, bf16[256,1792]{1,0:T(8,128)(2,1)S(1)} %collective-permute-done.4.refs_0_.far, ...), custom_call_target="tpu_custom_call" | custom-call | flops 10000000000 | bytes 1000 | tf_op jit(solution)/shard_map/half_weights/pallas_call | solution.py:160
  48.9 0.0 collective-permute-done.10.far_hidden
  48.9 2.3 %half_weights.3 = (bf16[1,1024,1792]{2,1,0:T(8,128)(2,1)}, bf16[16,128]{1,0:T(8,128)(2,1)S(1)}) custom-call(bf16[512,256]{1,0:T(8,128)(2,1)S(1)} %collective-permute-done.10.far_hidden, bf16[512,256]{1,0:T(8,128)(2,1)S(1)} %collective-permute-done.11.near_hidden, ...), custom_call_target="tpu_custom_call", output_to_operand_aliasing={{0}: (5, {})} | custom-call | flops 10000000000 | bytes 1000 | tf_op jit(solution)/shard_map/half_weights/pallas_call | solution.py:160
  51.2 0.0 collective-permute-done.6.refs_2_
  51.2 0.4 place_first.1.refs_1_
  51.6 2.4 %collective-permute-done.12.refs_2_ = bf16[256,512]{1,0:T(8,128)(2,1)S(1)} collective-permute-done((bf16[256,512]{1,0:T(8,128)(2,1)S(1)}, bf16[256,512]{1,0:T(8,128)(2,1)S(1)}, u32[]{:S(2)}, u32[]{:S(2)}) %collective-permute-start.12) | collective-permute-done | bytes 262176 | tf_op jit(solution)/shard_map/ppermute | solution.py:187
  54.0 1.1 %place_last.1 = bf16[512,512]{1,0:T(8,128)(2,1)} custom-call(bf16[512,768]{1,0:T(8,128)(2,1)S(1)} %get-tuple-element.24.refs_0_, bf16[512,512]{1,0:T(8,128)(2,1)S(1)} %place_first.1.refs_1_, bf16[256,512]{1,0:T(8,128)(2,1)S(1)} %collective-permute-done.12.refs_2_), custom_call_target="tpu_custom_call" | custom-call | flops 10000000000 | bytes 1000 | tf_op jit(solution)/shard_map/place_last/pallas_call | solution.py:26
  (9 shorter events, 0.1 us)
Async XLA Ops:
  1.9 26.3 %collective-permute-start.4 = (bf16[256,1792]{1,0:T(8,128)(2,1)S(1)}, bf16[256,1792]{1,0:T(8,128)(2,1)S(1)}, u32[]{:S(2)}, u32[]{:S(2)}) collective-permute-start(bf16[256,1792]{1,0:T(8,128)(2,1)S(1)} %slice.3.refs_2_), channel_id=1, source_target_pairs={{0,4},{2,6},{4,8},{6,10},{8,12},{10,14},{12,0},{14,2},{1,5},{3,7},... | collective-permute-start | bytes 2752520 | tf_op jit(solution)/shard_map/ppermute | solution.py:187
  5.0 1.5 %copy-start = (bf16[512,1792]{1,0:T(8,128)(2,1)S(1)}, bf16[512,1792]{1,0:T(8,128)(2,1)}, u32[]{:S(2)}) copy-start(bf16[512,1792]{1,0:T(8,128)(2,1)} %refs_1_.19) | copy-start | bytes 5505028
  6.5 0.7 %copy-start.4 = (s32[1,3]{1,0:T(1,128)S(1)}, s32[1,3]{1,0:T(1,128)}, u32[]{:S(2)}) copy-start(s32[1,3]{1,0:T(1,128)} %refs_0_.11) | copy-start | bytes 40
  7.1 2.5 %copy-start.1 = (bf16[512,1792]{1,0:T(8,128)(2,1)S(1)}, bf16[512,1792]{1,0:T(8,128)(2,1)}, u32[]{:S(2)}) copy-start(bf16[512,1792]{1,0:T(8,128)(2,1)} %refs_1_.19) | copy-start | bytes 5505028
  7.1 2.6 %copy-start.2 = (bf16[1,1024,1792]{2,1,0:T(8,128)(2,1)S(1)}, bf16[1,1024,1792]{2,1,0:T(8,128)(2,1)}, u32[]{:S(2)}) copy-start(bf16[1,1024,1792]{2,1,0:T(8,128)(2,1)} %refs_1_.17) | copy-start | bytes 11010052
  8.1 12.5 %collective-permute-start = (bf16[128,1792]{1,0:T(8,128)(2,1)S(1)}, bf16[128,1792]{1,0:T(8,128)(2,1)S(1)}, u32[]{:S(2)}, u32[]{:S(2)}) collective-permute-start(bf16[128,1792]{1,0:T(8,128)(2,1)S(1)} %pick_turned.1.refs_2_), channel_id=1, source_target_pairs={{0,2},{2,0},{4,6},{6,4},{8,10},{10,8},{12,14},{14,12},{1,3},{3,1},... | collective-permute-start | bytes 1376264 | tf_op jit(solution)/shard_map/ppermute | solution.py:187
  10.4 1.2 %copy-start.3 = (bf16[512,1024]{1,0:T(8,128)(2,1)S(1)}, bf16[512,1024]{1,0:T(8,128)(2,1)}, u32[]{:S(2)}) copy-start(bf16[512,1024]{1,0:T(8,128)(2,1)} %refs_1_.18) | copy-start | bytes 3145732
  10.4 4.8 %collective-permute-start.1 = (f32[256,512]{1,0:T(8,128)S(1)}, f32[256,512]{1,0:T(8,128)S(1)}, u32[]{:S(2)}, u32[]{:S(2)}) collective-permute-start(f32[256,512]{1,0:T(8,128)S(1)} %product_away.2.refs_2_), channel_id=1, source_target_pairs={{0,1},{1,0},{2,3},{3,2},{4,5},{5,4},{6,7},{7,6},{8,9},{9,8},{10,11... | collective-permute-start | bytes 1572872 | tf_op jit(solution)/shard_map/ppermute | solution.py:190
  13.6 25.6 %collective-permute-start.3 = (bf16[128,1792]{1,0:T(8,128)(2,1)S(1)}, bf16[128,1792]{1,0:T(8,128)(2,1)S(1)}, u32[]{:S(2)}, u32[]{:S(2)}) collective-permute-start(bf16[128,1792]{1,0:T(8,128)(2,1)S(1)} %pick_direct.1.refs_2_), channel_id=1, source_target_pairs={{0,2},{2,4},{4,6},{6,8},{8,10},{10,12},{12,14},{14,0},{1,3},{3,5},... | collective-permute-start | bytes 1376264 | tf_op jit(solution)/shard_map/ppermute | solution.py:187
  20.6 18.6 %collective-permute-start.2 = (bf16[128,1792]{1,0:T(8,128)(2,1)S(1)}, bf16[128,1792]{1,0:T(8,128)(2,1)S(1)}, u32[]{:S(2)}, u32[]{:S(2)}) collective-permute-start(bf16[128,1792]{1,0:T(8,128)(2,1)S(1)} %collective-permute-done.refs_2_.refs_0_), channel_id=1, source_target_pairs={{0,4},{4,8},{8,12},{12,0},{1,5},{5,9},{9,13},{13,1},{16,20},{20,24... | collective-permute-start | bytes 1376264 | tf_op jit(solution)/shard_map/ppermute | solution.py:187
  28.8 15.4 %collective-permute-start.9 = (f32[256,512]{1,0:T(8,128)S(1)}, f32[256,512]{1,0:T(8,128)S(1)}, u32[]{:S(2)}, u32[]{:S(2)}) collective-permute-start(f32[256,512]{1,0:T(8,128)S(1)} %product_away.3.refs_2_), channel_id=1, source_target_pairs={{0,1},{1,0},{2,3},{3,2},{4,5},{5,4},{6,7},{7,6},{8,9},{9,8},{10,11... | collective-permute-start | bytes 1572872 | tf_op jit(solution)/shard_map/ppermute | solution.py:190
  29.6 16.5 %collective-permute-start.7 = (bf16[512,256]{1,0:T(8,128)(2,1)S(1)}, bf16[512,256]{1,0:T(8,128)(2,1)S(1)}, u32[]{:S(2)}, u32[]{:S(2)}) collective-permute-start(bf16[512,256]{1,0:T(8,128)(2,1)S(1)} %get-tuple-element.26), channel_id=1, source_target_pairs={{0,2},{2,4},{4,6},{6,8},{8,10},{10,12},{12,14},{14,0},{1,3},{3,5},... | collective-permute-start | bytes 786440 | tf_op jit(solution)/shard_map/ppermute | solution.py:187
  31.4 14.7 %collective-permute-start.8 = (bf16[512,256]{1,0:T(8,128)(2,1)S(1)}, bf16[512,256]{1,0:T(8,128)(2,1)S(1)}, u32[]{:S(2)}, u32[]{:S(2)}) collective-permute-start(bf16[512,256]{1,0:T(8,128)(2,1)S(1)} %get-tuple-element.27.refs_2_), channel_id=1, source_target_pairs={{0,4},{2,6},{4,8},{6,10},{8,12},{10,14},{12,0},{14,2},{1,5},{3,7},... | collective-permute-start | bytes 786440 | tf_op jit(solution)/shard_map/ppermute | solution.py:187
  39.9 2.0 %collective-permute-start.5 = (f32[256,512]{1,0:T(8,128)S(1)}, f32[256,512]{1,0:T(8,128)S(1)}, u32[]{:S(2)}, u32[]{:S(2)}) collective-permute-start(f32[256,512]{1,0:T(8,128)S(1)} %get-tuple-element.23.refs_2_), channel_id=1, source_target_pairs={{0,1},{1,0},{2,3},{3,2},{4,5},{5,4},{6,7},{7,6},{8,9},{9,8},{10,11... | collective-permute-start | bytes 1572872 | tf_op jit(solution)/shard_map/ppermute | solution.py:190
  40.7 1.3 %copy-start.5 = (s32[1,3]{1,0:T(1,128)S(1)}, s32[1,3]{1,0:T(1,128)}, u32[]{:S(2)}) copy-start(s32[1,3]{1,0:T(1,128)} %refs_0_.11) | copy-start | bytes 40
  41.9 9.3 %collective-permute-start.6 = (bf16[256,512]{1,0:T(8,128)(2,1)S(1)}, bf16[256,512]{1,0:T(8,128)(2,1)S(1)}, u32[]{:S(2)}, u32[]{:S(2)}) collective-permute-start(bf16[256,512]{1,0:T(8,128)(2,1)S(1)} %add_halves.4.refs_2_), channel_id=1, source_target_pairs={{2,0},{4,2},{6,4},{8,6},{10,8},{12,10},{14,12},{0,14},{3,1},{5,3},... | collective-permute-start | bytes 786440 | tf_op jit(solution)/shard_map/ppermute | solution.py:187
  44.3 9.7 %collective-permute-start.12 = (bf16[256,512]{1,0:T(8,128)(2,1)S(1)}, bf16[256,512]{1,0:T(8,128)(2,1)S(1)}, u32[]{:S(2)}, u32[]{:S(2)}) collective-permute-start(bf16[256,512]{1,0:T(8,128)(2,1)S(1)} %add_halves.5), channel_id=1, source_target_pairs={{4,0},{6,2},{8,4},{10,6},{12,8},{14,10},{0,12},{2,14},{5,1},{7,3},... | collective-permute-start | bytes 786440 | tf_op jit(solution)/shard_map/ppermute | solution.py:187
  46.1 2.8 %collective-permute-start.10 = (bf16[512,256]{1,0:T(8,128)(2,1)S(1)}, bf16[512,256]{1,0:T(8,128)(2,1)S(1)}, u32[]{:S(2)}, u32[]{:S(2)}) collective-permute-start(bf16[512,256]{1,0:T(8,128)(2,1)S(1)} %collective-permute-done.8.far_hidden), channel_id=1, source_target_pairs={{0,1},{1,0},{2,3},{3,2},{4,5},{5,4},{6,7},{7,6},{8,9},{9,8},{10,11... | collective-permute-start | bytes 786440 | tf_op jit(solution)/shard_map/ppermute | solution.py:190
  46.1 2.8 %collective-permute-start.11 = (bf16[512,256]{1,0:T(8,128)(2,1)S(1)}, bf16[512,256]{1,0:T(8,128)(2,1)S(1)}, u32[]{:S(2)}, u32[]{:S(2)}) collective-permute-start(bf16[512,256]{1,0:T(8,128)(2,1)S(1)} %collective-permute-done.7.near_hidden), channel_id=1, source_target_pairs={{0,1},{1,0},{2,3},{3,2},{4,5},{5,4},{6,7},{7,6},{8,9},{9,8},{10,11... | collective-permute-start | bytes 786440 | tf_op jit(solution)/shard_map/ppermute | solution.py:190

commit v6 on v5

--- a/solution.py
+++ b/solution.py
@@ -92,13 +92,15 @@
         out[...] = dot(hidden[:, columns], picker(counts, index, rows), (0, 1)).astype(BF16)
 
 
-def pick_own(counts, hidden, own, places):
+def pick_own(counts, hidden, own, places, mask):
     rows, units = hidden.shape
     pick = picker(counts, 0, rows)
     for tile in tiles(units):
         own[tile, :] = dot(hidden[:, tile], pick, (0, 1)).astype(BF16)
-    for index in range(3):
+    for index in range(2):
         places[:, index * CAP : (index + 1) * CAP] = placer(counts, index, rows)
+    place = lax.broadcasted_iota(jnp.int32, mask.shape, 0)
+    mask[...] = (place >= CAP - counts[0, LAST]).astype(BF16)
 
 
 def product_away(grad, weights, away):
@@ -131,12 +133,23 @@
 
 
 def place_first(places, own, near, out):
-    total = dot(places[:, :CAP], own[...])
-    out[...] = (total + dot(places[:, CAP : 2 * CAP], near[...])).astype(BF16)
-
-
-def place_last(places, first, far, out):
-    out[...] = (first[...].astype(F32) + dot(places[:, 2 * CAP :], far[...])).astype(BF16)
+    out[...] = (dot(places[:, :CAP], own[...]) + dot(places[:, CAP:], near[...])).astype(BF16)
+
+
+def place_last(first, mask, early, late, out):
+    rows = first.shape[0]
+    group, size = lax.axis_index("grp"), lax.axis_size("grp")
+    step = pl.program_id(0)
+
+    @pl.when(step < rows // CAP - 1)
+    def _():
+        out[...] = first[half_of(step, CAP), :]
+
+    @pl.when(step == rows // CAP - 1)
+    def _():
+        far = jnp.where((group % 2 == 1) | (group == size - 2), late[...], early[...])
+        high = first[rows - CAP :, :].astype(F32)
+        out[...] = (high + far.astype(F32) * mask[...].astype(F32)).astype(BF16)
 
 
 def own_weights(own_hidden, own, total):
@@ -218,21 +231,23 @@
     near_hidden_in = send(near_hidden, by1)
     far_hidden_in = send(far_hidden, by2)
 
+    (far_block,) = call(add_halves, [block], far_here, far_other)
+    far_back_early = send(far_block, back2[:-2:2])
+    own_hidden, places, mask = call(
+        pick_own, [((units, CAP), BF16), ((rows, 2 * CAP), BF16), block], counts, hidden, scalars=1, after=(far_block,)
+    )
     near_in, near_away = call(
-        join_near, [((CAP, features), BF16), partial], turned_in, relayed_in, direct_in, weights, after=(far_here,)
+        join_near, [((CAP, features), BF16), partial], turned_in, relayed_in, direct_in, weights, after=(places,)
     )
     near_other = swap_cores(near_away)
     (near_here,) = call(product_here, [partial], near_in, weights, after=(near_away,))
     (near_block,) = call(add_halves, [block], near_here, near_other)
     near_back = send(near_block, back1)
-    own_hidden, places = call(
-        pick_own, [((units, CAP), BF16), ((rows, 3 * CAP), BF16)], counts, hidden, scalars=1, after=(near_block,)
-    )
-    (total,) = call(own_weights, [((units, features), F32)], own_hidden, grad_out)
-    (far_block,) = call(add_halves, [block], far_here, far_other, after=(total,))
-    far_back = send(far_block, back2)
-
-    near_hidden_in, far_hidden_in, far_block = lax.optimization_barrier((near_hidden_in, far_hidden_in, far_block))
+    (total,) = call(own_weights, [((units, features), F32)], own_hidden, grad_out, after=(near_block,))
+    (late_block,) = call(add_halves, [block], far_here, far_other, after=(total,))
+    far_back_late = send(late_block, back2[1::2] + back2[-2:-1])
+
+    near_hidden_in, far_hidden_in, late_block = lax.optimization_barrier((near_hidden_in, far_hidden_in, late_block))
     here, _ = rows_of_half(
         lambda: lax.axis_index("loc"), far_hidden_in, near_hidden_in, far_in, near_in, total, units=units, features=features
     )
@@ -240,8 +255,11 @@
         lambda: 1 - lax.axis_index("loc"), swap_cores(far_hidden_in), swap_cores(near_hidden_in), far_in, near_in, total,
         units=units, features=features, before=(here,),
     )
-    (placed,) = call(place_first, [((rows, half), BF16)], places, own_block, near_back, after=(done,))
-    (grad_hidden,) = call(place_last, [((rows, half), BF16)], places, placed, far_back)
+    (first,) = call(place_first, [((rows, half), BF16)], places, own_block, near_back, after=(done,))
+    (grad_hidden,) = call(
+        place_last, [((rows, half), BF16)], first, mask, far_back_early, far_back_late,
+        grid=(rows // CAP,), out_specs=[pl.BlockSpec((CAP, half), lambda step: (step, 0))],
+    )
     return grad_hidden, grad_weights
 
 

time: 55.4 us -> 54.9 us (level)
  waiting for transfers between devices: 20.8 us -> 17.3 us
  starting transfers between devices: 14.2 us -> 17.4 us
    ppermute x8 -> x9, waiting for transfers between devices: 19.6 us -> 16.1 us  [send(): return lax.ppermute(value, 'grp', pairs)]
    ppermute x8 -> x9, starting transfers between devices: 13.4 us -> 16.6 us  [send(): return lax.ppermute(value, 'grp', pairs)]
    pallas_call x16 -> x17, Pallas kernels: 10.8 us -> 10.7 us  [call(): pl.pallas_call(body, out_shape=[jax.ShapeDtypeStruct(shape, dtype) for sh...]
  transfers between devices with their start and end apart: 13 -> 14, of which waited for: 5 -> 5; matrix products, arithmetic and copies ran while one was open for 0% -> 0% of each run, Pallas kernels for 26% -> 26%
where the time goes in v6:
time: 54.9 us; the launch traced here: 54.6 us
  starting transfers between devices  17.4 us (32%)
  waiting for transfers between devices  17.3 us (32%)
  Pallas kernels  15.2 us (28%)
  local copies, waits for them, and re-layouts  3.91 us (7%)
  between operations  0.86 us (2%)
    ppermute x9, starting transfers between devices, send(): return lax.ppermute(value, 'grp', pairs)  16.6 us
    ppermute x9, waiting for transfers between devices, send(): return lax.ppermute(value, 'grp', pairs)  16.1 us
    pallas_call x17, Pallas kernels, call(): pl.pallas_call(body, out_shape=[jax.ShapeDtypeStruct(shape, dtype) for sh...  10.7 us
    pallas_call x2, Pallas kernels, rows_of_half(): pl.pallas_call(functools.partial(half_weights, side), out_shape=[jax.Shap...  4.48 us
    unnamed x12, local copies, waits for them, and re-layouts  2.67 us
    slice x1, local copies, waits for them, and re-layouts, local(): far = grad_out[rows - CAP:]  1.24 us
    ppermute x5, waiting for transfers between devices, swap_cores(): return lax.ppermute(value, 'loc', [(0, 1), (1, 0)])  1.23 us
  transfers between devices with their start and end apart: 14, of which 5 were waited for; matrix products, arithmetic and copies ran while one was open for 0% of the time, Pallas kernels for 26%

profile of v6, /device:TPU:0, one launch (start us, length us, event | category | flops | bytes accessed | tf_op | source)
XLA Modules:
  0.0 54.6 jit_solution(1348221774351514928)
XLA Ops:
  0.6 1.2 %slice.3.refs_2_ = bf16[256,1792]{1,0:T(8,128)(2,1)S(1)} slice(bf16[512,1792]{1,0:T(8,128)(2,1)} %refs_1_.19), slice={[256:512], [0:1792]} | slice | bytes 1835008 | tf_op jit(solution)/shard_map/slice | solution.py:207
  1.9 3.1 %collective-permute-start = (bf16[256,1792]{1,0:T(8,128)(2,1)S(1)}, bf16[256,1792]{1,0:T(8,128)(2,1)S(1)}, u32[]{:S(2)}, u32[]{:S(2)}) collective-permute-start(bf16[256,1792]{1,0:T(8,128)(2,1)S(1)} %slice.3.refs_2_), channel_id=1, source_target_pairs={{0,4},{2,6},{4,8},{6,10},{8,12},{10,14},{12,0},{14,2},{1,5},{3,7},... | collective-permute-start | bytes 2752520 | tf_op jit(solution)/shard_map/ppermute | solution.py:200
  5.0 1.5 %copy-done = bf16[512,1792]{1,0:T(8,128)(2,1)S(1)} copy-done((bf16[512,1792]{1,0:T(8,128)(2,1)S(1)}, bf16[512,1792]{1,0:T(8,128)(2,1)}, u32[]{:S(2)}) %copy-start) | copy-done | bytes 1835032
  6.5 0.7 %copy-done.4 = s32[1,3]{1,0:T(1,128)S(1)} copy-done((s32[1,3]{1,0:T(1,128)S(1)}, s32[1,3]{1,0:T(1,128)}, u32[]{:S(2)}) %copy-start.4) | copy-done | bytes 36
  7.1 0.9 %pick_turned.1.refs_2_ = bf16[128,1792]{1,0:T(8,128)(2,1)S(1)} custom-call(s32[1,3]{1,0:T(1,128)S(1)} %copy-done.4, bf16[512,1792]{1,0:T(8,128)(2,1)S(1)} %copy-done, bf16[256,1792]{1,0:T(8,128)(2,1)S(1)} %slice.3.refs_2_), custom_call_target="tpu_custom_call" | custom-call | flops 10000000000 | bytes 1000 | tf_op jit(solution)/shard_map/pick_turned/pallas_call | solution.py:26
  8.1 1.6 %collective-permute-start.1 = (bf16[128,1792]{1,0:T(8,128)(2,1)S(1)}, bf16[128,1792]{1,0:T(8,128)(2,1)S(1)}, u32[]{:S(2)}, u32[]{:S(2)}) collective-permute-start(bf16[128,1792]{1,0:T(8,128)(2,1)S(1)} %pick_turned.1.refs_2_), channel_id=1, source_target_pairs={{0,2},{2,0},{4,6},{6,4},{8,10},{10,8},{12,14},{14,12},{1,3},{3,1},... | collective-permute-start | bytes 1376264 | tf_op jit(solution)/shard_map/ppermute | solution.py:200
  9.7 0.0 copy-done.2
  9.7 0.7 %product_away.2.refs_2_ = f32[256,512]{1,0:T(8,128)S(1)} custom-call(bf16[512,1792]{1,0:T(8,128)(2,1)S(1)} %copy-done.1, bf16[1,1024,1792]{2,1,0:T(8,128)(2,1)S(1)} %copy-done.2, bf16[128,1792]{1,0:T(8,128)(2,1)S(1)} %pick_turned.1.refs_2_), custom_call_target="tpu_custom_call" | custom-call | flops 10000000000 | bytes 1000 | tf_op jit(solution)/shard_map/product_away/pallas_call | solution.py:26
  10.4 0.0 copy-start.3
  10.4 0.1 collective-permute-start.2
  10.5 0.7 %product_here.3.refs_2_.refs_0_ = f32[256,512]{1,0:T(8,128)S(1)} custom-call(bf16[512,1792]{1,0:T(8,128)(2,1)S(1)} %copy-done.1, bf16[1,1024,1792]{2,1,0:T(8,128)(2,1)S(1)} %copy-done.2, f32[256,512]{1,0:T(8,128)S(1)} %product_away.2.refs_2_), custom_call_target="tpu_custom_call" | custom-call | flops 10000000000 | bytes 1000 | tf_op jit(solution)/shard_map/product_here/pallas_call | solution.py:26
  11.1 0.5 copy-done.3
  11.6 1.0 %pick_hidden.1 = (bf16[512,256]{1,0:T(8,128)(2,1)S(1)}, bf16[512,256]{1,0:T(8,128)(2,1)S(1)}) custom-call(s32[1,3]{1,0:T(1,128)S(1)} %copy-done.4, bf16[512,1024]{1,0:T(8,128)(2,1)S(1)} %copy-done.3, f32[256,512]{1,0:T(8,128)S(1)} %product_here.3.refs_2_.refs_0_), custom_call_target="tpu_custom_call" | custom-call | flops 10000000000 | bytes 1000 | tf_op jit(solution)/shard_map/pick_hidden/pallas_call | solution.py:26
  12.6 0.9 %pick_direct.1.refs_2_ = bf16[128,1792]{1,0:T(8,128)(2,1)S(1)} custom-call(s32[1,3]{1,0:T(1,128)S(1)} %copy-done.4, bf16[512,1792]{1,0:T(8,128)(2,1)S(1)} %copy-done.1, bf16[512,256]{1,0:T(8,128)(2,1)S(1)} %get-tuple-element.28.refs_2_), custom_call_target="tpu_custom_call" | custom-call | flops 10000000000 | bytes 1000 | tf_op jit(solution)/shard_map/pick_direct/pallas_call | solution.py:26
  13.6 1.6 %collective-permute-start.5 = (bf16[128,1792]{1,0:T(8,128)(2,1)S(1)}, bf16[128,1792]{1,0:T(8,128)(2,1)S(1)}, u32[]{:S(2)}, u32[]{:S(2)}) collective-permute-start(bf16[128,1792]{1,0:T(8,128)(2,1)S(1)} %pick_direct.1.refs_2_), channel_id=1, source_target_pairs={{0,2},{2,4},{4,6},{6,8},{8,10},{10,12},{12,14},{14,0},{1,3},{3,5},... | collective-permute-start | bytes 1376264 | tf_op jit(solution)/shard_map/ppermute | solution.py:200
  15.2 0.0 collective-permute-done.2.refs_1_
  15.2 0.1 add_halves.4.refs_1_
  15.3 5.4 %collective-permute-done.1.refs_2_.refs_0_ = bf16[128,1792]{1,0:T(8,128)(2,1)S(1)} collective-permute-done((bf16[128,1792]{1,0:T(8,128)(2,1)S(1)}, bf16[128,1792]{1,0:T(8,128)(2,1)S(1)}, u32[]{:S(2)}, u32[]{:S(2)}) %collective-permute-start.1) | collective-permute-done | bytes 458784 | tf_op jit(solution)/shard_map/ppermute | solution.py:200
  20.6 3.5 %collective-permute-start.4 = (bf16[128,1792]{1,0:T(8,128)(2,1)S(1)}, bf16[128,1792]{1,0:T(8,128)(2,1)S(1)}, u32[]{:S(2)}, u32[]{:S(2)}) collective-permute-start(bf16[128,1792]{1,0:T(8,128)(2,1)S(1)} %collective-permute-done.1.refs_2_.refs_0_), channel_id=1, source_target_pairs={{0,4},{4,8},{8,12},{12,0},{1,5},{5,9},{9,13},{13,1},{16,20},{20,24... | collective-permute-start | bytes 1376264 | tf_op jit(solution)/shard_map/ppermute | solution.py:200
  24.1 4.1 %collective-permute-done.refs_0_.far = bf16[256,1792]{1,0:T(8,128)(2,1)S(1)} collective-permute-done((bf16[256,1792]{1,0:T(8,128)(2,1)S(1)}, bf16[256,1792]{1,0:T(8,128)(2,1)S(1)}, u32[]{:S(2)}, u32[]{:S(2)}) %collective-permute-start) | collective-permute-done | bytes 917536 | tf_op jit(solution)/shard_map/ppermute | solution.py:200
  28.2 0.7 %product_away.3.refs_2_ = f32[256,512]{1,0:T(8,128)S(1)} custom-call(bf16[256,1792]{1,0:T(8,128)(2,1)S(1)} %collective-permute-done.refs_0_.far, bf16[1,1024,1792]{2,1,0:T(8,128)(2,1)S(1)} %copy-done.2, bf16[128,1792]{1,0:T(8,128)(2,1)S(1)} %collective-permute-done.1.refs_2_.refs_0_), custom_call_target="tpu_custom_call" | custom-call | flops 10000000000 | bytes 1000 | tf_op jit(solution)/shard_map/product_away/pallas_call | solution.py:26
  28.8 0.1 collective-permute-start.3
  28.9 0.7 %product_here.4.refs_0_ = f32[256,512]{1,0:T(8,128)S(1)} custom-call(bf16[256,1792]{1,0:T(8,128)(2,1)S(1)} %collective-permute-done.refs_0_.far, bf16[1,1024,1792]{2,1,0:T(8,128)(2,1)S(1)} %copy-done.2, f32[256,512]{1,0:T(8,128)S(1)} %product_away.3.refs_2_), custom_call_target="tpu_custom_call" | custom-call | flops 10000000000 | bytes 1000 | tf_op jit(solution)/shard_map/product_here/pallas_call | solution.py:26
  29.6 0.0 copy-start.5
  29.6 1.8 %collective-permute-start.8 = (bf16[512,256]{1,0:T(8,128)(2,1)S(1)}, bf16[512,256]{1,0:T(8,128)(2,1)S(1)}, u32[]{:S(2)}, u32[]{:S(2)}) collective-permute-start(bf16[512,256]{1,0:T(8,128)(2,1)S(1)} %get-tuple-element.27), channel_id=1, source_target_pairs={{0,2},{2,4},{4,6},{6,8},{8,10},{10,12},{12,14},{14,0},{1,3},{3,5},... | collective-permute-start | bytes 786440 | tf_op jit(solution)/shard_map/ppermute | solution.py:200
  31.4 0.0 collective-permute-start.9
  31.4 0.0 collective-permute-done.3.refs_1_
  31.5 1.3 %collective-permute-start.12 = (bf16[256,512]{1,0:T(8,128)(2,1)S(1)}, bf16[256,512]{1,0:T(8,128)(2,1)S(1)}, u32[]{:S(2)}, u32[]{:S(2)}) collective-permute-start(bf16[256,512]{1,0:T(8,128)(2,1)S(1)} %add_halves.5.refs_2_), channel_id=1, source_target_pairs={{4,0},{8,4},{12,8},{5,1},{9,5},{13,9},{20,16},{24,20},{28,24},{21,... | collective-permute-start | bytes 786440 | tf_op jit(solution)/shard_map/ppermute | solution.py:200
  32.8 1.1 %pick_own.1 = (bf16[1024,256]{1,0:T(8,128)(2,1)S(1)}, bf16[512,512]{1,0:T(8,128)(2,1)S(1)}, bf16[256,512]{1,0:T(8,128)(2,1)S(1)}) custom-call(s32[1,3]{1,0:T(1,128)S(1)} %copy-done.5, bf16[512,1024]{1,0:T(8,128)(2,1)S(1)} %copy-done.3, bf16[256,512]{1,0:T(8,128)(2,1)S(1)} %add_halves.5.refs_2_), custom_call_target="tpu_custom_call" | custom-call | flops 10000000000 | bytes 1000 | tf_op jit(solution)/shard_map/pick_own/pallas_call | solution.py:26
  33.8 5.3 %collective-permute-done.5.refs_2_ = bf16[128,1792]{1,0:T(8,128)(2,1)S(1)} collective-permute-done((bf16[128,1792]{1,0:T(8,128)(2,1)S(1)}, bf16[128,1792]{1,0:T(8,128)(2,1)S(1)}, u32[]{:S(2)}, u32[]{:S(2)}) %collective-permute-start.5) | collective-permute-done | bytes 458784 | tf_op jit(solution)/shard_map/ppermute | solution.py:200
  39.2 0.0 collective-permute-done.4.refs_1_
  39.2 0.7 %join_near.1 = (bf16[256,1792]{1,0:T(8,128)(2,1)S(1)}, f32[256,512]{1,0:T(8,128)S(1)}) custom-call(bf16[128,1792]{1,0:T(8,128)(2,1)S(1)} %collective-permute-done.1.refs_2_.refs_0_, bf16[128,1792]{1,0:T(8,128)(2,1)S(1)} %collective-permute-done.4.refs_1_, bf16[128,1792]{1,0:T(8,128)(2,1)S(1)} %collective-permute-done.5.refs_2_, ...), custom_call_target="tpu_custom_call" | custom-call | flops 10000000000 | bytes 1000 | tf_op jit(solution)/shard_map/join_near/pallas_call | solution.py:26
  39.9 0.1 collective-permute-start.6
  40.0 0.7 %product_here.5.refs_0_ = f32[256,512]{1,0:T(8,128)S(1)} custom-call(bf16[256,1792]{1,0:T(8,128)(2,1)S(1)} %get-tuple-element.25.refs_0_.near, bf16[1,1024,1792]{2,1,0:T(8,128)(2,1)S(1)} %copy-done.2, f32[256,512]{1,0:T(8,128)S(1)} %get-tuple-element.26.refs_2_), custom_call_target="tpu_custom_call" | custom-call | flops 10000000000 | bytes 1000 | tf_op jit(solution)/shard_map/product_here/pallas_call | solution.py:26
  40.7 1.2 %collective-permute-done.6.refs_1_ = f32[256,512]{1,0:T(8,128)S(1)} collective-permute-done((f32[256,512]{1,0:T(8,128)S(1)}, f32[256,512]{1,0:T(8,128)S(1)}, u32[]{:S(2)}, u32[]{:S(2)}) %collective-permute-start.6) | collective-permute-done | bytes 524320 | tf_op jit(solution)/shard_map/ppermute | solution.py:203
  41.9 0.1 collective-permute-start.7
  42.0 1.1 %own_weights.1.refs_2_.before = f32[1024,1792]{1,0:T(8,128)S(1)} custom-call(bf16[1024,256]{1,0:T(8,128)(2,1)S(1)} %get-tuple-element.29.refs_0_, bf16[512,1792]{1,0:T(8,128)(2,1)S(1)} %copy-done.1, bf16[256,512]{1,0:T(8,128)(2,1)S(1)} %add_halves.6.refs_2_), custom_call_target="tpu_custom_call" | custom-call | flops 10000000000 | bytes 1000 | tf_op jit(solution)/shard_map/own_weights/pallas_call | solution.py:26
  43.1 0.1 add_halves.7
  43.2 3.7 %collective-permute-start.13 = (bf16[256,512]{1,0:T(8,128)(2,1)S(1)}, bf16[256,512]{1,0:T(8,128)(2,1)S(1)}, u32[]{:S(2)}, u32[]{:S(2)}) collective-permute-start(bf16[256,512]{1,0:T(8,128)(2,1)S(1)} %add_halves.7), channel_id=1, source_target_pairs={{6,2},{10,6},{14,10},{2,14},{0,12},{7,3},{11,7},{15,11},{3,15},{1,... | collective-permute-start | bytes 786440 | tf_op jit(solution)/shard_map/ppermute | solution.py:200
  46.9 0.0 collective-permute-done.9.far_hidden
  46.9 0.1 collective-permute-start.10
  47.0 0.5 collective-permute-start.11
  47.5 2.2 %half_weights.2 = (bf16[1,1024,1792]{2,1,0:T(8,128)(2,1)}, bf16[16,128]{1,0:T(8,128)(2,1)}) custom-call(bf16[512,256]{1,0:T(8,128)(2,1)S(1)} %collective-permute-done.9.far_hidden, bf16[512,256]{1,0:T(8,128)(2,1)S(1)} %collective-permute-done.8.near_hidden, bf16[256,1792]{1,0:T(8,128)(2,1)S(1)} %collective-permute-done.refs_0_.far, ...), custom_call_target="tpu_custom_call" | custom-call | flops 10000000000 | bytes 1000 | tf_op jit(solution)/shard_map/half_weights/pallas_call | solution.py:173
  49.8 2.2 %half_weights.3 = (bf16[1,1024,1792]{2,1,0:T(8,128)(2,1)}, bf16[16,128]{1,0:T(8,128)(2,1)S(1)}) custom-call(bf16[512,256]{1,0:T(8,128)(2,1)S(1)} %collective-permute-done.10.far_hidden, bf16[512,256]{1,0:T(8,128)(2,1)S(1)} %collective-permute-done.11.near_hidden, ...), custom_call_target="tpu_custom_call", output_to_operand_aliasing={{0}: (5, {})} | custom-call | flops 10000000000 | bytes 1000 | tf_op jit(solution)/shard_map/half_weights/pallas_call | solution.py:173
  52.0 0.4 place_first.1.refs_0_
  52.4 0.0 collective-permute-done.12.refs_2_
  52.5 1.3 %collective-permute-done.13.refs_3_ = bf16[256,512]{1,0:T(8,128)(2,1)S(1)} collective-permute-done((bf16[256,512]{1,0:T(8,128)(2,1)S(1)}, bf16[256,512]{1,0:T(8,128)(2,1)S(1)}, u32[]{:S(2)}, u32[]{:S(2)}) %collective-permute-start.13) | collective-permute-done | bytes 262176 | tf_op jit(solution)/shard_map/ppermute | solution.py:200
  53.7 0.9 %place_last.1 = bf16[512,512]{1,0:T(8,128)(2,1)} custom-call(bf16[512,512]{1,0:T(8,128)(2,1)S(1)} %place_first.1.refs_0_, bf16[256,512]{1,0:T(8,128)(2,1)S(1)} %get-tuple-element.34.refs_1_, bf16[256,512]{1,0:T(8,128)(2,1)S(1)} %collective-permute-done.12.refs_2_, bf16[256,512]{1,0:T(8,128)(2,1)S(1)} %collective-permute-done.13.refs_3_), custom_call_target="tpu_custom_call" | custom-call | flops 10000000000 | bytes 1000 | tf_op jit(solution)/shard_map/place_last/pallas_call | solution.py:26
  (12 shorter events, 0.1 us)
Async XLA Ops:
  1.9 26.3 %collective-permute-start = (bf16[256,1792]{1,0:T(8,128)(2,1)S(1)}, bf16[256,1792]{1,0:T(8,128)(2,1)S(1)}, u32[]{:S(2)}, u32[]{:S(2)}) collective-permute-start(bf16[256,1792]{1,0:T(8,128)(2,1)S(1)} %slice.3.refs_2_), channel_id=1, source_target_pairs={{0,4},{2,6},{4,8},{6,10},{8,12},{10,14},{12,0},{14,2},{1,5},{3,7},... | collective-permute-start | bytes 2752520 | tf_op jit(solution)/shard_map/ppermute | solution.py:200
  5.0 1.5 %copy-start = (bf16[512,1792]{1,0:T(8,128)(2,1)S(1)}, bf16[512,1792]{1,0:T(8,128)(2,1)}, u32[]{:S(2)}) copy-start(bf16[512,1792]{1,0:T(8,128)(2,1)} %refs_1_.19) | copy-start | bytes 5505028
  6.5 0.7 %copy-start.4 = (s32[1,3]{1,0:T(1,128)S(1)}, s32[1,3]{1,0:T(1,128)}, u32[]{:S(2)}) copy-start(s32[1,3]{1,0:T(1,128)} %refs_0_.11) | copy-start | bytes 40
  7.1 2.5 %copy-start.1 = (bf16[512,1792]{1,0:T(8,128)(2,1)S(1)}, bf16[512,1792]{1,0:T(8,128)(2,1)}, u32[]{:S(2)}) copy-start(bf16[512,1792]{1,0:T(8,128)(2,1)} %refs_1_.19) | copy-start | bytes 5505028
  7.1 2.6 %copy-start.2 = (bf16[1,1024,1792]{2,1,0:T(8,128)(2,1)S(1)}, bf16[1,1024,1792]{2,1,0:T(8,128)(2,1)}, u32[]{:S(2)}) copy-start(bf16[1,1024,1792]{2,1,0:T(8,128)(2,1)} %refs_1_.18) | copy-start | bytes 11010052
  8.1 12.5 %collective-permute-start.1 = (bf16[128,1792]{1,0:T(8,128)(2,1)S(1)}, bf16[128,1792]{1,0:T(8,128)(2,1)S(1)}, u32[]{:S(2)}, u32[]{:S(2)}) collective-permute-start(bf16[128,1792]{1,0:T(8,128)(2,1)S(1)} %pick_turned.1.refs_2_), channel_id=1, source_target_pairs={{0,2},{2,0},{4,6},{6,4},{8,10},{10,8},{12,14},{14,12},{1,3},{3,1},... | collective-permute-start | bytes 1376264 | tf_op jit(solution)/shard_map/ppermute | solution.py:200
  10.4 1.2 %copy-start.3 = (bf16[512,1024]{1,0:T(8,128)(2,1)S(1)}, bf16[512,1024]{1,0:T(8,128)(2,1)}, u32[]{:S(2)}) copy-start(bf16[512,1024]{1,0:T(8,128)(2,1)} %refs_1_.17) | copy-start | bytes 3145732
  10.4 4.8 %collective-permute-start.2 = (f32[256,512]{1,0:T(8,128)S(1)}, f32[256,512]{1,0:T(8,128)S(1)}, u32[]{:S(2)}, u32[]{:S(2)}) collective-permute-start(f32[256,512]{1,0:T(8,128)S(1)} %product_away.2.refs_2_), channel_id=1, source_target_pairs={{0,1},{1,0},{2,3},{3,2},{4,5},{5,4},{6,7},{7,6},{8,9},{9,8},{10,11... | collective-permute-start | bytes 1572872 | tf_op jit(solution)/shard_map/ppermute | solution.py:203
  13.6 25.6 %collective-permute-start.5 = (bf16[128,1792]{1,0:T(8,128)(2,1)S(1)}, bf16[128,1792]{1,0:T(8,128)(2,1)S(1)}, u32[]{:S(2)}, u32[]{:S(2)}) collective-permute-start(bf16[128,1792]{1,0:T(8,128)(2,1)S(1)} %pick_direct.1.refs_2_), channel_id=1, source_target_pairs={{0,2},{2,4},{4,6},{6,8},{8,10},{10,12},{12,14},{14,0},{1,3},{3,5},... | collective-permute-start | bytes 1376264 | tf_op jit(solution)/shard_map/ppermute | solution.py:200
  20.6 18.6 %collective-permute-start.4 = (bf16[128,1792]{1,0:T(8,128)(2,1)S(1)}, bf16[128,1792]{1,0:T(8,128)(2,1)S(1)}, u32[]{:S(2)}, u32[]{:S(2)}) collective-permute-start(bf16[128,1792]{1,0:T(8,128)(2,1)S(1)} %collective-permute-done.1.refs_2_.refs_0_), channel_id=1, source_target_pairs={{0,4},{4,8},{8,12},{12,0},{1,5},{5,9},{9,13},{13,1},{16,20},{20,24... | collective-permute-start | bytes 1376264 | tf_op jit(solution)/shard_map/ppermute | solution.py:200
  28.8 2.6 %collective-permute-start.3 = (f32[256,512]{1,0:T(8,128)S(1)}, f32[256,512]{1,0:T(8,128)S(1)}, u32[]{:S(2)}, u32[]{:S(2)}) collective-permute-start(f32[256,512]{1,0:T(8,128)S(1)} %product_away.3.refs_2_), channel_id=1, source_target_pairs={{0,1},{1,0},{2,3},{3,2},{4,5},{5,4},{6,7},{7,6},{8,9},{9,8},{10,11... | collective-permute-start | bytes 1572872 | tf_op jit(solution)/shard_map/ppermute | solution.py:203
  29.6 3.2 %copy-start.5 = (s32[1,3]{1,0:T(1,128)S(1)}, s32[1,3]{1,0:T(1,128)}, u32[]{:S(2)}) copy-start(s32[1,3]{1,0:T(1,128)} %refs_0_.11) | copy-start | bytes 40
  29.6 17.3 %collective-permute-start.8 = (bf16[512,256]{1,0:T(8,128)(2,1)S(1)}, bf16[512,256]{1,0:T(8,128)(2,1)S(1)}, u32[]{:S(2)}, u32[]{:S(2)}) collective-permute-start(bf16[512,256]{1,0:T(8,128)(2,1)S(1)} %get-tuple-element.27), channel_id=1, source_target_pairs={{0,2},{2,4},{4,6},{6,8},{8,10},{10,12},{12,14},{14,0},{1,3},{3,5},... | collective-permute-start | bytes 786440 | tf_op jit(solution)/shard_map/ppermute | solution.py:200
  31.4 15.5 %collective-permute-start.9 = (bf16[512,256]{1,0:T(8,128)(2,1)S(1)}, bf16[512,256]{1,0:T(8,128)(2,1)S(1)}, u32[]{:S(2)}, u32[]{:S(2)}) collective-permute-start(bf16[512,256]{1,0:T(8,128)(2,1)S(1)} %get-tuple-element.28.refs_2_), channel_id=1, source_target_pairs={{0,4},{2,6},{4,8},{6,10},{8,12},{10,14},{12,0},{14,2},{1,5},{3,7},... | collective-permute-start | bytes 786440 | tf_op jit(solution)/shard_map/ppermute | solution.py:200
  31.5 21.0 %collective-permute-start.12 = (bf16[256,512]{1,0:T(8,128)(2,1)S(1)}, bf16[256,512]{1,0:T(8,128)(2,1)S(1)}, u32[]{:S(2)}, u32[]{:S(2)}) collective-permute-start(bf16[256,512]{1,0:T(8,128)(2,1)S(1)} %add_halves.5.refs_2_), channel_id=1, source_target_pairs={{4,0},{8,4},{12,8},{5,1},{9,5},{13,9},{20,16},{24,20},{28,24},{21,... | collective-permute-start | bytes 786440 | tf_op jit(solution)/shard_map/ppermute | solution.py:200
  39.9 2.0 %collective-permute-start.6 = (f32[256,512]{1,0:T(8,128)S(1)}, f32[256,512]{1,0:T(8,128)S(1)}, u32[]{:S(2)}, u32[]{:S(2)}) collective-permute-start(f32[256,512]{1,0:T(8,128)S(1)} %get-tuple-element.26.refs_2_), channel_id=1, source_target_pairs={{0,1},{1,0},{2,3},{3,2},{4,5},{5,4},{6,7},{7,6},{8,9},{9,8},{10,11... | collective-permute-start | bytes 1572872 | tf_op jit(solution)/shard_map/ppermute | solution.py:203
  41.9 10.1 %collective-permute-start.7 = (bf16[256,512]{1,0:T(8,128)(2,1)S(1)}, bf16[256,512]{1,0:T(8,128)(2,1)S(1)}, u32[]{:S(2)}, u32[]{:S(2)}) collective-permute-start(bf16[256,512]{1,0:T(8,128)(2,1)S(1)} %add_halves.6.refs_2_), channel_id=1, source_target_pairs={{2,0},{4,2},{6,4},{8,6},{10,8},{12,10},{14,12},{0,14},{3,1},{5,3},... | collective-permute-start | bytes 786440 | tf_op jit(solution)/shard_map/ppermute | solution.py:200
  43.2 10.6 %collective-permute-start.13 = (bf16[256,512]{1,0:T(8,128)(2,1)S(1)}, bf16[256,512]{1,0:T(8,128)(2,1)S(1)}, u32[]{:S(2)}, u32[]{:S(2)}) collective-permute-start(bf16[256,512]{1,0:T(8,128)(2,1)S(1)} %add_halves.7), channel_id=1, source_target_pairs={{6,2},{10,6},{14,10},{2,14},{0,12},{7,3},{11,7},{15,11},{3,15},{1,... | collective-permute-start | bytes 786440 | tf_op jit(solution)/shard_map/ppermute | solution.py:200
  46.9 2.8 %collective-permute-start.10 = (bf16[512,256]{1,0:T(8,128)(2,1)S(1)}, bf16[512,256]{1,0:T(8,128)(2,1)S(1)}, u32[]{:S(2)}, u32[]{:S(2)}) collective-permute-start(bf16[512,256]{1,0:T(8,128)(2,1)S(1)} %collective-permute-done.9.far_hidden), channel_id=1, source_target_pairs={{0,1},{1,0},{2,3},{3,2},{4,5},{5,4},{6,7},{7,6},{8,9},{9,8},{10,11... | collective-permute-start | bytes 786440 | tf_op jit(solution)/shard_map/ppermute | solution.py:203
  47.0 2.7 %collective-permute-start.11 = (bf16[512,256]{1,0:T(8,128)(2,1)S(1)}, bf16[512,256]{1,0:T(8,128)(2,1)S(1)}, u32[]{:S(2)}, u32[]{:S(2)}) collective-permute-start(bf16[512,256]{1,0:T(8,128)(2,1)S(1)} %collective-permute-done.8.near_hidden), channel_id=1, source_target_pairs={{0,1},{1,0},{2,3},{3,2},{4,5},{5,4},{6,7},{7,6},{8,9},{9,8},{10,11... | collective-permute-start | bytes 786440 | tf_op jit(solution)/shard_map/ppermute | solution.py:203

commit v7 on v6

--- a/solution.py
+++ b/solution.py
@@ -9,6 +9,7 @@
 
 CAP = 256
 RELAYED = 128
+HEAD = 128
 LAST = 2
 TILE = 256
 BLOCK = 256
@@ -128,28 +129,41 @@
     product_away(near, weights, away)
 
 
+def take_rest(grad_out, rest):
+    rest[...] = grad_out[grad_out.shape[0] - rest.shape[0] :, :]
+
+
+def join_far(head, rest, weights, far, away):
+    far[: head.shape[0], :] = head[...]
+    far[head.shape[0] :, :] = rest[...]
+    product_away(far, weights, away)
+
+
 def add_halves(here, other, out):
     out[...] = (here[...] + other[...]).astype(BF16)
 
 
-def place_first(places, own, near, out):
-    out[...] = (dot(places[:, :CAP], own[...]) + dot(places[:, CAP:], near[...])).astype(BF16)
-
-
-def place_last(first, mask, early, late, out):
-    rows = first.shape[0]
+def late_results():
     group, size = lax.axis_index("grp"), lax.axis_size("grp")
-    step = pl.program_id(0)
-
-    @pl.when(step < rows // CAP - 1)
-    def _():
-        out[...] = first[half_of(step, CAP), :]
-
-    @pl.when(step == rows // CAP - 1)
-    def _():
-        far = jnp.where((group % 2 == 1) | (group == size - 2), late[...], early[...])
-        high = first[rows - CAP :, :].astype(F32)
-        out[...] = (high + far.astype(F32) * mask[...].astype(F32)).astype(BF16)
+    return (group % 2 == 1) | (group == size - 2)
+
+
+def place(first, far, mask, sums, out, copied):
+    low = first.shape[0] - CAP
+    sums[:low, :] = first[:low, :]
+    sums[low:, :] = (first[low:, :].astype(F32) + far[...].astype(F32) * mask[...].astype(F32)).astype(BF16)
+    copy = pltpu.make_async_copy(sums, out, copied)
+    copy.start()
+    copy.wait()
+
+
+def place_early(places, own, near, mask, far, done, out, first, sums, copied):
+    first[...] = (dot(places[:, :CAP], own[...]) + dot(places[:, CAP:], near[...])).astype(BF16)
+    pl.when(jnp.logical_not(late_results()))(lambda: place(first, far, mask, sums, out, copied))
+
+
+def place_late(first, mask, far, before, out, sums, copied):
+    pl.when(late_results())(lambda: place(first, far, mask, sums, out, copied))
 
 
 def own_weights(own_hidden, own, total):
@@ -204,12 +218,14 @@
 
     partial = ((CAP, half), F32)
     block = ((CAP, half), BF16)
-    far = grad_out[rows - CAP :]
-    far_in = send(far, by2)
-    (turned,) = call(pick_turned, [((RELAYED, features), BF16)], counts, grad_out, scalars=1, after=(far,))
+    head = grad_out[rows - CAP : rows - CAP + HEAD]
+    head_in = send(head, by2)
+    (turned,) = call(pick_turned, [((RELAYED, features), BF16)], counts, grad_out, scalars=1, after=(head,))
     turned_in = send(turned, turn)
-
-    (own_away,) = call(product_away, [partial], grad_out, weights, after=(turned,))
+    (rest,) = call(take_rest, [((CAP - HEAD, features), BF16)], grad_out, after=(turned,))
+    rest_in = send(rest, by2)
+
+    (own_away,) = call(product_away, [partial], grad_out, weights, after=(rest,))
     own_other = swap_cores(own_away)
     (own_here,) = call(product_here, [partial], grad_out, weights, after=(own_away,))
     far_hidden, near_hidden = call(
@@ -224,7 +240,9 @@
     turned_in, own_block = lax.optimization_barrier((turned_in, own_block))
     relayed_in = send(turned_in, even_by2)
 
-    (far_away,) = call(product_away, [partial], far_in, weights, after=(turned_in,))
+    far_in, far_away = call(
+        join_far, [((CAP, features), BF16), partial], head_in, rest_in, weights, after=(turned_in,)
+    )
     far_other = swap_cores(far_away)
     (far_here,) = call(product_here, [partial], far_in, weights, after=(far_away,))
     far_hidden, near_hidden, far_here = lax.optimization_barrier((far_hidden, near_hidden, far_here))
@@ -255,11 +273,19 @@
         lambda: 1 - lax.axis_index("loc"), swap_cores(far_hidden_in), swap_cores(near_hidden_in), far_in, near_in, total,
         units=units, features=features, before=(here,),
     )
-    (first,) = call(place_first, [((rows, half), BF16)], places, own_block, near_back, after=(done,))
-    (grad_hidden,) = call(
-        place_last, [((rows, half), BF16)], first, mask, far_back_early, far_back_late,
-        grid=(rows // CAP,), out_specs=[pl.BlockSpec((CAP, half), lambda step: (step, 0))],
-    )
+    whole = jax.ShapeDtypeStruct((rows, half), BF16)
+    common = {
+        "scratch_shapes": [pltpu.VMEM((rows, half), BF16), pltpu.SemaphoreType.DMA],
+        "cost_estimate": pl.CostEstimate(flops=10**10, bytes_accessed=10**3, transcendentals=0),
+        "compiler_params": pltpu.CompilerParams(vmem_limit_bytes=16 << 20),
+    }
+    placed, first = pl.pallas_call(
+        place_early, out_shape=[whole, whole], in_specs=[VMEM] * 5 + [ANY], out_specs=[ANY, VMEM], name="place_early", **common
+    )(places, own_block, near_back, mask, far_back_early, done)
+    grad_hidden = pl.pallas_call(
+        place_late, out_shape=whole, in_specs=[VMEM] * 3 + [ANY], out_specs=ANY, input_output_aliases={3: 0},
+        name="place_late", **common,
+    )(first, mask, far_back_late, placed)
     return grad_hidden, grad_weights
 
 

time: 54.9 us -> 54.2 us (0.987)
  waiting for transfers between devices: 17.3 us -> 15.8 us
  starting transfers between devices: 17.4 us -> 18 us
    ppermute x9 -> x10, waiting for transfers between devices: 16.1 us -> 14.6 us  [send(): return lax.ppermute(value, 'grp', pairs)]
    pallas_call x0 -> x2, Pallas kernels: none -> 1.34 us  [the longest x1 1.33 us: local(): pl.pallas_call(place_early, out_shape=[whole, whole], in_specs=[VMEM] * 5...]
    pallas_call x17 -> x16, Pallas kernels: 10.7 us -> 9.37 us  [call(): pl.pallas_call(body, out_shape=[jax.ShapeDtypeStruct(shape, dtype) for sh...]
    ppermute x9 -> x10, starting transfers between devices: 16.6 us -> 17.2 us  [send(): return lax.ppermute(value, 'grp', pairs)]
  transfers between devices with their start and end apart: 14 -> 15, of which waited for: 5 -> 5; matrix products, arithmetic and copies ran while one was open for 0% -> 0% of each run, Pallas kernels for 26% -> 28%
where the time goes in v7:
time: 54.2 us; the launch traced here: 53.6 us
  starting transfers between devices  18 us (33%)
  waiting for transfers between devices  15.8 us (29%)
  Pallas kernels  15.2 us (28%)
  local copies, waits for them, and re-layouts  3.68 us (7%)
  between operations  0.86 us (2%)
    ppermute x10, starting transfers between devices, send(): return lax.ppermute(value, 'grp', pairs)  17.2 us
    ppermute x10, waiting for transfers between devices, send(): return lax.ppermute(value, 'grp', pairs)  14.6 us
    pallas_call x16, Pallas kernels, call(): pl.pallas_call(body, out_shape=[jax.ShapeDtypeStruct(shape, dtype) for sh...  9.37 us
    pallas_call x2, Pallas kernels, rows_of_half(): pl.pallas_call(functools.partial(half_weights, side), out_shape=[jax.Shap...  4.49 us
    unnamed x12, local copies, waits for them, and re-layouts  2.63 us
    pallas_call x1, Pallas kernels, local(): pl.pallas_call(place_early, out_shape=[whole, whole], in_specs=[VMEM] * 5...  1.33 us
    ppermute x5, waiting for transfers between devices, swap_cores(): return lax.ppermute(value, 'loc', [(0, 1), (1, 0)])  1.23 us
  transfers between devices with their start and end apart: 15, of which 5 were waited for; matrix products, arithmetic and copies ran while one was open for 0% of the time, Pallas kernels for 28%

profile of v7, /device:TPU:0, one launch (start us, length us, event | category | flops | bytes accessed | tf_op | source)
XLA Modules:
  0.0 53.6 jit_solution(7248074478586214134)
XLA Ops:
  0.6 1.1 %slice.3.refs_2_ = bf16[128,1792]{1,0:T(8,128)(2,1)S(1)} slice(bf16[512,1792]{1,0:T(8,128)(2,1)} %refs_1_.17), slice={[256:384], [0:1792]} | slice | bytes 917504 | tf_op jit(solution)/shard_map/slice | solution.py:221
  1.7 3.1 %collective-permute-start = (bf16[128,1792]{1,0:T(8,128)(2,1)S(1)}, bf16[128,1792]{1,0:T(8,128)(2,1)S(1)}, u32[]{:S(2)}, u32[]{:S(2)}) collective-permute-start(bf16[128,1792]{1,0:T(8,128)(2,1)S(1)} %slice.3.refs_2_), channel_id=1, source_target_pairs={{0,4},{2,6},{4,8},{6,10},{8,12},{10,14},{12,0},{14,2},{1,5},{3,7},... | collective-permute-start | bytes 1376264 | tf_op jit(solution)/shard_map/ppermute | solution.py:214
  4.8 1.5 %copy-done = bf16[512,1792]{1,0:T(8,128)(2,1)S(1)} copy-done((bf16[512,1792]{1,0:T(8,128)(2,1)S(1)}, bf16[512,1792]{1,0:T(8,128)(2,1)}, u32[]{:S(2)}) %copy-start) | copy-done | bytes 1835032
  6.3 0.7 %copy-done.4 = s32[1,3]{1,0:T(1,128)S(1)} copy-done((s32[1,3]{1,0:T(1,128)S(1)}, s32[1,3]{1,0:T(1,128)}, u32[]{:S(2)}) %copy-start.4) | copy-done | bytes 36
  6.9 0.9 %pick_turned.1.refs_1_ = bf16[128,1792]{1,0:T(8,128)(2,1)S(1)} custom-call(s32[1,3]{1,0:T(1,128)S(1)} %copy-done.4, bf16[512,1792]{1,0:T(8,128)(2,1)S(1)} %copy-done, bf16[128,1792]{1,0:T(8,128)(2,1)S(1)} %slice.3.refs_2_), custom_call_target="tpu_custom_call" | custom-call | flops 10000000000 | bytes 1000 | tf_op jit(solution)/shard_map/pick_turned/pallas_call | solution.py:27
  7.9 0.0 copy-start.2
  7.9 1.6 %collective-permute-start.2 = (bf16[128,1792]{1,0:T(8,128)(2,1)S(1)}, bf16[128,1792]{1,0:T(8,128)(2,1)S(1)}, u32[]{:S(2)}, u32[]{:S(2)}) collective-permute-start(bf16[128,1792]{1,0:T(8,128)(2,1)S(1)} %pick_turned.1.refs_1_), channel_id=1, source_target_pairs={{0,2},{2,0},{4,6},{6,4},{8,10},{10,8},{12,14},{14,12},{1,3},{3,1},... | collective-permute-start | bytes 1376264 | tf_op jit(solution)/shard_map/ppermute | solution.py:214
  9.5 1.6 %collective-permute-start.1 = (bf16[128,1792]{1,0:T(8,128)(2,1)S(1)}, bf16[128,1792]{1,0:T(8,128)(2,1)S(1)}, u32[]{:S(2)}, u32[]{:S(2)}) collective-permute-start(bf16[128,1792]{1,0:T(8,128)(2,1)S(1)} %take_rest.1.refs_2_), channel_id=1, source_target_pairs={{0,4},{2,6},{4,8},{6,10},{8,12},{10,14},{12,0},{14,2},{1,5},{3,7},... | collective-permute-start | bytes 1376264 | tf_op jit(solution)/shard_map/ppermute | solution.py:214
  11.1 0.7 %product_away.1.refs_2_ = f32[256,512]{1,0:T(8,128)S(1)} custom-call(bf16[512,1792]{1,0:T(8,128)(2,1)S(1)} %copy-done.1, bf16[1,1024,1792]{2,1,0:T(8,128)(2,1)S(1)} %copy-done.2, bf16[128,1792]{1,0:T(8,128)(2,1)S(1)} %take_rest.1.refs_2_), custom_call_target="tpu_custom_call" | custom-call | flops 10000000000 | bytes 1000 | tf_op jit(solution)/shard_map/product_away/pallas_call | solution.py:27
  11.8 0.0 copy-start.3
  11.8 0.1 collective-permute-start.3
  11.9 0.7 %product_here.3.refs_2_.refs_0_ = f32[256,512]{1,0:T(8,128)S(1)} custom-call(bf16[512,1792]{1,0:T(8,128)(2,1)S(1)} %copy-done.1, bf16[1,1024,1792]{2,1,0:T(8,128)(2,1)S(1)} %copy-done.2, f32[256,512]{1,0:T(8,128)S(1)} %product_away.1.refs_2_), custom_call_target="tpu_custom_call" | custom-call | flops 10000000000 | bytes 1000 | tf_op jit(solution)/shard_map/product_here/pallas_call | solution.py:27
  12.6 0.5 copy-done.3
  13.0 1.0 %pick_hidden.1 = (bf16[512,256]{1,0:T(8,128)(2,1)S(1)}, bf16[512,256]{1,0:T(8,128)(2,1)S(1)}) custom-call(s32[1,3]{1,0:T(1,128)S(1)} %copy-done.4, bf16[512,1024]{1,0:T(8,128)(2,1)S(1)} %copy-done.3, f32[256,512]{1,0:T(8,128)S(1)} %product_here.3.refs_2_.refs_0_), custom_call_target="tpu_custom_call" | custom-call | flops 10000000000 | bytes 1000 | tf_op jit(solution)/shard_map/pick_hidden/pallas_call | solution.py:27
  14.1 1.0 %pick_direct.1.refs_2_ = bf16[128,1792]{1,0:T(8,128)(2,1)S(1)} custom-call(s32[1,3]{1,0:T(1,128)S(1)} %copy-done.4, bf16[512,1792]{1,0:T(8,128)(2,1)S(1)} %copy-done.1, bf16[512,256]{1,0:T(8,128)(2,1)S(1)} %get-tuple-element.35.refs_2_), custom_call_target="tpu_custom_call" | custom-call | flops 10000000000 | bytes 1000 | tf_op jit(solution)/shard_map/pick_direct/pallas_call | solution.py:27
  15.0 0.6 %collective-permute-start.6 = (bf16[128,1792]{1,0:T(8,128)(2,1)S(1)}, bf16[128,1792]{1,0:T(8,128)(2,1)S(1)}, u32[]{:S(2)}, u32[]{:S(2)}) collective-permute-start(bf16[128,1792]{1,0:T(8,128)(2,1)S(1)} %pick_direct.1.refs_2_), channel_id=1, source_target_pairs={{0,2},{2,4},{4,6},{6,8},{8,10},{10,12},{12,14},{14,0},{1,3},{3,5},... | collective-permute-start | bytes 1376264 | tf_op jit(solution)/shard_map/ppermute | solution.py:214
  15.6 0.0 collective-permute-done.3.refs_1_
  15.6 4.8 %collective-permute-done.2.refs_3_.refs_0_ = bf16[128,1792]{1,0:T(8,128)(2,1)S(1)} collective-permute-done((bf16[128,1792]{1,0:T(8,128)(2,1)S(1)}, bf16[128,1792]{1,0:T(8,128)(2,1)S(1)}, u32[]{:S(2)}, u32[]{:S(2)}) %collective-permute-start.2) | collective-permute-done | bytes 458784 | tf_op jit(solution)/shard_map/ppermute | solution.py:214
  20.4 3.5 %collective-permute-start.5 = (bf16[128,1792]{1,0:T(8,128)(2,1)S(1)}, bf16[128,1792]{1,0:T(8,128)(2,1)S(1)}, u32[]{:S(2)}, u32[]{:S(2)}) collective-permute-start(bf16[128,1792]{1,0:T(8,128)(2,1)S(1)} %collective-permute-done.2.refs_3_.refs_0_), channel_id=1, source_target_pairs={{0,4},{4,8},{8,12},{12,0},{1,5},{5,9},{9,13},{13,1},{16,20},{20,24... | collective-permute-start | bytes 1376264 | tf_op jit(solution)/shard_map/ppermute | solution.py:214
  23.9 4.0 %collective-permute-done.1.refs_1_ = bf16[128,1792]{1,0:T(8,128)(2,1)S(1)} collective-permute-done((bf16[128,1792]{1,0:T(8,128)(2,1)S(1)}, bf16[128,1792]{1,0:T(8,128)(2,1)S(1)}, u32[]{:S(2)}, u32[]{:S(2)}) %collective-permute-start.1) | collective-permute-done | bytes 458784 | tf_op jit(solution)/shard_map/ppermute | solution.py:214
  28.0 0.0 collective-permute-done.refs_0_
  28.0 0.7 %join_far.1 = (bf16[256,1792]{1,0:T(8,128)(2,1)S(1)}, f32[256,512]{1,0:T(8,128)S(1)}) custom-call(bf16[128,1792]{1,0:T(8,128)(2,1)S(1)} %collective-permute-done.refs_0_, bf16[128,1792]{1,0:T(8,128)(2,1)S(1)} %collective-permute-done.1.refs_1_, bf16[1,1024,1792]{2,1,0:T(8,128)(2,1)S(1)} %copy-done.2, bf16[128,1792]{1,0:T(8,128)(2,1)S(1)} %collective-permute-done.2.refs_3_.refs_0_), custom_call_target="tpu_custom_call" | custom-call | flops 10000000000 | bytes 1000 | tf_op jit(solution)/shard_map/join_far/pallas_call | solution.py:27
  28.6 0.1 collective-permute-start.4
  28.7 0.7 %product_here.4.refs_0_ = f32[256,512]{1,0:T(8,128)S(1)} custom-call(bf16[256,1792]{1,0:T(8,128)(2,1)S(1)} %get-tuple-element.26.refs_0_.far, bf16[1,1024,1792]{2,1,0:T(8,128)(2,1)S(1)} %copy-done.2, f32[256,512]{1,0:T(8,128)S(1)} %get-tuple-element.27.refs_2_), custom_call_target="tpu_custom_call" | custom-call | flops 10000000000 | bytes 1000 | tf_op jit(solution)/shard_map/product_here/pallas_call | solution.py:27
  29.4 0.0 copy-start.5
  29.4 1.8 %collective-permute-start.10 = (bf16[512,256]{1,0:T(8,128)(2,1)S(1)}, bf16[512,256]{1,0:T(8,128)(2,1)S(1)}, u32[]{:S(2)}, u32[]{:S(2)}) collective-permute-start(bf16[512,256]{1,0:T(8,128)(2,1)S(1)} %get-tuple-element.34), channel_id=1, source_target_pairs={{0,2},{2,4},{4,6},{6,8},{8,10},{10,12},{12,14},{14,0},{1,3},{3,5},... | collective-permute-start | bytes 786440 | tf_op jit(solution)/shard_map/ppermute | solution.py:214
  31.2 0.0 collective-permute-start.11
  31.2 0.0 collective-permute-done.4.refs_1_
  31.3 1.3 %collective-permute-start.9 = (bf16[256,512]{1,0:T(8,128)(2,1)S(1)}, bf16[256,512]{1,0:T(8,128)(2,1)S(1)}, u32[]{:S(2)}, u32[]{:S(2)}) collective-permute-start(bf16[256,512]{1,0:T(8,128)(2,1)S(1)} %add_halves.5.refs_2_), channel_id=1, source_target_pairs={{4,0},{8,4},{12,8},{5,1},{9,5},{13,9},{20,16},{24,20},{28,24},{21,... | collective-permute-start | bytes 786440 | tf_op jit(solution)/shard_map/ppermute | solution.py:214
  32.6 1.0 %pick_own.1 = (bf16[1024,256]{1,0:T(8,128)(2,1)S(1)}, bf16[512,512]{1,0:T(8,128)(2,1)S(1)}, bf16[256,512]{1,0:T(8,128)(2,1)S(1)}) custom-call(s32[1,3]{1,0:T(1,128)S(1)} %copy-done.5, bf16[512,1024]{1,0:T(8,128)(2,1)S(1)} %copy-done.3, bf16[256,512]{1,0:T(8,128)(2,1)S(1)} %add_halves.5.refs_2_), custom_call_target="tpu_custom_call" | custom-call | flops 10000000000 | bytes 1000 | tf_op jit(solution)/shard_map/pick_own/pallas_call | solution.py:27
  33.7 5.3 %collective-permute-done.6.refs_2_ = bf16[128,1792]{1,0:T(8,128)(2,1)S(1)} collective-permute-done((bf16[128,1792]{1,0:T(8,128)(2,1)S(1)}, bf16[128,1792]{1,0:T(8,128)(2,1)S(1)}, u32[]{:S(2)}, u32[]{:S(2)}) %collective-permute-start.6) | collective-permute-done | bytes 458784 | tf_op jit(solution)/shard_map/ppermute | solution.py:214
  39.0 0.7 %join_near.1 = (bf16[256,1792]{1,0:T(8,128)(2,1)S(1)}, f32[256,512]{1,0:T(8,128)S(1)}) custom-call(bf16[128,1792]{1,0:T(8,128)(2,1)S(1)} %collective-permute-done.2.refs_3_.refs_0_, bf16[128,1792]{1,0:T(8,128)(2,1)S(1)} %collective-permute-done.5.refs_1_, bf16[128,1792]{1,0:T(8,128)(2,1)S(1)} %collective-permute-done.6.refs_2_, ...), custom_call_target="tpu_custom_call" | custom-call | flops 10000000000 | bytes 1000 | tf_op jit(solution)/shard_map/join_near/pallas_call | solution.py:27
  39.7 0.1 collective-permute-start.7
  39.8 0.7 %product_here.5.refs_0_ = f32[256,512]{1,0:T(8,128)S(1)} custom-call(bf16[256,1792]{1,0:T(8,128)(2,1)S(1)} %get-tuple-element.31.refs_0_.near, bf16[1,1024,1792]{2,1,0:T(8,128)(2,1)S(1)} %copy-done.2, f32[256,512]{1,0:T(8,128)S(1)} %get-tuple-element.32.refs_2_), custom_call_target="tpu_custom_call" | custom-call | flops 10000000000 | bytes 1000 | tf_op jit(solution)/shard_map/product_here/pallas_call | solution.py:27
  40.5 1.2 %collective-permute-done.7.refs_1_ = f32[256,512]{1,0:T(8,128)S(1)} collective-permute-done((f32[256,512]{1,0:T(8,128)S(1)}, f32[256,512]{1,0:T(8,128)S(1)}, u32[]{:S(2)}, u32[]{:S(2)}) %collective-permute-start.7) | collective-permute-done | bytes 524320 | tf_op jit(solution)/shard_map/ppermute | solution.py:217
  41.7 0.1 collective-permute-start.8
  41.8 1.1 %own_weights.1.refs_2_.before = f32[1024,1792]{1,0:T(8,128)S(1)} custom-call(bf16[1024,256]{1,0:T(8,128)(2,1)S(1)} %get-tuple-element.36.refs_0_, bf16[512,1792]{1,0:T(8,128)(2,1)S(1)} %copy-done.1, bf16[256,512]{1,0:T(8,128)(2,1)S(1)} %add_halves.6.refs_2_), custom_call_target="tpu_custom_call" | custom-call | flops 10000000000 | bytes 1000 | tf_op jit(solution)/shard_map/own_weights/pallas_call | solution.py:27
  42.9 0.1 add_halves.7
  43.0 3.7 %collective-permute-start.14 = (bf16[256,512]{1,0:T(8,128)(2,1)S(1)}, bf16[256,512]{1,0:T(8,128)(2,1)S(1)}, u32[]{:S(2)}, u32[]{:S(2)}) collective-permute-start(bf16[256,512]{1,0:T(8,128)(2,1)S(1)} %add_halves.7), channel_id=1, source_target_pairs={{6,2},{10,6},{14,10},{2,14},{0,12},{7,3},{11,7},{15,11},{3,15},{1,... | collective-permute-start | bytes 786440 | tf_op jit(solution)/shard_map/ppermute | solution.py:214
  46.7 0.0 collective-permute-done.10.near_hidden
  46.7 0.1 collective-permute-start.12
  46.8 0.5 collective-permute-start.13
  47.3 2.2 %half_weights.2 = (bf16[1,1024,1792]{2,1,0:T(8,128)(2,1)}, bf16[16,128]{1,0:T(8,128)(2,1)}) custom-call(bf16[512,256]{1,0:T(8,128)(2,1)S(1)} %collective-permute-done.11.far_hidden, bf16[512,256]{1,0:T(8,128)(2,1)S(1)} %collective-permute-done.10.near_hidden, bf16[256,1792]{1,0:T(8,128)(2,1)S(1)} %get-tuple-element.26.refs_0_.far, ...), custom_call_target="tpu_custom_call" | custom-call | flops 10000000000 | bytes 1000 | tf_op jit(solution)/shard_map/half_weights/pallas_call | solution.py:187
  49.6 0.0 collective-permute-done.12.far_hidden
  49.6 0.0 collective-permute-done.13.near_hidden
  49.6 2.3 %half_weights.3 = (bf16[1,1024,1792]{2,1,0:T(8,128)(2,1)}, bf16[16,128]{1,0:T(8,128)(2,1)S(1)}) custom-call(bf16[512,256]{1,0:T(8,128)(2,1)S(1)} %collective-permute-done.12.far_hidden, bf16[512,256]{1,0:T(8,128)(2,1)S(1)} %collective-permute-done.13.near_hidden, ...), custom_call_target="tpu_custom_call", output_to_operand_aliasing={{0}: (5, {})} | custom-call | flops 10000000000 | bytes 1000 | tf_op jit(solution)/shard_map/half_weights/pallas_call | solution.py:187
  51.8 1.3 %place_early.1 = (bf16[512,512]{1,0:T(8,128)(2,1)}, bf16[512,512]{1,0:T(8,128)(2,1)S(1)}) custom-call(bf16[512,512]{1,0:T(8,128)(2,1)S(1)} %get-tuple-element.29.refs_4_.places, bf16[256,512]{1,0:T(8,128)(2,1)S(1)} %add_halves.4.own, bf16[256,512]{1,0:T(8,128)(2,1)S(1)} %collective-permute-done.8.near, bf16[256,512]{1,0:T(8,128)(2,1)S(1)} %get-tuple-element.33.mask, ...), custom_call_target="tpu_custom_call" | custom-call | flops 10000000000 | bytes 1000 | tf_op jit(solution)/shard_map/place_early/pallas_call | solution.py:282
  53.2 0.4 collective-permute-done.14.far
  (15 shorter events, 0.2 us)
Async XLA Ops:
  1.7 26.3 %collective-permute-start = (bf16[128,1792]{1,0:T(8,128)(2,1)S(1)}, bf16[128,1792]{1,0:T(8,128)(2,1)S(1)}, u32[]{:S(2)}, u32[]{:S(2)}) collective-permute-start(bf16[128,1792]{1,0:T(8,128)(2,1)S(1)} %slice.3.refs_2_), channel_id=1, source_target_pairs={{0,4},{2,6},{4,8},{6,10},{8,12},{10,14},{12,0},{14,2},{1,5},{3,7},... | collective-permute-start | bytes 1376264 | tf_op jit(solution)/shard_map/ppermute | solution.py:214
  4.8 1.5 %copy-start = (bf16[512,1792]{1,0:T(8,128)(2,1)S(1)}, bf16[512,1792]{1,0:T(8,128)(2,1)}, u32[]{:S(2)}) copy-start(bf16[512,1792]{1,0:T(8,128)(2,1)} %refs_1_.17) | copy-start | bytes 5505028
  6.3 0.7 %copy-start.4 = (s32[1,3]{1,0:T(1,128)S(1)}, s32[1,3]{1,0:T(1,128)}, u32[]{:S(2)}) copy-start(s32[1,3]{1,0:T(1,128)} %refs_0_.13) | copy-start | bytes 40
  6.9 2.6 %copy-start.1 = (bf16[512,1792]{1,0:T(8,128)(2,1)S(1)}, bf16[512,1792]{1,0:T(8,128)(2,1)}, u32[]{:S(2)}) copy-start(bf16[512,1792]{1,0:T(8,128)(2,1)} %refs_1_.17) | copy-start | bytes 5505028
  7.9 3.3 %copy-start.2 = (bf16[1,1024,1792]{2,1,0:T(8,128)(2,1)S(1)}, bf16[1,1024,1792]{2,1,0:T(8,128)(2,1)}, u32[]{:S(2)}) copy-start(bf16[1,1024,1792]{2,1,0:T(8,128)(2,1)} %refs_1_.16) | copy-start | bytes 11010052
  7.9 12.5 %collective-permute-start.2 = (bf16[128,1792]{1,0:T(8,128)(2,1)S(1)}, bf16[128,1792]{1,0:T(8,128)(2,1)S(1)}, u32[]{:S(2)}, u32[]{:S(2)}) collective-permute-start(bf16[128,1792]{1,0:T(8,128)(2,1)S(1)} %pick_turned.1.refs_1_), channel_id=1, source_target_pairs={{0,2},{2,0},{4,6},{6,4},{8,10},{10,8},{12,14},{14,12},{1,3},{3,1},... | collective-permute-start | bytes 1376264 | tf_op jit(solution)/shard_map/ppermute | solution.py:214
  9.5 18.5 %collective-permute-start.1 = (bf16[128,1792]{1,0:T(8,128)(2,1)S(1)}, bf16[128,1792]{1,0:T(8,128)(2,1)S(1)}, u32[]{:S(2)}, u32[]{:S(2)}) collective-permute-start(bf16[128,1792]{1,0:T(8,128)(2,1)S(1)} %take_rest.1.refs_2_), channel_id=1, source_target_pairs={{0,4},{2,6},{4,8},{6,10},{8,12},{10,14},{12,0},{14,2},{1,5},{3,7},... | collective-permute-start | bytes 1376264 | tf_op jit(solution)/shard_map/ppermute | solution.py:214
  11.8 1.2 %copy-start.3 = (bf16[512,1024]{1,0:T(8,128)(2,1)S(1)}, bf16[512,1024]{1,0:T(8,128)(2,1)}, u32[]{:S(2)}) copy-start(bf16[512,1024]{1,0:T(8,128)(2,1)} %refs_1_.15) | copy-start | bytes 3145732
  11.8 3.8 %collective-permute-start.3 = (f32[256,512]{1,0:T(8,128)S(1)}, f32[256,512]{1,0:T(8,128)S(1)}, u32[]{:S(2)}, u32[]{:S(2)}) collective-permute-start(f32[256,512]{1,0:T(8,128)S(1)} %product_away.1.refs_2_), channel_id=1, source_target_pairs={{0,1},{1,0},{2,3},{3,2},{4,5},{5,4},{6,7},{7,6},{8,9},{9,8},{10,11... | collective-permute-start | bytes 1572872 | tf_op jit(solution)/shard_map/ppermute | solution.py:217
  15.0 24.0 %collective-permute-start.6 = (bf16[128,1792]{1,0:T(8,128)(2,1)S(1)}, bf16[128,1792]{1,0:T(8,128)(2,1)S(1)}, u32[]{:S(2)}, u32[]{:S(2)}) collective-permute-start(bf16[128,1792]{1,0:T(8,128)(2,1)S(1)} %pick_direct.1.refs_2_), channel_id=1, source_target_pairs={{0,2},{2,4},{4,6},{6,8},{8,10},{10,12},{12,14},{14,0},{1,3},{3,5},... | collective-permute-start | bytes 1376264 | tf_op jit(solution)/shard_map/ppermute | solution.py:214
  20.4 18.6 %collective-permute-start.5 = (bf16[128,1792]{1,0:T(8,128)(2,1)S(1)}, bf16[128,1792]{1,0:T(8,128)(2,1)S(1)}, u32[]{:S(2)}, u32[]{:S(2)}) collective-permute-start(bf16[128,1792]{1,0:T(8,128)(2,1)S(1)} %collective-permute-done.2.refs_3_.refs_0_), channel_id=1, source_target_pairs={{0,4},{4,8},{8,12},{12,0},{1,5},{5,9},{9,13},{13,1},{16,20},{20,24... | collective-permute-start | bytes 1376264 | tf_op jit(solution)/shard_map/ppermute | solution.py:214
  28.6 2.6 %collective-permute-start.4 = (f32[256,512]{1,0:T(8,128)S(1)}, f32[256,512]{1,0:T(8,128)S(1)}, u32[]{:S(2)}, u32[]{:S(2)}) collective-permute-start(f32[256,512]{1,0:T(8,128)S(1)} %get-tuple-element.27.refs_2_), channel_id=1, source_target_pairs={{0,1},{1,0},{2,3},{3,2},{4,5},{5,4},{6,7},{7,6},{8,9},{9,8},{10,11... | collective-permute-start | bytes 1572872 | tf_op jit(solution)/shard_map/ppermute | solution.py:217
  29.4 3.2 %copy-start.5 = (s32[1,3]{1,0:T(1,128)S(1)}, s32[1,3]{1,0:T(1,128)}, u32[]{:S(2)}) copy-start(s32[1,3]{1,0:T(1,128)} %refs_0_.13) | copy-start | bytes 40
  29.4 17.3 %collective-permute-start.10 = (bf16[512,256]{1,0:T(8,128)(2,1)S(1)}, bf16[512,256]{1,0:T(8,128)(2,1)S(1)}, u32[]{:S(2)}, u32[]{:S(2)}) collective-permute-start(bf16[512,256]{1,0:T(8,128)(2,1)S(1)} %get-tuple-element.34), channel_id=1, source_target_pairs={{0,2},{2,4},{4,6},{6,8},{8,10},{10,12},{12,14},{14,0},{1,3},{3,5},... | collective-permute-start | bytes 786440 | tf_op jit(solution)/shard_map/ppermute | solution.py:214
  31.2 15.5 %collective-permute-start.11 = (bf16[512,256]{1,0:T(8,128)(2,1)S(1)}, bf16[512,256]{1,0:T(8,128)(2,1)S(1)}, u32[]{:S(2)}, u32[]{:S(2)}) collective-permute-start(bf16[512,256]{1,0:T(8,128)(2,1)S(1)} %get-tuple-element.35.refs_2_), channel_id=1, source_target_pairs={{0,4},{2,6},{4,8},{6,10},{8,12},{10,14},{12,0},{14,2},{1,5},{3,7},... | collective-permute-start | bytes 786440 | tf_op jit(solution)/shard_map/ppermute | solution.py:214
  31.3 20.5 %collective-permute-start.9 = (bf16[256,512]{1,0:T(8,128)(2,1)S(1)}, bf16[256,512]{1,0:T(8,128)(2,1)S(1)}, u32[]{:S(2)}, u32[]{:S(2)}) collective-permute-start(bf16[256,512]{1,0:T(8,128)(2,1)S(1)} %add_halves.5.refs_2_), channel_id=1, source_target_pairs={{4,0},{8,4},{12,8},{5,1},{9,5},{13,9},{20,16},{24,20},{28,24},{21,... | collective-permute-start | bytes 786440 | tf_op jit(solution)/shard_map/ppermute | solution.py:214
  39.7 2.0 %collective-permute-start.7 = (f32[256,512]{1,0:T(8,128)S(1)}, f32[256,512]{1,0:T(8,128)S(1)}, u32[]{:S(2)}, u32[]{:S(2)}) collective-permute-start(f32[256,512]{1,0:T(8,128)S(1)} %get-tuple-element.32.refs_2_), channel_id=1, source_target_pairs={{0,1},{1,0},{2,3},{3,2},{4,5},{5,4},{6,7},{7,6},{8,9},{9,8},{10,11... | collective-permute-start | bytes 1572872 | tf_op jit(solution)/shard_map/ppermute | solution.py:217
  41.7 10.1 %collective-permute-start.8 = (bf16[256,512]{1,0:T(8,128)(2,1)S(1)}, bf16[256,512]{1,0:T(8,128)(2,1)S(1)}, u32[]{:S(2)}, u32[]{:S(2)}) collective-permute-start(bf16[256,512]{1,0:T(8,128)(2,1)S(1)} %add_halves.6.refs_2_), channel_id=1, source_target_pairs={{2,0},{4,2},{6,4},{8,6},{10,8},{12,10},{14,12},{0,14},{3,1},{5,3},... | collective-permute-start | bytes 786440 | tf_op jit(solution)/shard_map/ppermute | solution.py:214
  43.0 10.6 %collective-permute-start.14 = (bf16[256,512]{1,0:T(8,128)(2,1)S(1)}, bf16[256,512]{1,0:T(8,128)(2,1)S(1)}, u32[]{:S(2)}, u32[]{:S(2)}) collective-permute-start(bf16[256,512]{1,0:T(8,128)(2,1)S(1)} %add_halves.7), channel_id=1, source_target_pairs={{6,2},{10,6},{14,10},{2,14},{0,12},{7,3},{11,7},{15,11},{3,15},{1,... | collective-permute-start | bytes 786440 | tf_op jit(solution)/shard_map/ppermute | solution.py:214
  46.7 2.8 %collective-permute-start.12 = (bf16[512,256]{1,0:T(8,128)(2,1)S(1)}, bf16[512,256]{1,0:T(8,128)(2,1)S(1)}, u32[]{:S(2)}, u32[]{:S(2)}) collective-permute-start(bf16[512,256]{1,0:T(8,128)(2,1)S(1)} %collective-permute-done.11.far_hidden), channel_id=1, source_target_pairs={{0,1},{1,0},{2,3},{3,2},{4,5},{5,4},{6,7},{7,6},{8,9},{9,8},{10,11... | collective-permute-start | bytes 786440 | tf_op jit(solution)/shard_map/ppermute | solution.py:217
  46.8 2.7 %collective-permute-start.13 = (bf16[512,256]{1,0:T(8,128)(2,1)S(1)}, bf16[512,256]{1,0:T(8,128)(2,1)S(1)}, u32[]{:S(2)}, u32[]{:S(2)}) collective-permute-start(bf16[512,256]{1,0:T(8,128)(2,1)S(1)} %collective-permute-done.10.near_hidden), channel_id=1, source_target_pairs={{0,1},{1,0},{2,3},{3,2},{4,5},{5,4},{6,7},{7,6},{8,9},{9,8},{10,11... | collective-permute-start | bytes 786440 | tf_op jit(solution)/shard_map/ppermute | solution.py:217

commit v8 on v7

--- a/solution.py
+++ b/solution.py
@@ -114,6 +114,16 @@
     here[...] = dot(grad[:CAP, :], weights[0, half_of(lax.axis_index("loc"), half), :], (1, 1))
 
 
+def product_part(part, grad, weights, away):
+    quarter = away.shape[1]
+    rows = half_of(2 * (1 - lax.axis_index("loc")) + part, quarter)
+    away[...] = dot(grad[:CAP, :], weights[0, rows, :], (1, 1))
+
+
+def product_rest(grad, weights, away):
+    product_part(1, grad, weights, away)
+
+
 def join_near(turned, relayed, direct, weights, near, away):
     odd = lax.axis_index("grp") % 2 == 1
 
@@ -126,7 +136,13 @@
         near[:RELAYED, :] = relayed[...]
 
     near[RELAYED:, :] = direct[...]
-    product_away(near, weights, away)
+    product_part(0, near, weights, away)
+
+
+def add_parts(here, left, right, out):
+    quarter = left.shape[1]
+    out[:, :quarter] = (here[:, :quarter] + left[...]).astype(BF16)
+    out[:, quarter:] = (here[:, quarter:] + right[...]).astype(BF16)
 
 
 def take_rest(grad_out, rest):
@@ -150,11 +166,13 @@
 
 def place(first, far, mask, sums, out, copied):
     low = first.shape[0] - CAP
-    sums[:low, :] = first[:low, :]
-    sums[low:, :] = (first[low:, :].astype(F32) + far[...].astype(F32) * mask[...].astype(F32)).astype(BF16)
-    copy = pltpu.make_async_copy(sums, out, copied)
-    copy.start()
-    copy.wait()
+    head = pltpu.make_async_copy(first.at[pl.ds(0, low)], out.at[pl.ds(0, low)], copied.at[0])
+    head.start()
+    sums[...] = (first[low:, :].astype(F32) + far[...].astype(F32) * mask[...].astype(F32)).astype(BF16)
+    last = pltpu.make_async_copy(sums, out.at[pl.ds(low, CAP)], copied.at[1])
+    last.start()
+    head.wait()
+    last.wait()
 
 
 def place_early(places, own, near, mask, far, done, out, first, sums, copied):
@@ -254,12 +272,15 @@
     own_hidden, places, mask = call(
         pick_own, [((units, CAP), BF16), ((rows, 2 * CAP), BF16), block], counts, hidden, scalars=1, after=(far_block,)
     )
-    near_in, near_away = call(
-        join_near, [((CAP, features), BF16), partial], turned_in, relayed_in, direct_in, weights, after=(places,)
-    )
-    near_other = swap_cores(near_away)
-    (near_here,) = call(product_here, [partial], near_in, weights, after=(near_away,))
-    (near_block,) = call(add_halves, [block], near_here, near_other)
+    quarter = ((CAP, half // 2), F32)
+    near_in, near_left = call(
+        join_near, [((CAP, features), BF16), quarter], turned_in, relayed_in, direct_in, weights, after=(places,)
+    )
+    near_left_other = swap_cores(near_left)
+    (near_right,) = call(product_rest, [quarter], near_in, weights, after=(near_left,))
+    near_right_other = swap_cores(near_right)
+    (near_here,) = call(product_here, [partial], near_in, weights, after=(near_right,))
+    (near_block,) = call(add_parts, [block], near_here, near_left_other, near_right_other)
     near_back = send(near_block, back1)
     (total,) = call(own_weights, [((units, features), F32)], own_hidden, grad_out, after=(near_block,))
     (late_block,) = call(add_halves, [block], far_here, far_other, after=(total,))
@@ -275,7 +296,7 @@
     )
     whole = jax.ShapeDtypeStruct((rows, half), BF16)
     common = {
-        "scratch_shapes": [pltpu.VMEM((rows, half), BF16), pltpu.SemaphoreType.DMA],
+        "scratch_shapes": [pltpu.VMEM((CAP, half), BF16), pltpu.SemaphoreType.DMA((2,))],
         "cost_estimate": pl.CostEstimate(flops=10**10, bytes_accessed=10**3, transcendentals=0),
         "compiler_params": pltpu.CompilerParams(vmem_limit_bytes=16 << 20),
     }

time: 54.2 us -> 54.2 us (level)
  starting transfers between devices: 18 us -> 18.6 us
    ppermute x5 -> x6, waiting for transfers between devices: 1.23 us -> 0.5 us  [swap_cores(): return lax.ppermute(value, 'loc', [(0, 1), (1, 0)])]
    ppermute x5 -> x6, starting transfers between devices: 0.78 us -> 1.34 us  [swap_cores(): return lax.ppermute(value, 'loc', [(0, 1), (1, 0)])]
    pallas_call x16 -> x17, Pallas kernels: 9.37 us -> 9.58 us  [call(): pl.pallas_call(body, out_shape=[jax.ShapeDtypeStruct(shape, dtype) for sh...]
  transfers between devices with their start and end apart: 15 -> 16, of which waited for: 5 -> 5; matrix products, arithmetic and copies ran while one was open for 0% -> 0% of each run, Pallas kernels for 28% -> 28%
where the time goes in v8:
time: 54.2 us; the launch traced here: 53.9 us
  starting transfers between devices  18.6 us (34%)
  waiting for transfers between devices  15.4 us (28%)
  Pallas kernels  15.3 us (28%)
  local copies, waits for them, and re-layouts  3.68 us (7%)
  between operations  0.87 us (2%)
    ppermute x10, starting transfers between devices, send(): return lax.ppermute(value, 'grp', pairs)  17.2 us
    ppermute x10, waiting for transfers between devices, send(): return lax.ppermute(value, 'grp', pairs)  14.9 us
    pallas_call x17, Pallas kernels, call(): pl.pallas_call(body, out_shape=[jax.ShapeDtypeStruct(shape, dtype) for sh...  9.58 us
    pallas_call x2, Pallas kernels, rows_of_half(): pl.pallas_call(functools.partial(half_weights, side), out_shape=[jax.Shap...  4.49 us
    unnamed x12, local copies, waits for them, and re-layouts  2.63 us
    ppermute x6, starting transfers between devices, swap_cores(): return lax.ppermute(value, 'loc', [(0, 1), (1, 0)])  1.34 us
    pallas_call x1, Pallas kernels, local(): pl.pallas_call(place_early, out_shape=[whole, whole], in_specs=[VMEM] * 5...  1.25 us
  transfers between devices with their start and end apart: 16, of which 5 were waited for; matrix products, arithmetic and copies ran while one was open for 0% of the time, Pallas kernels for 28%

profile of v8, /device:TPU:0, one launch (start us, length us, event | category | flops | bytes accessed | tf_op | source)
XLA Modules:
  0.0 53.9 jit_solution(2436707969503451707)
XLA Ops:
  0.6 1.1 %slice.3.refs_2_ = bf16[128,1792]{1,0:T(8,128)(2,1)S(1)} slice(bf16[512,1792]{1,0:T(8,128)(2,1)} %refs_1_.19), slice={[256:384], [0:1792]} | slice | bytes 917504 | tf_op jit(solution)/shard_map/slice | solution.py:239
  1.7 3.1 %collective-permute-start = (bf16[128,1792]{1,0:T(8,128)(2,1)S(1)}, bf16[128,1792]{1,0:T(8,128)(2,1)S(1)}, u32[]{:S(2)}, u32[]{:S(2)}) collective-permute-start(bf16[128,1792]{1,0:T(8,128)(2,1)S(1)} %slice.3.refs_2_), channel_id=1, source_target_pairs={{0,4},{2,6},{4,8},{6,10},{8,12},{10,14},{12,0},{14,2},{1,5},{3,7},... | collective-permute-start | bytes 1376264 | tf_op jit(solution)/shard_map/ppermute | solution.py:232
  4.8 1.5 %copy-done = bf16[512,1792]{1,0:T(8,128)(2,1)S(1)} copy-done((bf16[512,1792]{1,0:T(8,128)(2,1)S(1)}, bf16[512,1792]{1,0:T(8,128)(2,1)}, u32[]{:S(2)}) %copy-start) | copy-done | bytes 1835032
  6.3 0.7 %copy-done.4 = s32[1,3]{1,0:T(1,128)S(1)} copy-done((s32[1,3]{1,0:T(1,128)S(1)}, s32[1,3]{1,0:T(1,128)}, u32[]{:S(2)}) %copy-start.4) | copy-done | bytes 36
  6.9 0.9 %pick_turned.1.refs_1_ = bf16[128,1792]{1,0:T(8,128)(2,1)S(1)} custom-call(s32[1,3]{1,0:T(1,128)S(1)} %copy-done.4, bf16[512,1792]{1,0:T(8,128)(2,1)S(1)} %copy-done, bf16[128,1792]{1,0:T(8,128)(2,1)S(1)} %slice.3.refs_2_), custom_call_target="tpu_custom_call" | custom-call | flops 10000000000 | bytes 1000 | tf_op jit(solution)/shard_map/pick_turned/pallas_call | solution.py:27
  7.9 0.0 copy-start.2
  7.9 1.6 %collective-permute-start.2 = (bf16[128,1792]{1,0:T(8,128)(2,1)S(1)}, bf16[128,1792]{1,0:T(8,128)(2,1)S(1)}, u32[]{:S(2)}, u32[]{:S(2)}) collective-permute-start(bf16[128,1792]{1,0:T(8,128)(2,1)S(1)} %pick_turned.1.refs_1_), channel_id=1, source_target_pairs={{0,2},{2,0},{4,6},{6,4},{8,10},{10,8},{12,14},{14,12},{1,3},{3,1},... | collective-permute-start | bytes 1376264 | tf_op jit(solution)/shard_map/ppermute | solution.py:232
  9.5 1.6 %collective-permute-start.1 = (bf16[128,1792]{1,0:T(8,128)(2,1)S(1)}, bf16[128,1792]{1,0:T(8,128)(2,1)S(1)}, u32[]{:S(2)}, u32[]{:S(2)}) collective-permute-start(bf16[128,1792]{1,0:T(8,128)(2,1)S(1)} %take_rest.1.refs_2_), channel_id=1, source_target_pairs={{0,4},{2,6},{4,8},{6,10},{8,12},{10,14},{12,0},{14,2},{1,5},{3,7},... | collective-permute-start | bytes 1376264 | tf_op jit(solution)/shard_map/ppermute | solution.py:232
  11.1 0.7 %product_away.1.refs_2_ = f32[256,512]{1,0:T(8,128)S(1)} custom-call(bf16[512,1792]{1,0:T(8,128)(2,1)S(1)} %copy-done.1, bf16[1,1024,1792]{2,1,0:T(8,128)(2,1)S(1)} %copy-done.2, bf16[128,1792]{1,0:T(8,128)(2,1)S(1)} %take_rest.1.refs_2_), custom_call_target="tpu_custom_call" | custom-call | flops 10000000000 | bytes 1000 | tf_op jit(solution)/shard_map/product_away/pallas_call | solution.py:27
  11.8 0.0 copy-start.3
  11.8 0.1 collective-permute-start.3
  11.9 0.7 %product_here.3.refs_2_.refs_0_ = f32[256,512]{1,0:T(8,128)S(1)} custom-call(bf16[512,1792]{1,0:T(8,128)(2,1)S(1)} %copy-done.1, bf16[1,1024,1792]{2,1,0:T(8,128)(2,1)S(1)} %copy-done.2, f32[256,512]{1,0:T(8,128)S(1)} %product_away.1.refs_2_), custom_call_target="tpu_custom_call" | custom-call | flops 10000000000 | bytes 1000 | tf_op jit(solution)/shard_map/product_here/pallas_call | solution.py:27
  12.6 0.5 copy-done.3
  13.0 1.0 %pick_hidden.1 = (bf16[512,256]{1,0:T(8,128)(2,1)S(1)}, bf16[512,256]{1,0:T(8,128)(2,1)S(1)}) custom-call(s32[1,3]{1,0:T(1,128)S(1)} %copy-done.4, bf16[512,1024]{1,0:T(8,128)(2,1)S(1)} %copy-done.3, f32[256,512]{1,0:T(8,128)S(1)} %product_here.3.refs_2_.refs_0_), custom_call_target="tpu_custom_call" | custom-call | flops 10000000000 | bytes 1000 | tf_op jit(solution)/shard_map/pick_hidden/pallas_call | solution.py:27
  14.1 1.0 %pick_direct.1.refs_2_ = bf16[128,1792]{1,0:T(8,128)(2,1)S(1)} custom-call(s32[1,3]{1,0:T(1,128)S(1)} %copy-done.4, bf16[512,1792]{1,0:T(8,128)(2,1)S(1)} %copy-done.1, bf16[512,256]{1,0:T(8,128)(2,1)S(1)} %get-tuple-element.35.refs_2_), custom_call_target="tpu_custom_call" | custom-call | flops 10000000000 | bytes 1000 | tf_op jit(solution)/shard_map/pick_direct/pallas_call | solution.py:27
  15.0 0.6 %collective-permute-start.6 = (bf16[128,1792]{1,0:T(8,128)(2,1)S(1)}, bf16[128,1792]{1,0:T(8,128)(2,1)S(1)}, u32[]{:S(2)}, u32[]{:S(2)}) collective-permute-start(bf16[128,1792]{1,0:T(8,128)(2,1)S(1)} %pick_direct.1.refs_2_), channel_id=1, source_target_pairs={{0,2},{2,4},{4,6},{6,8},{8,10},{10,12},{12,14},{14,0},{1,3},{3,5},... | collective-permute-start | bytes 1376264 | tf_op jit(solution)/shard_map/ppermute | solution.py:232
  15.6 0.0 collective-permute-done.3.refs_1_
  15.6 4.8 %collective-permute-done.2.refs_3_.refs_0_ = bf16[128,1792]{1,0:T(8,128)(2,1)S(1)} collective-permute-done((bf16[128,1792]{1,0:T(8,128)(2,1)S(1)}, bf16[128,1792]{1,0:T(8,128)(2,1)S(1)}, u32[]{:S(2)}, u32[]{:S(2)}) %collective-permute-start.2) | collective-permute-done | bytes 458784 | tf_op jit(solution)/shard_map/ppermute | solution.py:232
  20.4 3.5 %collective-permute-start.5 = (bf16[128,1792]{1,0:T(8,128)(2,1)S(1)}, bf16[128,1792]{1,0:T(8,128)(2,1)S(1)}, u32[]{:S(2)}, u32[]{:S(2)}) collective-permute-start(bf16[128,1792]{1,0:T(8,128)(2,1)S(1)} %collective-permute-done.2.refs_3_.refs_0_), channel_id=1, source_target_pairs={{0,4},{4,8},{8,12},{12,0},{1,5},{5,9},{9,13},{13,1},{16,20},{20,24... | collective-permute-start | bytes 1376264 | tf_op jit(solution)/shard_map/ppermute | solution.py:232
  23.9 4.0 %collective-permute-done.1.refs_1_ = bf16[128,1792]{1,0:T(8,128)(2,1)S(1)} collective-permute-done((bf16[128,1792]{1,0:T(8,128)(2,1)S(1)}, bf16[128,1792]{1,0:T(8,128)(2,1)S(1)}, u32[]{:S(2)}, u32[]{:S(2)}) %collective-permute-start.1) | collective-permute-done | bytes 458784 | tf_op jit(solution)/shard_map/ppermute | solution.py:232
  28.0 0.0 collective-permute-done.refs_0_
  28.0 0.7 %join_far.1 = (bf16[256,1792]{1,0:T(8,128)(2,1)S(1)}, f32[256,512]{1,0:T(8,128)S(1)}) custom-call(bf16[128,1792]{1,0:T(8,128)(2,1)S(1)} %collective-permute-done.refs_0_, bf16[128,1792]{1,0:T(8,128)(2,1)S(1)} %collective-permute-done.1.refs_1_, bf16[1,1024,1792]{2,1,0:T(8,128)(2,1)S(1)} %copy-done.2, bf16[128,1792]{1,0:T(8,128)(2,1)S(1)} %collective-permute-done.2.refs_3_.refs_0_), custom_call_target="tpu_custom_call" | custom-call | flops 10000000000 | bytes 1000 | tf_op jit(solution)/shard_map/join_far/pallas_call | solution.py:27
  28.6 0.1 collective-permute-start.4
  28.7 0.7 %product_here.4.refs_0_ = f32[256,512]{1,0:T(8,128)S(1)} custom-call(bf16[256,1792]{1,0:T(8,128)(2,1)S(1)} %get-tuple-element.26.refs_0_.far, bf16[1,1024,1792]{2,1,0:T(8,128)(2,1)S(1)} %copy-done.2, f32[256,512]{1,0:T(8,128)S(1)} %get-tuple-element.27.refs_2_), custom_call_target="tpu_custom_call" | custom-call | flops 10000000000 | bytes 1000 | tf_op jit(solution)/shard_map/product_here/pallas_call | solution.py:27
  29.4 0.0 copy-start.5
  29.4 1.8 %collective-permute-start.11 = (bf16[512,256]{1,0:T(8,128)(2,1)S(1)}, bf16[512,256]{1,0:T(8,128)(2,1)S(1)}, u32[]{:S(2)}, u32[]{:S(2)}) collective-permute-start(bf16[512,256]{1,0:T(8,128)(2,1)S(1)} %get-tuple-element.34), channel_id=1, source_target_pairs={{0,2},{2,4},{4,6},{6,8},{8,10},{10,12},{12,14},{14,0},{1,3},{3,5},... | collective-permute-start | bytes 786440 | tf_op jit(solution)/shard_map/ppermute | solution.py:232
  31.3 1.3 %collective-permute-start.10 = (bf16[256,512]{1,0:T(8,128)(2,1)S(1)}, bf16[256,512]{1,0:T(8,128)(2,1)S(1)}, u32[]{:S(2)}, u32[]{:S(2)}) collective-permute-start(bf16[256,512]{1,0:T(8,128)(2,1)S(1)} %add_halves.4.refs_2_), channel_id=1, source_target_pairs={{4,0},{8,4},{12,8},{5,1},{9,5},{13,9},{20,16},{24,20},{28,24},{21,... | collective-permute-start | bytes 786440 | tf_op jit(solution)/shard_map/ppermute | solution.py:232
  32.6 1.0 %pick_own.1 = (bf16[1024,256]{1,0:T(8,128)(2,1)S(1)}, bf16[512,512]{1,0:T(8,128)(2,1)S(1)}, bf16[256,512]{1,0:T(8,128)(2,1)S(1)}) custom-call(s32[1,3]{1,0:T(1,128)S(1)} %copy-done.5, bf16[512,1024]{1,0:T(8,128)(2,1)S(1)} %copy-done.3, bf16[256,512]{1,0:T(8,128)(2,1)S(1)} %add_halves.4.refs_2_), custom_call_target="tpu_custom_call" | custom-call | flops 10000000000 | bytes 1000 | tf_op jit(solution)/shard_map/pick_own/pallas_call | solution.py:27
  33.7 5.3 %collective-permute-done.6.refs_2_ = bf16[128,1792]{1,0:T(8,128)(2,1)S(1)} collective-permute-done((bf16[128,1792]{1,0:T(8,128)(2,1)S(1)}, bf16[128,1792]{1,0:T(8,128)(2,1)S(1)}, u32[]{:S(2)}, u32[]{:S(2)}) %collective-permute-start.6) | collective-permute-done | bytes 458784 | tf_op jit(solution)/shard_map/ppermute | solution.py:232
  39.0 0.5 join_near.1
  39.5 0.1 collective-permute-start.7
  39.6 0.4 product_rest.1.refs_2_
  40.0 0.6 %collective-permute-start.8 = (f32[256,256]{1,0:T(8,128)S(1)}, f32[256,256]{1,0:T(8,128)S(1)}, u32[]{:S(2)}, u32[]{:S(2)}) collective-permute-start(f32[256,256]{1,0:T(8,128)S(1)} %product_rest.1.refs_2_), channel_id=1, source_target_pairs={{0,1},{1,0},{2,3},{3,2},{4,5},{5,4},{6,7},{7,6},{8,9},{9,8},{10,11... | collective-permute-start | bytes 786440 | tf_op jit(solution)/shard_map/ppermute | solution.py:235
  40.6 0.7 %product_here.5.refs_0_ = f32[256,512]{1,0:T(8,128)S(1)} custom-call(bf16[256,1792]{1,0:T(8,128)(2,1)S(1)} %get-tuple-element.31.refs_0_.near, bf16[1,1024,1792]{2,1,0:T(8,128)(2,1)S(1)} %copy-done.2, f32[256,256]{1,0:T(8,128)S(1)} %product_rest.1.refs_2_), custom_call_target="tpu_custom_call" | custom-call | flops 10000000000 | bytes 1000 | tf_op jit(solution)/shard_map/product_here/pallas_call | solution.py:27
  41.2 0.5 collective-permute-done.8.refs_2_
  41.7 0.1 add_parts.1.refs_2_
  41.8 0.1 collective-permute-start.9
  41.8 1.1 %own_weights.1.refs_2_.before = f32[1024,1792]{1,0:T(8,128)S(1)} custom-call(bf16[1024,256]{1,0:T(8,128)(2,1)S(1)} %get-tuple-element.36.refs_0_, bf16[512,1792]{1,0:T(8,128)(2,1)S(1)} %copy-done.1, bf16[256,512]{1,0:T(8,128)(2,1)S(1)} %add_parts.1.refs_2_), custom_call_target="tpu_custom_call" | custom-call | flops 10000000000 | bytes 1000 | tf_op jit(solution)/shard_map/own_weights/pallas_call | solution.py:27
  43.0 0.1 add_halves.5
  43.0 3.7 %collective-permute-start.15 = (bf16[256,512]{1,0:T(8,128)(2,1)S(1)}, bf16[256,512]{1,0:T(8,128)(2,1)S(1)}, u32[]{:S(2)}, u32[]{:S(2)}) collective-permute-start(bf16[256,512]{1,0:T(8,128)(2,1)S(1)} %add_halves.5), channel_id=1, source_target_pairs={{6,2},{10,6},{14,10},{2,14},{0,12},{7,3},{11,7},{15,11},{3,15},{1,... | collective-permute-start | bytes 786440 | tf_op jit(solution)/shard_map/ppermute | solution.py:232
  46.8 0.1 collective-permute-start.13
  46.9 0.4 collective-permute-start.14
  47.4 2.2 %half_weights.2 = (bf16[1,1024,1792]{2,1,0:T(8,128)(2,1)}, bf16[16,128]{1,0:T(8,128)(2,1)}) custom-call(bf16[512,256]{1,0:T(8,128)(2,1)S(1)} %collective-permute-done.12.far_hidden, bf16[512,256]{1,0:T(8,128)(2,1)S(1)} %collective-permute-done.11.near_hidden, bf16[256,1792]{1,0:T(8,128)(2,1)S(1)} %get-tuple-element.26.refs_0_.far, ...), custom_call_target="tpu_custom_call" | custom-call | flops 10000000000 | bytes 1000 | tf_op jit(solution)/shard_map/half_weights/pallas_call | solution.py:205
  49.6 2.3 %half_weights.3 = (bf16[1,1024,1792]{2,1,0:T(8,128)(2,1)}, bf16[16,128]{1,0:T(8,128)(2,1)S(1)}) custom-call(bf16[512,256]{1,0:T(8,128)(2,1)S(1)} %collective-permute-done.13.far_hidden, bf16[512,256]{1,0:T(8,128)(2,1)S(1)} %collective-permute-done.14.near_hidden, ...), custom_call_target="tpu_custom_call", output_to_operand_aliasing={{0}: (5, {})} | custom-call | flops 10000000000 | bytes 1000 | tf_op jit(solution)/shard_map/half_weights/pallas_call | solution.py:205
  51.9 0.0 collective-permute-done.10.far
  51.9 0.0 collective-permute-done.9.near
  51.9 1.2 %place_early.1 = (bf16[512,512]{1,0:T(8,128)(2,1)}, bf16[512,512]{1,0:T(8,128)(2,1)S(1)}) custom-call(bf16[512,512]{1,0:T(8,128)(2,1)S(1)} %get-tuple-element.29.refs_4_.places, bf16[256,512]{1,0:T(8,128)(2,1)S(1)} %add_halves.3.own, bf16[256,512]{1,0:T(8,128)(2,1)S(1)} %collective-permute-done.9.near, bf16[256,512]{1,0:T(8,128)(2,1)S(1)} %get-tuple-element.33.mask, ...), custom_call_target="tpu_custom_call" | custom-call | flops 10000000000 | bytes 1000 | tf_op jit(solution)/shard_map/place_early/pallas_call | solution.py:303
  53.1 0.7 %collective-permute-done.15.far = bf16[256,512]{1,0:T(8,128)(2,1)S(1)} collective-permute-done((bf16[256,512]{1,0:T(8,128)(2,1)S(1)}, bf16[256,512]{1,0:T(8,128)(2,1)S(1)}, u32[]{:S(2)}, u32[]{:S(2)}) %collective-permute-start.15) | collective-permute-done | bytes 262176 | tf_op jit(solution)/shard_map/ppermute | solution.py:232
  (18 shorter events, 0.2 us)
Async XLA Ops:
  1.7 26.3 %collective-permute-start = (bf16[128,1792]{1,0:T(8,128)(2,1)S(1)}, bf16[128,1792]{1,0:T(8,128)(2,1)S(1)}, u32[]{:S(2)}, u32[]{:S(2)}) collective-permute-start(bf16[128,1792]{1,0:T(8,128)(2,1)S(1)} %slice.3.refs_2_), channel_id=1, source_target_pairs={{0,4},{2,6},{4,8},{6,10},{8,12},{10,14},{12,0},{14,2},{1,5},{3,7},... | collective-permute-start | bytes 1376264 | tf_op jit(solution)/shard_map/ppermute | solution.py:232
  4.8 1.5 %copy-start = (bf16[512,1792]{1,0:T(8,128)(2,1)S(1)}, bf16[512,1792]{1,0:T(8,128)(2,1)}, u32[]{:S(2)}) copy-start(bf16[512,1792]{1,0:T(8,128)(2,1)} %refs_1_.19) | copy-start | bytes 5505028
  6.3 0.7 %copy-start.4 = (s32[1,3]{1,0:T(1,128)S(1)}, s32[1,3]{1,0:T(1,128)}, u32[]{:S(2)}) copy-start(s32[1,3]{1,0:T(1,128)} %refs_0_.13) | copy-start | bytes 40
  6.9 2.6 %copy-start.1 = (bf16[512,1792]{1,0:T(8,128)(2,1)S(1)}, bf16[512,1792]{1,0:T(8,128)(2,1)}, u32[]{:S(2)}) copy-start(bf16[512,1792]{1,0:T(8,128)(2,1)} %refs_1_.19) | copy-start | bytes 5505028
  7.9 3.3 %copy-start.2 = (bf16[1,1024,1792]{2,1,0:T(8,128)(2,1)S(1)}, bf16[1,1024,1792]{2,1,0:T(8,128)(2,1)}, u32[]{:S(2)}) copy-start(bf16[1,1024,1792]{2,1,0:T(8,128)(2,1)} %refs_1_.18) | copy-start | bytes 11010052
  7.9 12.5 %collective-permute-start.2 = (bf16[128,1792]{1,0:T(8,128)(2,1)S(1)}, bf16[128,1792]{1,0:T(8,128)(2,1)S(1)}, u32[]{:S(2)}, u32[]{:S(2)}) collective-permute-start(bf16[128,1792]{1,0:T(8,128)(2,1)S(1)} %pick_turned.1.refs_1_), channel_id=1, source_target_pairs={{0,2},{2,0},{4,6},{6,4},{8,10},{10,8},{12,14},{14,12},{1,3},{3,1},... | collective-permute-start | bytes 1376264 | tf_op jit(solution)/shard_map/ppermute | solution.py:232
  9.5 18.5 %collective-permute-start.1 = (bf16[128,1792]{1,0:T(8,128)(2,1)S(1)}, bf16[128,1792]{1,0:T(8,128)(2,1)S(1)}, u32[]{:S(2)}, u32[]{:S(2)}) collective-permute-start(bf16[128,1792]{1,0:T(8,128)(2,1)S(1)} %take_rest.1.refs_2_), channel_id=1, source_target_pairs={{0,4},{2,6},{4,8},{6,10},{8,12},{10,14},{12,0},{14,2},{1,5},{3,7},... | collective-permute-start | bytes 1376264 | tf_op jit(solution)/shard_map/ppermute | solution.py:232
  11.8 1.2 %copy-start.3 = (bf16[512,1024]{1,0:T(8,128)(2,1)S(1)}, bf16[512,1024]{1,0:T(8,128)(2,1)}, u32[]{:S(2)}) copy-start(bf16[512,1024]{1,0:T(8,128)(2,1)} %refs_1_.16) | copy-start | bytes 3145732
  11.8 3.8 %collective-permute-start.3 = (f32[256,512]{1,0:T(8,128)S(1)}, f32[256,512]{1,0:T(8,128)S(1)}, u32[]{:S(2)}, u32[]{:S(2)}) collective-permute-start(f32[256,512]{1,0:T(8,128)S(1)} %product_away.1.refs_2_), channel_id=1, source_target_pairs={{0,1},{1,0},{2,3},{3,2},{4,5},{5,4},{6,7},{7,6},{8,9},{9,8},{10,11... | collective-permute-start | bytes 1572872 | tf_op jit(solution)/shard_map/ppermute | solution.py:235
  15.0 24.0 %collective-permute-start.6 = (bf16[128,1792]{1,0:T(8,128)(2,1)S(1)}, bf16[128,1792]{1,0:T(8,128)(2,1)S(1)}, u32[]{:S(2)}, u32[]{:S(2)}) collective-permute-start(bf16[128,1792]{1,0:T(8,128)(2,1)S(1)} %pick_direct.1.refs_2_), channel_id=1, source_target_pairs={{0,2},{2,4},{4,6},{6,8},{8,10},{10,12},{12,14},{14,0},{1,3},{3,5},... | collective-permute-start | bytes 1376264 | tf_op jit(solution)/shard_map/ppermute | solution.py:232
  20.4 18.6 %collective-permute-start.5 = (bf16[128,1792]{1,0:T(8,128)(2,1)S(1)}, bf16[128,1792]{1,0:T(8,128)(2,1)S(1)}, u32[]{:S(2)}, u32[]{:S(2)}) collective-permute-start(bf16[128,1792]{1,0:T(8,128)(2,1)S(1)} %collective-permute-done.2.refs_3_.refs_0_), channel_id=1, source_target_pairs={{0,4},{4,8},{8,12},{12,0},{1,5},{5,9},{9,13},{13,1},{16,20},{20,24... | collective-permute-start | bytes 1376264 | tf_op jit(solution)/shard_map/ppermute | solution.py:232
  28.6 2.6 %collective-permute-start.4 = (f32[256,512]{1,0:T(8,128)S(1)}, f32[256,512]{1,0:T(8,128)S(1)}, u32[]{:S(2)}, u32[]{:S(2)}) collective-permute-start(f32[256,512]{1,0:T(8,128)S(1)} %get-tuple-element.27.refs_2_), channel_id=1, source_target_pairs={{0,1},{1,0},{2,3},{3,2},{4,5},{5,4},{6,7},{7,6},{8,9},{9,8},{10,11... | collective-permute-start | bytes 1572872 | tf_op jit(solution)/shard_map/ppermute | solution.py:235
  29.4 3.2 %copy-start.5 = (s32[1,3]{1,0:T(1,128)S(1)}, s32[1,3]{1,0:T(1,128)}, u32[]{:S(2)}) copy-start(s32[1,3]{1,0:T(1,128)} %refs_0_.13) | copy-start | bytes 40
  29.4 17.4 %collective-permute-start.11 = (bf16[512,256]{1,0:T(8,128)(2,1)S(1)}, bf16[512,256]{1,0:T(8,128)(2,1)S(1)}, u32[]{:S(2)}, u32[]{:S(2)}) collective-permute-start(bf16[512,256]{1,0:T(8,128)(2,1)S(1)} %get-tuple-element.34), channel_id=1, source_target_pairs={{0,2},{2,4},{4,6},{6,8},{8,10},{10,12},{12,14},{14,0},{1,3},{3,5},... | collective-permute-start | bytes 786440 | tf_op jit(solution)/shard_map/ppermute | solution.py:232
  31.2 15.6 %collective-permute-start.12 = (bf16[512,256]{1,0:T(8,128)(2,1)S(1)}, bf16[512,256]{1,0:T(8,128)(2,1)S(1)}, u32[]{:S(2)}, u32[]{:S(2)}) collective-permute-start(bf16[512,256]{1,0:T(8,128)(2,1)S(1)} %get-tuple-element.35.refs_2_), channel_id=1, source_target_pairs={{0,4},{2,6},{4,8},{6,10},{8,12},{10,14},{12,0},{14,2},{1,5},{3,7},... | collective-permute-start | bytes 786440 | tf_op jit(solution)/shard_map/ppermute | solution.py:232
  31.3 20.6 %collective-permute-start.10 = (bf16[256,512]{1,0:T(8,128)(2,1)S(1)}, bf16[256,512]{1,0:T(8,128)(2,1)S(1)}, u32[]{:S(2)}, u32[]{:S(2)}) collective-permute-start(bf16[256,512]{1,0:T(8,128)(2,1)S(1)} %add_halves.4.refs_2_), channel_id=1, source_target_pairs={{4,0},{8,4},{12,8},{5,1},{9,5},{13,9},{20,16},{24,20},{28,24},{21,... | collective-permute-start | bytes 786440 | tf_op jit(solution)/shard_map/ppermute | solution.py:232
  39.5 2.2 %collective-permute-start.7 = (f32[256,256]{1,0:T(8,128)S(1)}, f32[256,256]{1,0:T(8,128)S(1)}, u32[]{:S(2)}, u32[]{:S(2)}) collective-permute-start(f32[256,256]{1,0:T(8,128)S(1)} %get-tuple-element.32.refs_2_), channel_id=1, source_target_pairs={{0,1},{1,0},{2,3},{3,2},{4,5},{5,4},{6,7},{7,6},{8,9},{9,8},{10,11... | collective-permute-start | bytes 786440 | tf_op jit(solution)/shard_map/ppermute | solution.py:235
  40.0 1.7 %collective-permute-start.8 = (f32[256,256]{1,0:T(8,128)S(1)}, f32[256,256]{1,0:T(8,128)S(1)}, u32[]{:S(2)}, u32[]{:S(2)}) collective-permute-start(f32[256,256]{1,0:T(8,128)S(1)} %product_rest.1.refs_2_), channel_id=1, source_target_pairs={{0,1},{1,0},{2,3},{3,2},{4,5},{5,4},{6,7},{7,6},{8,9},{9,8},{10,11... | collective-permute-start | bytes 786440 | tf_op jit(solution)/shard_map/ppermute | solution.py:235
  41.8 10.1 %collective-permute-start.9 = (bf16[256,512]{1,0:T(8,128)(2,1)S(1)}, bf16[256,512]{1,0:T(8,128)(2,1)S(1)}, u32[]{:S(2)}, u32[]{:S(2)}) collective-permute-start(bf16[256,512]{1,0:T(8,128)(2,1)S(1)} %add_parts.1.refs_2_), channel_id=1, source_target_pairs={{2,0},{4,2},{6,4},{8,6},{10,8},{12,10},{14,12},{0,14},{3,1},{5,3},... | collective-permute-start | bytes 786440 | tf_op jit(solution)/shard_map/ppermute | solution.py:232
  43.0 10.8 %collective-permute-start.15 = (bf16[256,512]{1,0:T(8,128)(2,1)S(1)}, bf16[256,512]{1,0:T(8,128)(2,1)S(1)}, u32[]{:S(2)}, u32[]{:S(2)}) collective-permute-start(bf16[256,512]{1,0:T(8,128)(2,1)S(1)} %add_halves.5), channel_id=1, source_target_pairs={{6,2},{10,6},{14,10},{2,14},{0,12},{7,3},{11,7},{15,11},{3,15},{1,... | collective-permute-start | bytes 786440 | tf_op jit(solution)/shard_map/ppermute | solution.py:232
  46.8 2.8 %collective-permute-start.13 = (bf16[512,256]{1,0:T(8,128)(2,1)S(1)}, bf16[512,256]{1,0:T(8,128)(2,1)S(1)}, u32[]{:S(2)}, u32[]{:S(2)}) collective-permute-start(bf16[512,256]{1,0:T(8,128)(2,1)S(1)} %collective-permute-done.12.far_hidden), channel_id=1, source_target_pairs={{0,1},{1,0},{2,3},{3,2},{4,5},{5,4},{6,7},{7,6},{8,9},{9,8},{10,11... | collective-permute-start | bytes 786440 | tf_op jit(solution)/shard_map/ppermute | solution.py:235
  46.9 2.7 %collective-permute-start.14 = (bf16[512,256]{1,0:T(8,128)(2,1)S(1)}, bf16[512,256]{1,0:T(8,128)(2,1)S(1)}, u32[]{:S(2)}, u32[]{:S(2)}) collective-permute-start(bf16[512,256]{1,0:T(8,128)(2,1)S(1)} %collective-permute-done.11.near_hidden), channel_id=1, source_target_pairs={{0,1},{1,0},{2,3},{3,2},{4,5},{5,4},{6,7},{7,6},{8,9},{9,8},{10,11... | collective-permute-start | bytes 786440 | tf_op jit(solution)/shard_map/ppermute | solution.py:235
